TPU v7x, 128 devices: a whole 4x4x4 slice. The times are simulated.
128 devices in a mesh: tile: 64 (over y, x, z), sec: 2 (over core).
Axes of the slice: x: 4, y: 4, z: 4, core: 2. Of those that a mesh axis runs over, the one named last changes fastest.
Arguments:
- features: bfloat16 [2, 2048, 384, 128], P('sec', 'tile'), may hold values from -6 to 6
- fold_mask: int32 [2, 2048, 384], P('sec', 'tile'), may hold values 0 or 1
- encoder_weight: bfloat16 [3, 3, 128, 128], replicated, may hold values from -0.1875 to 0.1875
- encoder_bias: float32 [128], replicated, may hold values from -3 to 3
- head_weight: bfloat16 [3, 3, 128, 256], replicated, may hold values from -0.1875 to 0.1875
- head_bias: float32 [256], replicated, may hold values from -3 to 3
- final_weight: bfloat16 [256, 256], replicated, may hold values from -0.375 to 0.375
- final_bias: float32 [256], replicated, may hold values from -3 to 3
- pair_source: int32 [2, 4096], P('sec', 'tile'), may hold values from 0 to 95
- pair_target: int32 [2, 4096], replicated, may hold values from 0 to 6143, as said below
Outputs:
- descriptors: bfloat16 [2, 2048, 384, 256], P('sec', 'tile')
- confidence: float32 [2, 4096, 128], P('sec', 'tile')
Inputs may be any that keep to these rules, and one draw needn't show every extreme that they name: `pair_target`: row s names blocks of section 1 - s by their number in that section; the 64 entries of one band name at most 2 blocks of any one band of the other section, and exactly 2 of some band.
All inputs are finite; a program needn't handle non-finite values. No bound on the sum of `fold_mask` on one device may be relied on, other than what follows from the above.
Results may differ from a plain program's by a relative error of at most 0.0076.
Values may be sent and summed in bfloat16 or wider, within the bound.
No kernel may reach another device: no remote copies, remote signals or barrier semaphores. Data moves between devices by JAX's collectives and lax.ppermute only.
A program may use at most 128 MiB of HBM per device.

v0:
```python
import jax
import jax.numpy as jnp
from jax import lax
from jax.sharding import PartitionSpec as P

BLOCK = 128


SCORE_SCALE = 10.0
FOLD_PENALTY = 200.0


def padded_2(block, sides, width):
    for axis, dim in sides:
        count = lax.axis_size(axis)
        forward = [(i, i + 1) for i in range(count - 1)]
        backward = [(target, source) for source, target in forward]
        low = lax.ppermute(
            lax.slice_in_dim(block, block.shape[dim] - width, None, axis=dim), axis, forward
        )
        high = lax.ppermute(lax.slice_in_dim(block, 0, width, axis=dim), axis, backward)
        block = jnp.concatenate([low, block, high], axis=dim)
    return block


def swapped(block, axis, distance):
    count = lax.axis_size(axis)
    route = []
    for low in range(count):
        high = low | 1 << distance
        if high != low and high < count:
            route += [(low, high), (high, low)]
    return lax.ppermute(block, axis, route)


def convolve(padded, kernel):
    height = padded.shape[0] - 2
    span_cols = padded.shape[1]
    channels = padded.shape[2]
    framed = jnp.pad(padded, ((0, 0), (1, 1), (0, 0)))
    summed = jnp.zeros((height * span_cols, kernel.shape[3]), jnp.float32)
    for down_shift in range(3):
        for side_shift in range(3):
            window = framed[
                down_shift : down_shift + height, side_shift : side_shift + span_cols, :
            ].reshape(height * span_cols, channels)
            summed = summed + jnp.dot(
                window, kernel[down_shift, side_shift], preferred_element_type=jnp.float32
            )
    return summed.reshape(height, span_cols, kernel.shape[3])


def dual_score(scores):
    row_peak = jnp.max(scores, axis=-1, keepdims=True)
    row_weight = jnp.exp(scores - row_peak)
    row_soft = row_weight / jnp.sum(row_weight, axis=-1, keepdims=True)
    column_peak = jnp.max(scores, axis=-2, keepdims=True)
    column_weight = jnp.exp(scores - column_peak)
    column_soft = column_weight / jnp.sum(column_weight, axis=-2, keepdims=True)
    return jnp.max(row_soft * column_soft, axis=-1)


def local(
    features,
    fold_mask,
    encoder_weight,
    encoder_bias,
    head_weight,
    head_bias,
    final_weight,
    final_bias,
    pair_source,
    pair_target,
):
    own_band = features[0]
    band_rows = own_band.shape[0]
    band_cols = own_band.shape[1]
    tile_count = lax.axis_size("tile")
    tile_here = lax.axis_index("tile")
    section = lax.axis_index("sec")
    padded = padded_2(own_band, (("tile", 0),), 1)
    encoded = jax.nn.relu(convolve(padded, encoder_weight) + encoder_bias).astype(jnp.bfloat16)
    encoded_padded = padded_2(encoded, (("tile", 0),), 1)
    hidden = jax.nn.relu(convolve(encoded_padded, head_weight) + head_bias).astype(jnp.bfloat16)
    feature_count = hidden.shape[2]
    raw_output = (
        jnp.dot(hidden.reshape(-1, feature_count), final_weight, preferred_element_type=jnp.float32)
        + final_bias
    )
    described = (
        raw_output / jnp.sqrt(jnp.sum(raw_output * raw_output, axis=-1, keepdims=True) + 1e-06)
    ).astype(jnp.bfloat16)
    block_count = band_rows * band_cols // BLOCK
    own_blocks = described.reshape(block_count, BLOCK, feature_count)
    own_folds = fold_mask[0].reshape(block_count, BLOCK).astype(jnp.bfloat16)
    pair_count = pair_source.shape[1]
    capacity = max(2, 2 * pair_count // tile_count)
    wanted_by_others = lax.dynamic_index_in_dim(
        pair_target, 1 - section, 0, keepdims=False
    ).reshape(tile_count, pair_count)
    matched = (wanted_by_others // block_count == tile_here).astype(jnp.int32)
    order_rank = jnp.cumsum(matched, axis=1) - matched
    slot_hot = matched[:, :, None] * (
        order_rank[:, :, None] == jnp.arange(capacity)[None, None, :]
    ).astype(jnp.int32)
    chosen = jnp.sum(slot_hot * (wanted_by_others % block_count)[:, :, None], axis=1)
    send_blocks = own_blocks[chosen]
    send_folds = own_folds[chosen]
    moved_blocks, moved_folds = (
        lax.all_to_all(send_blocks, "tile", split_axis=0, concat_axis=0, tiled=True),
        lax.all_to_all(send_folds, "tile", split_axis=0, concat_axis=0, tiled=True),
    )
    arrived_blocks, arrived_folds = swapped((moved_blocks, moved_folds), "sec", 0)
    own_targets = lax.dynamic_index_in_dim(pair_target, section, 0, keepdims=False).reshape(
        tile_count, pair_count
    )
    own_targets = lax.dynamic_index_in_dim(own_targets, tile_here, 0, keepdims=False)
    owners = own_targets // block_count
    earlier = jnp.arange(pair_count)[None, :] < jnp.arange(pair_count)[:, None]
    slot_rank = jnp.sum(((owners[None, :] == owners[:, None]) & earlier).astype(jnp.int32), axis=1)
    slot_index = owners * capacity + slot_rank
    partner = arrived_blocks.reshape(tile_count * capacity, BLOCK, feature_count)[slot_index]
    partner_folds = arrived_folds.reshape(tile_count * capacity, BLOCK)[slot_index].astype(
        jnp.float32
    )
    anchor = own_blocks[pair_source[0]]
    anchor_folds = own_folds[pair_source[0]].astype(jnp.float32)
    products = jnp.einsum("pid,pjd->pij", anchor, partner, preferred_element_type=jnp.float32)
    scores = SCORE_SCALE * products - FOLD_PENALTY * (
        anchor_folds[:, :, None] + partner_folds[:, None, :]
    )
    confidence = dual_score(scores)
    return (described.reshape(1, band_rows, band_cols, feature_count), confidence[None])


def solution(mesh):
    return jax.shard_map(
        local,
        mesh=mesh,
        in_specs=(
            P("sec", "tile", None, None),
            P("sec", "tile", None),
            P(),
            P(),
            P(),
            P(),
            P(),
            P(),
            P("sec", "tile"),
            P(),
        ),
        out_specs=(P("sec", "tile", None, None), P("sec", "tile", None)),
        check_vma=False,
    )
```

profile of v0, /device:TPU:1, one launch (start us, length us, event | category | flops | bytes accessed | tf_op | source)
XLA Modules:
  0.0 312.5 jit_solution(5655124264255456980)
XLA Ops:
  1.6 4.4 %collective-permute-start = (bf16[1,384,128]{2,1,0:T(8,128)(2,1)S(1)}, bf16[1,384,128]{2,1,0:T(8,128)(2,1)S(1)}, u32[]{:S(2)}, u32[]{:S(2)}) collective-permute-start(bf16[1,384,128]{2,1,0:T(8,128)(2,1)S(1)} %get-tuple-element.26), channel_id=1, source_target_pairs={{0,2},{2,4},{4,6},{6,8},{8,10},{10,12},{12,14},{14,16},{16,18},{18... | collective-permute-start | bytes 294920 | tf_op jit(solution)/shard_map/ppermute | solution.py:18
  12.2 4.1 %fusion.14 = bf16[34,386,128]{2,1,0:T(8,128)(2,1)S(1)} fusion(bf16[1,384,128]{2,1,0:T(8,128)(2,1)S(1)} %collective-permute-done.1, bf16[32,384,128]{2,1,0:T(8,128)(2,1)} %bitcast.141, bf16[1,384,128]{2,1,0:T(8,128)(2,1)S(1)} %collective-permute-done), kind=kLoop, calls=%fused_computation.47 | loop fusion | flops 20158464 | bytes 6702080 | tf_op jit(solution)/shard_map/concatenate | solution.py:22
  16.3 7.2 %fusion.83 = (bf16[32,384,128]{2,1,0:T(8,128)(2,1)S(1)}, bf16[32,384,128]{2,1,0:T(8,128)(2,1)S(1)}, bf16[32,384,128]{2,1,0:T(8,128)(2,1)S(1)}, bf16[32,384,128]{...) fusion(bf16[34,386,128]{2,1,0:T(8,128)(2,1)S(1)} %fusion.14), kind=kLoop, calls=%fused_computation.143 | loop fusion | bytes 37748736 | tf_op jit(solution)/shard_map/slice | solution.py:44
  23.5 3.0 fusion.49
  28.4 2.1 pad_maximum_fusion.2
  41.0 3.4 %collective-permute-start.2 = (bf16[1,384,128]{2,1,0:T(8,128)(2,1)S(1)}, bf16[1,384,128]{2,1,0:T(8,128)(2,1)S(1)}, u32[]{:S(2)}, u32[]{:S(2)}) collective-permute-start(bf16[1,384,128]{2,1,0:T(8,128)(2,1)S(1)} %get-tuple-element.22), channel_id=1, source_target_pairs={{0,2},{2,4},{4,6},{6,8},{8,10},{10,12},{12,14},{14,16},{16,18},{18... | collective-permute-start | bytes 294920 | tf_op jit(solution)/shard_map/ppermute | solution.py:18
  46.0 3.7 %collective-permute-done.3 = bf16[1,384,128]{2,1,0:T(8,128)(2,1)S(1)} collective-permute-done((bf16[1,384,128]{2,1,0:T(8,128)(2,1)S(1)}, bf16[1,384,128]{2,1,0:T(8,128)(2,1)S(1)}, u32[]{:S(2)}, u32[]{:S(2)}) %collective-permute-start.3) | collective-permute-done | bytes 98336 | tf_op jit(solution)/shard_map/ppermute | solution.py:21
  49.8 2.5 select_maximum_fusion
  52.3 6.5 %fusion.82 = (bf16[32,384,128]{2,1,0:T(8,128)(2,1)}, bf16[32,384,128]{2,1,0:T(8,128)(2,1)}, bf16[32,384,128]{2,1,0:T(8,128)(2,1)}, bf16[32,384,128]{2,1,0:T(8,12...) fusion(bf16[34,386,128]{2,1,0:T(8,128)(2,1)S(1)} %select_maximum_fusion), kind=kLoop, calls=%fused_computation.142 | loop fusion | bytes 37748736 | tf_op jit(solution)/shard_map/slice | solution.py:44
  60.5 3.2 %pad_maximum_fusion = (bf16[32,384,128]{2,1,0:T(8,128)(2,1)}, bf16[32,384,128]{2,1,0:T(8,128)(2,1)}) fusion(bf16[1,384,128]{2,1,0:T(8,128)(2,1)S(1)} %collective-permute-done.3, bf16[32,384,128]{2,1,0:T(8,128)(2,1)S(1)} %maximum_convert_fusion.1, bf16[1,384,128]{2,1,0:T(8,128)(2,1)S(1)} %collective-permute-done.2), kind=kLoop, calls=%fused_computation.48 | loop fusion | flops 3145728 | bytes 9633792 | tf_op jit(solution)/shard_map/concatenate | solution.py:22
  63.7 3.7 %convolution_add_fusion.7 = f32[12288,256]{1,0:T(8,128)S(1)} fusion(f32[12288,256]{1,0:T(8,128)S(1)} %fusion.28, bf16[12288,128]{1,0:T(8,128)(2,1)} %bitcast.154, bf16[3,3,128,256]{3,2,1,0:T(8,128)(2,1)S(1)} %copy-done.8), kind=kOutput, calls=%fused_computation.18 | convolution fusion | flops 808452096 | bytes 28377088 | tf_op jit(solution)/shard_map/dot_general | solution.py:47
  67.4 3.7 %convolution_add_fusion.6 = f32[12288,256]{1,0:T(8,128)S(1)} fusion(f32[12288,256]{1,0:T(8,128)S(1)} %convolution_add_fusion.7, bf16[12288,128]{1,0:T(8,128)(2,1)} %bitcast.153, bf16[3,3,128,256]{3,2,1,0:T(8,128)(2,1)S(1)} %copy-done.8), kind=kOutput, calls=%fused_computation.17 | convolution fusion | flops 808452096 | bytes 28377088 | tf_op jit(solution)/shard_map/dot_general | solution.py:47
  71.0 8.2 %convolution_add_fusion.5 = f32[12288,256]{1,0:T(8,128)} fusion(f32[12288,256]{1,0:T(8,128)S(1)} %convolution_add_fusion.6, bf16[12288,128]{1,0:T(8,128)(2,1)} %bitcast.152, bf16[3,3,128,256]{3,2,1,0:T(8,128)(2,1)S(1)} %copy-done.8), kind=kOutput, calls=%fused_computation.16 | convolution fusion | flops 808452096 | bytes 28377088 | tf_op jit(solution)/shard_map/dot_general | solution.py:47
  79.3 8.3 %convolution_add_fusion.4 = f32[12288,256]{1,0:T(8,128)S(1)} fusion(f32[12288,256]{1,0:T(8,128)} %convolution_add_fusion.5, f32[12288,128]{1,0:T(8,128)} %copy-done.1, f32[128]{0:T(128)S(1)} %copy-done.14, bf16[3,3,128,256]{3,2,1,0:T(8,128)(2,1)S(1)} %copy-done.8), kind=kOutput, calls=%fused_computation.15 | convolution fusion | flops 813170688 | bytes 31523328 | tf_op jit(solution)/shard_map/dot_general | solution.py:47
  87.6 6.3 %fusion.19 = f32[12288,256]{1,0:T(8,128)} fusion(bf16[12288,128]{1,0:T(8,128)(2,1)S(1)} %bitcast.157, bf16[3,3,128,256]{3,2,1,0:T(8,128)(2,1)S(1)} %copy-done.8), kind=kOutput, calls=%fused_computation.58 | convolution fusion | flops 805306368 | bytes 15794176 | tf_op jit(solution)/shard_map/dot_general | solution.py:47
  94.0 6.2 %convolution_add_fusion.3 = f32[12288,256]{1,0:T(8,128)} fusion(f32[12288,256]{1,0:T(8,128)S(1)} %convolution_add_fusion.4, bf16[12288,128]{1,0:T(8,128)(2,1)S(1)} %bitcast.151, bf16[3,3,128,256]{3,2,1,0:T(8,128)(2,1)S(1)} %copy-done.8), kind=kOutput, calls=%fused_computation.14 | convolution fusion | flops 808452096 | bytes 28377088 | tf_op jit(solution)/shard_map/dot_general | solution.py:47
  100.3 10.8 %convolution_add_fusion.2 = f32[12288,256]{1,0:T(8,128)} fusion(f32[12288,256]{1,0:T(8,128)} %convolution_add_fusion.3, bf16[12288,128]{1,0:T(8,128)(2,1)S(1)} %bitcast.150, bf16[3,3,128,256]{3,2,1,0:T(8,128)(2,1)S(1)} %copy-done.8), kind=kOutput, calls=%fused_computation.13 | convolution fusion | flops 808452096 | bytes 28377088 | tf_op jit(solution)/shard_map/dot_general | solution.py:47
  111.1 10.8 %fusion.7 = bf16[12288,256]{1,0:T(8,128)(2,1)S(1)} fusion(f32[12288,256]{1,0:T(8,128)} %fusion.19, f32[12288,256]{1,0:T(8,128)} %convolution_add_fusion.2, bf16[12288,128]{1,0:T(8,128)(2,1)} %bitcast.159, f32[256]{0:T(256)S(1)} %copy-done.16, bf16[3,3,128,256]{3,2,1,0:T(8,128)(2,1)S(1)} %copy-done.8), kind=kOutput, calls=%fused_computation.21 | convolution fusion | flops 821035008 | bytes 34669568 | tf_op jit(solution)/shard_map/dot_general | solution.py:47
  121.9 1.9 multiply_reduce_fusion
  123.9 3.9 %divide_convert_fusion = bf16[12288,256]{1,0:T(8,128)(2,1)} fusion(f32[12288,256]{1,0:T(8,128)S(1)} %get-tuple-element.29, f32[12288]{0:T(1024)S(1)} %add_sqrt_fusion), kind=kLoop, calls=%fused_computation.30 | loop fusion | flops 6291456 | bytes 18923520 | tf_op jit(solution)/shard_map/convert_element_type | solution.py:92
  127.8 9.2 %gather_fusion.1 = bf16[128,128,256]{2,1,0:T(8,128)(2,1)} fusion(bf16[96,128,256]{2,1,0:T(8,128)(2,1)} %bitcast.138, s32[1024]{0:T(1024)S(1)} %pad_clamp_fusion.1), kind=kCustom, calls=%fused_computation.1 | custom fusion | bytes 16777728 | tf_op jit(solution)/shard_map/gather | solution.py:107
  137.0 112.0 %all_to_all.10 = bf16[64,2,128,256]{3,2,1,0:T(8,128)(2,1)} all-to-all(bf16[64,2,128,256]{3,2,1,0:T(8,128)(2,1)} %bitcast.144), channel_id=1, replica_groups=mesh['tile'=64,'sec'=2] {'tile'}, dimensions={0} | all-to-all | bytes 16777216 | tf_op jit(solution)/shard_map/all_to_all | solution.py:110
  249.0 3.9 %collective-permute-start.4 = (bf16[64,2,128,256]{3,2,1,0:T(8,128)(2,1)}, bf16[64,2,128,256]{3,2,1,0:T(8,128)(2,1)}, u32[]{:S(2)}, u32[]{:S(2)}) collective-permute-start(bf16[64,2,128,256]{3,2,1,0:T(8,128)(2,1)} %all_to_all.10), channel_id=1, source_target_pairs={{0,1},{1,0},{2,3},{3,2},{4,5},{5,4},{6,7},{7,6},{8,9},{9,8},{10,11... | collective-permute-start | bytes 25165832 | tf_op jit(solution)/shard_map/ppermute | solution.py:33
  254.3 5.0 %all-to-all-start.1 = ((bf16[64,2,128]{2,1,0:T(2,128)(2,1)}), bf16[64,2,128]{2,1,0:T(2,128)(2,1)S(1)}, u32[]{:S(2)}, u32[]{:S(2)}) async-start(bf16[64,2,128]{2,1,0:T(2,128)(2,1)} %bitcast.53), calls=%async_computation.1 | async-start | bytes 65536 | tf_op jit(solution)/shard_map/all_to_all | solution.py:111
  259.6 8.0 %all-to-all-done.1 = bf16[64,2,128]{2,1,0:T(2,128)(2,1)S(1)} async-done(((bf16[64,2,128]{2,1,0:T(2,128)(2,1)}), bf16[64,2,128]{2,1,0:T(2,128)(2,1)S(1)}, u32[]{:S(2)}, u32[]{:S(2)}) %all-to-all-start.1) | async-done | bytes 32800 | tf_op jit(solution)/shard_map/all_to_all | solution.py:111
  270.6 5.5 %gather_fusion = bf16[64,128,256]{2,1,0:T(8,128)(2,1)} fusion(bf16[96,128,256]{2,1,0:T(8,128)(2,1)} %bitcast.139, s32[1024]{0:T(1024)S(1)} %pad_clamp_fusion.2), kind=kCustom, calls=%fused_computation | custom fusion | bytes 8388864 | tf_op jit(solution)/shard_map/gather | solution.py:126
  276.1 6.2 %gather_fusion.2 = bf16[64,128,256]{2,1,0:T(8,128)(2,1)} fusion(bf16[128,128,256]{2,1,0:T(8,128)(2,1)} %bitcast.45, s32[1024]{0:T(1024)S(1)} %pad_clamp_fusion), kind=kCustom, calls=%fused_computation.2 | custom fusion | bytes 8388864 | tf_op jit(solution)/shard_map/gather | solution.py:122
  282.3 6.6 %fusion.85 = f32[64,128,128]{1,2,0:T(8,128)} fusion(bf16[64,128,256]{2,1,0:T(8,128)(2,1)} %gather_fusion, bf16[64,128,256]{2,1,0:T(8,128)(2,1)} %gather_fusion.2), kind=kOutput, calls=%fused_computation.145 | convolution fusion | flops 536870912 | bytes 12582912 | tf_op jit(solution)/shard_map/pid,pjd->pij/dot_general | solution.py:128
  288.9 4.6 %fusion.2 = f32[64,128,128]{1,2,0:T(8,128)} fusion(f32[64,128,128]{1,2,0:T(8,128)} %fusion.85, f32[64,128]{1,0:T(8,128)S(1)} %convert_element_type.63, f32[64,128]{1,0:T(8,128)S(1)} %convert_element_type.62), kind=kOutput, calls=%fused_computation.8 | output fusion | flops 5259518 | bytes 8454144 | tf_op jit(solution)/shard_map/div | solution.py:56
  293.5 4.3 %subtract_exponential_fusion.1 = f32[64,128,128]{1,2,0:T(8,128)} fusion(f32[64,128,128]{1,2,0:T(8,128)} %fusion.85, f32[64,128]{1,0:T(8,128)S(1)} %convert_element_type.63, f32[64,128]{1,0:T(8,128)S(1)} %convert_element_type.62), kind=kOutput, calls=%fused_computation.39 | output fusion | flops 5251199 | bytes 8454144 | tf_op jit(solution)/shard_map/sub | solution.py:55
  297.8 6.6 %fusion = f32[64,128,128]{1,2,0:T(8,128)} fusion(f32[64,128,128]{1,2,0:T(8,128)} %fusion.85, f32[64,128]{1,0:T(8,128)S(1)} %convert_element_type.63, f32[64,128]{1,0:T(8,128)S(1)} %convert_element_type.62), kind=kOutput, calls=%fused_computation.6 | output fusion | flops 5259518 | bytes 8454144 | tf_op jit(solution)/shard_map/div | solution.py:59
  304.5 7.9 %multiply_reduce_fusion.1 = f32[64,128]{1,0:T(8,128)} fusion(f32[64,128,128]{1,2,0:T(8,128)} %fusion, f32[64,128,128]{1,2,0:T(8,128)} %subtract_exponential_fusion.1, f32[64,128,128]{1,2,0:T(8,128)} %fusion.2, f32[64,128,128]{1,2,0:T(8,128)} %fusion.85, f32[64,128]{1,0:T(8,128)S(1)} %convert_element_type.63, f32[64,128]{1,0:T(8,128)S(1)} %convert_element_type.62), kind=kOutput, calls=%fused_computation.37 | output fusion | flops 9437311 | bytes 16875520 | tf_op jit(solution)/shard_map/sub | solution.py:58
  (86 shorter events, 27.4 us)
Async XLA Ops:
  0.6 121.3 %copy-start = (bf16[256,256]{1,0:T(8,128)(2,1)S(1)}, bf16[256,256]{1,0:T(8,128)(2,1)}, u32[]{:S(2)}) copy-start(bf16[256,256]{1,0:T(8,128)(2,1)} %param.16) | copy-start | bytes 393220
  1.6 9.0 %collective-permute-start = (bf16[1,384,128]{2,1,0:T(8,128)(2,1)S(1)}, bf16[1,384,128]{2,1,0:T(8,128)(2,1)S(1)}, u32[]{:S(2)}, u32[]{:S(2)}) collective-permute-start(bf16[1,384,128]{2,1,0:T(8,128)(2,1)S(1)} %get-tuple-element.26), channel_id=1, source_target_pairs={{0,2},{2,4},{4,6},{6,8},{8,10},{10,12},{12,14},{14,16},{16,18},{18... | collective-permute-start | bytes 294920 | tf_op jit(solution)/shard_map/ppermute | solution.py:18
  6.0 5.5 %collective-permute-start.1 = (bf16[1,384,128]{2,1,0:T(8,128)(2,1)S(1)}, bf16[1,384,128]{2,1,0:T(8,128)(2,1)S(1)}, u32[]{:S(2)}, u32[]{:S(2)}) collective-permute-start(bf16[1,384,128]{2,1,0:T(8,128)(2,1)S(1)} %get-tuple-element.27), channel_id=1, source_target_pairs={{2,0},{4,2},{6,4},{8,6},{10,8},{12,10},{14,12},{16,14},{18,16},{20... | collective-permute-start | bytes 294920 | tf_op jit(solution)/shard_map/ppermute | solution.py:21
  11.6 0.6 copy-start.9
  23.5 3.0 copy-start.5
  23.5 3.0 copy-start.11
  26.5 1.9 copy-start.2
  26.5 1.9 copy-start.10
  35.4 1.9 copy-start.7
  37.3 1.0 copy-start.14
  38.3 2.7 copy-start.1
  41.0 5.0 %collective-permute-start.2 = (bf16[1,384,128]{2,1,0:T(8,128)(2,1)S(1)}, bf16[1,384,128]{2,1,0:T(8,128)(2,1)S(1)}, u32[]{:S(2)}, u32[]{:S(2)}) collective-permute-start(bf16[1,384,128]{2,1,0:T(8,128)(2,1)S(1)} %get-tuple-element.22), channel_id=1, source_target_pairs={{0,2},{2,4},{4,6},{6,8},{8,10},{10,12},{12,14},{14,16},{16,18},{18... | collective-permute-start | bytes 294920 | tf_op jit(solution)/shard_map/ppermute | solution.py:18
  44.4 5.4 %collective-permute-start.3 = (bf16[1,384,128]{2,1,0:T(8,128)(2,1)S(1)}, bf16[1,384,128]{2,1,0:T(8,128)(2,1)S(1)}, u32[]{:S(2)}, u32[]{:S(2)}) collective-permute-start(bf16[1,384,128]{2,1,0:T(8,128)(2,1)S(1)} %get-tuple-element.23), channel_id=1, source_target_pairs={{2,0},{4,2},{6,4},{8,6},{10,8},{12,10},{14,12},{16,14},{18,16},{20... | collective-permute-start | bytes 294920 | tf_op jit(solution)/shard_map/ppermute | solution.py:21
  52.3 6.5 %copy-start.8 = (bf16[3,3,128,256]{3,2,1,0:T(8,128)(2,1)S(1)}, bf16[3,3,128,256]{3,2,1,0:T(8,128)(2,1)}, u32[]{:S(2)}) copy-start(bf16[3,3,128,256]{3,2,1,0:T(8,128)(2,1)} %param.14) | copy-start | bytes 1769476
  79.3 8.3 %copy-start.6 = (bf16[32,384,128]{2,1,0:T(8,128)(2,1)S(1)}, bf16[32,384,128]{2,1,0:T(8,128)(2,1)}, u32[]{:S(2)}) copy-start(bf16[32,384,128]{2,1,0:T(8,128)(2,1)} %get-tuple-element.13) | copy-start | bytes 9437188
  87.6 6.4 %copy-start.4 = (bf16[32,384,128]{2,1,0:T(8,128)(2,1)S(1)}, bf16[32,384,128]{2,1,0:T(8,128)(2,1)}, u32[]{:S(2)}) copy-start(bf16[32,384,128]{2,1,0:T(8,128)(2,1)} %get-tuple-element.9) | copy-start | bytes 9437188
  94.0 6.3 %copy-start.3 = (bf16[32,384,128]{2,1,0:T(8,128)(2,1)S(1)}, bf16[32,384,128]{2,1,0:T(8,128)(2,1)}, u32[]{:S(2)}) copy-start(bf16[32,384,128]{2,1,0:T(8,128)(2,1)} %get-tuple-element.8) | copy-start | bytes 9437188
  100.2 10.9 %copy-start.16 = (f32[256]{0:T(256)S(1)}, f32[256]{0:T(256)}, u32[]{:S(2)}) copy-start(f32[256]{0:T(256)} %param.15) | copy-start | bytes 3076
  111.1 10.8 %copy-start.15 = (f32[256]{0:T(256)S(1)}, f32[256]{0:T(256)}, u32[]{:S(2)}) copy-start(f32[256]{0:T(256)} %param.17) | copy-start | bytes 3076
  137.0 115.9 %copy-start.13 = (s32[1,32,384]{2,1,0:T(8,128)S(1)}, s32[1,32,384]{2,1,0:T(8,128)}, u32[]{:S(2)}) copy-start(s32[1,32,384]{2,1,0:T(8,128)} %param.11) | copy-start | bytes 147460
  137.0 122.3 %copy-start.12 = (s32[4096]{0:T(1024)S(1)}, s32[4096]{0:T(1024)}, u32[]{:S(2)}) copy-start(s32[4096]{0:T(1024)} %get-tuple-element.2) | copy-start | bytes 49156
  137.0 122.6 %copy-start.17 = (s32[1,64]{1,0:T(1,128)S(1)}, s32[1,64]{1,0:T(1,128)}, u32[]{:S(2)}) copy-start(s32[1,64]{1,0:T(1,128)} %param.18) | copy-start | bytes 772
  249.0 27.1 %collective-permute-start.4 = (bf16[64,2,128,256]{3,2,1,0:T(8,128)(2,1)}, bf16[64,2,128,256]{3,2,1,0:T(8,128)(2,1)}, u32[]{:S(2)}, u32[]{:S(2)}) collective-permute-start(bf16[64,2,128,256]{3,2,1,0:T(8,128)(2,1)} %all_to_all.10), channel_id=1, source_target_pairs={{0,1},{1,0},{2,3},{3,2},{4,5},{5,4},{6,7},{7,6},{8,9},{9,8},{10,11... | collective-permute-start | bytes 25165832 | tf_op jit(solution)/shard_map/ppermute | solution.py:33
  254.3 13.3 %all-to-all-start.1 = ((bf16[64,2,128]{2,1,0:T(2,128)(2,1)}), bf16[64,2,128]{2,1,0:T(2,128)(2,1)S(1)}, u32[]{:S(2)}, u32[]{:S(2)}) async-start(bf16[64,2,128]{2,1,0:T(2,128)(2,1)} %bitcast.53), calls=%async_computation.1 | async-start | bytes 65536 | tf_op jit(solution)/shard_map/all_to_all | solution.py:111
  267.6 2.3 collective-permute-start.5
where the time goes:
time: 319 us; the launch traced here: 313 us
  blocking collectives  112 us (35%)
  matrix products  79.3 us (25%)
  other arithmetic  43.2 us (14%)
  local copies, waits for them, and re-layouts  43 us (13%)
  starting transfers between devices  20.7 us (6%)
  waiting for transfers between devices  13.2 us (4%)
    all_to_all x1, blocking collectives, local(): lax.all_to_all(send_blocks, 'tile', split_axis=0, concat_axis=0, tiled=True)  112 us
    dot_general x18, matrix products, convolve(): jnp.dot(window, kernel[down_shift, side_shift], preferred_element_type=jn...  70.8 us
    slice x2, local copies, waits for them, and re-layouts, convolve(): framed[down_shift:down_shift + height, side_shift:side_shift + span_cols, :]  13.7 us
    concatenate x4, other arithmetic, padded_2(): block = jnp.concatenate([low, block, high], axis=dim)  11.8 us
    gather x1, local copies, waits for them, and re-layouts, local(): send_blocks = own_blocks[chosen]  9.21 us
    all_to_all x1, waiting for transfers between devices, local(): lax.all_to_all(send_folds, 'tile', split_axis=0, concat_axis=0, tiled=True)  7.99 us
    sub x1, other arithmetic, dual_score(): column_weight = jnp.exp(scores - column_peak)  7.87 us
    ppermute x2, starting transfers between devices, padded_2(): lax.ppermute(lax.slice_in_dim(block, block.shape[dim] - width, None, axis...  7.75 us
  transfers between devices with their start and end apart: 7, of which 5 were waited for; matrix products, arithmetic and copies ran while one was open for 4% of the time, Pallas kernels for 0%

commit v1 on v0

v1 whole, which is shorter than its diff:
```python
import functools

import jax
import jax.numpy as jnp
from jax import lax
from jax.experimental import pallas as pl
from jax.experimental.pallas import tpu as pltpu
from jax.sharding import PartitionSpec as P

BLOCK = 128
SCORE_SCALE = 10.0
FOLD_PENALTY = 200.0
ROWS_STEP = 4
PAIRS_STEP = 8


def side_copies(rows):
    cols = rows.shape[1]
    flat = rows.reshape(rows.shape[0] * cols, rows.shape[2])
    column = lax.broadcasted_iota(jnp.int32, rows.shape, 1).reshape(flat.shape)
    before = jnp.where(column == 0, 0.0, pltpu.roll(flat, 1, 0))
    after = jnp.where(column == cols - 1, 0.0, pltpu.roll(flat, flat.shape[0] - 1, 0))
    return [v.reshape(rows.shape).astype(jnp.bfloat16) for v in (before, flat, after)]


def describe_kernel(
    edge_ref, low_ref, own_ref, high_ref, enc_w_ref, enc_b_ref, head_w_ref, head_b_ref,
    final_w_ref, final_b_ref, out_ref, wide_ref, enc_ref, pair_w_ref,
):
    step = pl.program_id(0)
    last = pl.num_programs(0) - 1
    chan = own_ref.shape[2]

    def put_features(first, rows):
        for b, copy in enumerate(side_copies(rows.astype(jnp.float32))):
            wide_ref[pl.ds(first, 2), :, b * chan : (b + 1) * chan] = copy

    def encode(first):
        window = jnp.concatenate([wide_ref[first + a] for a in range(4)], axis=-1)
        both = jnp.dot(window, pair_w_ref[...], preferred_element_type=jnp.float32)
        both = jnp.maximum(both + enc_b_ref[...], 0.0)
        keep = [
            jnp.logical_not((first + d == edge_ref[0]) | (first + d == edge_ref[1]))
            for d in range(2)
        ]
        rows = jnp.stack(
            [jnp.where(keep[d], both[:, d * chan : (d + 1) * chan], 0.0) for d in range(2)]
        )
        for b, copy in enumerate(side_copies(rows)):
            enc_ref[pl.ds(first, 2), :, b * chan : (b + 1) * chan] = copy

    @pl.when(step == 0)
    def _():
        for p in range(4):
            for b in range(3):
                k = pl.ds((p * 3 + b) * chan, chan)
                zero = jnp.zeros((chan, chan), jnp.bfloat16)
                pair_w_ref[k, 0:chan] = enc_w_ref[p, b] if p < 3 else zero
                pair_w_ref[k, chan : 2 * chan] = enc_w_ref[p - 1, b] if p > 0 else zero
        put_features(0, low_ref[...])
        put_features(2, own_ref[pl.ds(0, 2)])
        encode(0)

    base = step * ROWS_STEP
    put_features(base + 4, own_ref[pl.ds(base + 2, 2)])

    @pl.when(step < last)
    def _():
        put_features(base + 6, own_ref[pl.ds(base + 4, 2)])

    @pl.when(step == last)
    def _():
        put_features(base + 6, high_ref[...])

    encode(base + 2)
    encode(base + 4)
    for r in range(0, ROWS_STEP, 2):
        parts = [enc_ref[pl.ds(base + r + a, 2)] for a in range(3)]
        cols = parts[0].shape[1]
        window = jnp.concatenate([v.reshape(2 * cols, 3 * chan) for v in parts], axis=-1)
        hidden = jnp.dot(window, head_w_ref[...], preferred_element_type=jnp.float32)
        hidden = jnp.maximum(hidden + head_b_ref[...], 0.0).astype(jnp.bfloat16)
        raw = jnp.dot(hidden, final_w_ref[...], preferred_element_type=jnp.float32)
        raw = raw + final_b_ref[...]
        norm = jnp.sum(raw * raw, axis=-1, keepdims=True)
        unit = (raw * lax.rsqrt(norm + 1e-06)).astype(jnp.bfloat16)
        out_ref[pl.ds(r, 2)] = unit.reshape(2, cols, unit.shape[1])


def describe(edge, low, own, high, enc_w, enc_b, head_w, head_b, final_w, final_b):
    rows, cols, chan = own.shape
    desc = final_w.shape[1]
    whole = pl.BlockSpec(memory_space=pltpu.VMEM)
    macs = rows * cols * (12 * chan * chan + 9 * chan * desc + desc * desc)
    return pl.pallas_call(
        describe_kernel,
        grid=(rows // ROWS_STEP,),
        in_specs=[pl.BlockSpec(memory_space=pltpu.SMEM)] + [whole] * 9,
        out_specs=pl.BlockSpec((ROWS_STEP, cols, desc), lambda i: (i, 0, 0)),
        out_shape=jax.ShapeDtypeStruct((rows, cols, desc), jnp.bfloat16),
        scratch_shapes=[
            pltpu.VMEM((rows + 4, cols, 3 * chan), jnp.bfloat16),
            pltpu.VMEM((rows + 2, cols, 3 * chan), jnp.bfloat16),
            pltpu.VMEM((12 * chan, 2 * chan), jnp.bfloat16),
        ],
        compiler_params=pltpu.CompilerParams(vmem_limit_bytes=56 * 2**20),
        cost_estimate=pl.CostEstimate(
            flops=2 * macs, bytes_accessed=rows * cols * (chan + desc) * 2, transcendentals=rows * cols
        ),
    )(
        edge, low, own, high, enc_w, jnp.tile(enc_b, 2)[None], head_w.reshape(-1, desc),
        head_b[None], final_w, final_b[None],
    )


def match_kernel(source_ref, slot_ref, anchor_fold_ref, partner_fold_ref, *refs):
    anchors, partners, out_ref = refs[:PAIRS_STEP], refs[PAIRS_STEP : 2 * PAIRS_STEP], refs[-1]
    first = pl.program_id(0) * PAIRS_STEP
    folds = jnp.concatenate(
        [partner_fold_ref[pl.ds(slot_ref[first + n], 1)] for n in range(PAIRS_STEP)]
    )
    folds = jnp.transpose(folds)
    for n in range(PAIRS_STEP):
        products = lax.dot_general(
            partners[n][0], anchors[n][0], (((1,), (1,)), ((), ())),
            preferred_element_type=jnp.float32,
        )
        penalty = anchor_fold_ref[pl.ds(source_ref[first + n], 1)] + folds[:, n : n + 1]
        scores = SCORE_SCALE * products - FOLD_PENALTY * penalty
        over_j = jnp.exp(scores - jnp.max(scores, axis=0, keepdims=True))
        over_i = jnp.exp(scores - jnp.max(scores, axis=1, keepdims=True))
        sum_j = jnp.sum(over_j, axis=0, keepdims=True)
        sum_i = jnp.sum(over_i, axis=1, keepdims=True)
        best = jnp.max(over_j * (over_i * (1.0 / sum_i)), axis=0, keepdims=True)
        out_ref[n : n + 1, :] = best / sum_j


def match(source, slot, anchor_folds, partner_folds, blocks, arrived):
    pairs = source.shape[0]
    shape = (1,) + blocks.shape[1:]

    def spec(which, n):
        return pl.BlockSpec(shape, lambda i, s, t: ((s, t)[which][i * PAIRS_STEP + n], 0, 0))

    return pl.pallas_call(
        match_kernel,
        grid_spec=pltpu.PrefetchScalarGridSpec(
            num_scalar_prefetch=2,
            grid=(pairs // PAIRS_STEP,),
            in_specs=[pl.BlockSpec(memory_space=pltpu.VMEM)] * 2
            + [spec(0, n) for n in range(PAIRS_STEP)]
            + [spec(1, n) for n in range(PAIRS_STEP)],
            out_specs=pl.BlockSpec((PAIRS_STEP, BLOCK), lambda i, s, t: (i, 0)),
        ),
        out_shape=jax.ShapeDtypeStruct((pairs, BLOCK), jnp.float32),
        compiler_params=pltpu.CompilerParams(vmem_limit_bytes=32 * 2**20),
    )(
        source, slot, anchor_folds, partner_folds,
        *([blocks] * PAIRS_STEP), *([arrived] * PAIRS_STEP),
    )


def pick_kernel(chosen_ref, blocks_ref, out_ref, sem):
    count = out_ref.shape[0]

    def copy(n):
        return pltpu.make_async_copy(blocks_ref.at[chosen_ref[n]], out_ref.at[n], sem)

    pl.loop(0, count)(lambda n: copy(n).start())
    pltpu.make_async_copy(out_ref, out_ref, sem).wait()


def pick(chosen, blocks):
    count = chosen.shape[0]
    return pl.pallas_call(
        pick_kernel,
        in_specs=[pl.BlockSpec(memory_space=pltpu.SMEM), pl.BlockSpec(memory_space=pl.ANY)],
        out_specs=pl.BlockSpec(memory_space=pl.ANY),
        out_shape=jax.ShapeDtypeStruct((count,) + blocks.shape[1:], blocks.dtype),
        scratch_shapes=[pltpu.SemaphoreType.DMA],
    )(chosen, blocks)


def local(
    features, fold_mask, encoder_weight, encoder_bias, head_weight, head_bias,
    final_weight, final_bias, pair_source, pair_target,
):
    own_band = features[0]
    band_rows, band_cols, _ = own_band.shape
    tile_count = lax.axis_size("tile")
    tile_here = lax.axis_index("tile")
    section = lax.axis_index("sec")
    down = [(i, i + 1) for i in range(tile_count - 1)]
    up = [(j, i) for i, j in down]
    low = lax.ppermute(own_band[-2:], "tile", down)
    high = lax.ppermute(own_band[:2], "tile", up)
    edge = jnp.stack(
        [
            jnp.where(tile_here == 0, 0, -1),
            jnp.where(tile_here == tile_count - 1, band_rows + 1, -1),
        ]
    ).astype(jnp.int32)
    described = describe(
        edge, low, own_band, high, encoder_weight, encoder_bias, head_weight, head_bias,
        final_weight, final_bias,
    )
    desc = described.shape[2]
    block_count = band_rows * band_cols // BLOCK
    own_blocks = described.reshape(block_count, BLOCK, desc)
    own_folds = fold_mask[0].reshape(block_count, BLOCK).astype(jnp.bfloat16)
    pair_count = pair_source.shape[1]
    capacity = max(2, 2 * pair_count // tile_count)
    wanted_by_others = lax.dynamic_index_in_dim(
        pair_target, 1 - section, 0, keepdims=False
    ).reshape(tile_count, pair_count)
    matched = (wanted_by_others // block_count == tile_here).astype(jnp.int32)
    order_rank = jnp.cumsum(matched, axis=1) - matched
    slot_hot = matched[:, :, None] * (
        order_rank[:, :, None] == jnp.arange(capacity)[None, None, :]
    ).astype(jnp.int32)
    chosen = jnp.sum(slot_hot * (wanted_by_others % block_count)[:, :, None], axis=1)
    send_folds = own_folds[chosen]
    send_blocks = pick(chosen.reshape(-1), own_blocks).reshape(
        tile_count, capacity, BLOCK, desc
    )
    swap = [(0, 1), (1, 0)]
    arrived_folds = lax.ppermute(
        lax.all_to_all(send_folds, "tile", split_axis=0, concat_axis=0, tiled=True), "sec", swap
    )
    arrived_blocks = lax.ppermute(
        lax.all_to_all(send_blocks, "tile", split_axis=0, concat_axis=0, tiled=True), "sec", swap
    )
    own_targets = lax.dynamic_index_in_dim(pair_target, section, 0, keepdims=False).reshape(
        tile_count, pair_count
    )
    own_targets = lax.dynamic_index_in_dim(own_targets, tile_here, 0, keepdims=False)
    owners = own_targets // block_count
    earlier = jnp.arange(pair_count)[None, :] < jnp.arange(pair_count)[:, None]
    slot_rank = jnp.sum(((owners[None, :] == owners[:, None]) & earlier).astype(jnp.int32), axis=1)
    slot_index = owners * capacity + slot_rank
    confidence = match(
        pair_source[0],
        slot_index,
        fold_mask[0].reshape(block_count, BLOCK).astype(jnp.float32),
        arrived_folds.reshape(tile_count * capacity, BLOCK).astype(jnp.float32),
        own_blocks,
        arrived_blocks.reshape(tile_count * capacity, BLOCK, desc),
    )
    return (described.reshape(1, band_rows, band_cols, desc), confidence[None])


def solution(mesh):
    return jax.shard_map(
        local,
        mesh=mesh,
        in_specs=(
            P("sec", "tile", None, None), P("sec", "tile", None), P(), P(), P(), P(), P(), P(),
            P("sec", "tile"), P(),
        ),
        out_specs=(P("sec", "tile", None, None), P("sec", "tile", None)),
        check_vma=False,
    )
```

time: 319 us -> 449 us (1.41); the launches traced: 313 us -> 448 us
  Pallas kernels: 0 us -> 301 us
  matrix products: 79.3 us -> 0 us
  other arithmetic: 43.2 us -> 3.1 us
  local copies, waits for them, and re-layouts: 43 us -> 7.68 us
  starting transfers between devices: 20.7 us -> 16 us
    pallas_call x0 -> x3, Pallas kernels: none -> 301 us  [the longest x1 256 us: pick(): pl.pallas_call(pick_kernel, in_specs=[pl.BlockSpec(memory_space=pltpu.SME...]
    dot_general x20 -> x0, matrix products: 79.3 us -> none  [the longest x18 70.8 us: convolve(): jnp.dot(window, kernel[down_shift, side_shift], preferred_element_type=jn...]
    gather x5 -> x0, local copies, waits for them, and re-layouts: 22.2 us -> none  [the longest x1 9.21 us: local(): send_blocks = own_blocks[chosen]]
    slice x4 -> x1, local copies, waits for them, and re-layouts: 14.7 us -> 1.05 us  [local(): high = lax.ppermute(own_band[:2], 'tile', up)]
    sub x2 -> x0, other arithmetic: 12.2 us -> none  [the longest x1 7.87 us: dual_score(): column_weight = jnp.exp(scores - column_peak)]
    concatenate x4 -> x0, other arithmetic: 11.8 us -> none  [padded_2(): block = jnp.concatenate([low, block, high], axis=dim)]
    div x2 -> x1, other arithmetic: 11.3 us -> 1.02 us  [local(): matched = (wanted_by_others // block_count == tile_here).astype(jnp.int32)]
    ppermute x6 -> x4, starting transfers between devices: 15.7 us -> 10.9 us  [the longest x1 4.38 us: local(): low = lax.ppermute(own_band[-2:], 'tile', down)]
  transfers between devices with their start and end apart: 7 -> 5, of which waited for: 5 -> 3; matrix products, arithmetic and copies ran while one was open for 4% -> 1% of each run, Pallas kernels for 0% -> 0%
where the time goes in v1:
time: 449 us; the launch traced here: 448 us
  Pallas kernels  301 us (67%)
  blocking collectives  108 us (24%)
  starting transfers between devices  16 us (4%)
  waiting for transfers between devices  11.4 us (3%)
  local copies, waits for them, and re-layouts  7.68 us (2%)
    pallas_call x1, Pallas kernels, pick(): pl.pallas_call(pick_kernel, in_specs=[pl.BlockSpec(memory_space=pltpu.SME...  256 us
    all_to_all x1, blocking collectives, local(): lax.all_to_all(send_blocks, 'tile', split_axis=0, concat_axis=0, tiled=True)  108 us
    pallas_call x1, Pallas kernels, describe(): pl.pallas_call(describe_kernel, grid=(rows // ROWS_STEP,), in_specs=[pl.B...  31.9 us
    pallas_call x1, Pallas kernels, match(): pl.pallas_call(match_kernel, grid_spec=pltpu.PrefetchScalarGridSpec(num_s...  13.6 us
  transfers between devices with their start and end apart: 5, of which 3 were waited for; matrix products, arithmetic and copies ran while one was open for 1% of the time, Pallas kernels for 0%

profile of v1, /device:TPU:1, one launch (start us, length us, event | category | flops | bytes accessed | tf_op | source)
XLA Modules:
  0.0 448.2 jit_solution(10261541616554320425)
XLA Ops:
  0.6 1.1 slice_bitcast_fusion
  1.7 4.4 collective-permute-start
  6.1 1.3 collective-permute-start.1
  7.4 0.8 compare_reduce_fusion
  8.2 1.0 divide_reduce_fusion
  9.2 0.1 rem.49
  9.3 0.1 div.37
  9.4 0.1 ne.88
  9.5 0.2 reduce_window_sum.11
  9.8 0.1 multiply_reduce_fusion
  9.9 0.1 copy.17
  10.0 0.6 reshape.148.chosen_ref
  10.6 0.6 pad_add_fusion.edge_ref
  11.3 2.5 collective-permute-done.1.high_ref
  13.8 1.2 tile.2
  15.0 31.9 %shard_map.113 = bf16[32,384,256]{2,1,0:T(8,128)(2,1)} custom-call(s32[2]{0:T(128)} %pad_add_fusion.edge_ref, bf16[2,384,128]{2,1,0:T(8,128)(2,1)} %copy-done.3, bf16[32,384,128]{2,1,0:T(8,128)(2,1)} %bitcast.42, bf16[2,384,128]{2,1,0:T(8,128)(2,1)} %copy-done.4, bf16[3,3,128,128]{3,2,1,0:T(8,128)(2,1)} %enc_w_ref.1, f32[1,256]{1,0:T(1,128)} %bitcast.48, ...), custom_call_target="tpu_custom_call" | custom-call | flops 13690208256 | bytes 9437184 | tf_op jit(solution)/shard_map/pallas_call | solution.py:95
  46.9 255.9 %shard_map.114 = bf16[128,128,256]{2,1,0:T(8,128)(2,1)} custom-call(s32[128]{0:T(128)} %reshape.148.chosen_ref, bf16[96,128,256]{2,1,0:T(8,128)(2,1)} %bitcast.30), custom_call_target="tpu_custom_call" | custom-call | tf_op jit(solution)/shard_map/pallas_call | solution.py:175
  302.8 0.0 copy-start.2
  302.8 0.0 copy-start.1
  302.8 107.9 %all_to_all.10 = bf16[64,2,128,256]{3,2,1,0:T(8,128)(2,1)} all-to-all(bf16[64,2,128,256]{3,2,1,0:T(8,128)(2,1)} %bitcast.41), channel_id=1, replica_groups=mesh['tile'=64,'sec'=2] {'tile'}, dimensions={0} | all-to-all | bytes 16777216 | tf_op jit(solution)/shard_map/all_to_all | solution.py:231
  410.7 3.8 collective-permute-start.3
  414.4 0.1 copy.16
  414.5 0.1 reshape.154
  414.7 1.3 gather_fusion
  416.0 5.1 %all-to-all-start = ((bf16[64,2,128]{2,1,0:T(2,128)(2,1)}), bf16[64,2,128]{2,1,0:T(2,128)(2,1)S(1)}, u32[]{:S(2)}, u32[]{:S(2)}) async-start(bf16[64,2,128]{2,1,0:T(2,128)(2,1)} %bitcast.15), calls=%async_computation | async-start | bytes 65536 | tf_op jit(solution)/shard_map/all_to_all | solution.py:228
  421.2 0.1 reshape.146
  421.3 0.2 convert_reduce_fusion
  421.4 8.0 %all-to-all-done = bf16[64,2,128]{2,1,0:T(2,128)(2,1)S(1)} async-done(((bf16[64,2,128]{2,1,0:T(2,128)(2,1)}), bf16[64,2,128]{2,1,0:T(2,128)(2,1)S(1)}, u32[]{:S(2)}, u32[]{:S(2)}) %all-to-all-start) | async-done | bytes 32800 | tf_op jit(solution)/shard_map/all_to_all | solution.py:228
  429.5 1.4 collective-permute-start.2
  430.9 0.9 collective-permute-done.2
  431.8 2.8 copy-done
  434.6 13.6 %shard_map.115 = f32[64,128]{1,0:T(8,128)} custom-call(s32[64]{0:T(128)S(1)} %bitcast.40, s32[64]{0:T(128)S(1)} %multiply_add_fusion.slot_ref, f32[96,128]{1,0:T(8,128)S(1)} %convert_element_type.36.anchor_fold_ref, f32[128,128]{1,0:T(8,128)S(1)} %convert.1.partner_fold_ref, bf16[96,128,256]{2,1,0:T(8,128)(2,1)S(1)} %bitcast.32, ...), custom_call_target="tpu_custom_call" | custom-call | tf_op jit(solution)/shard_map/pallas_call | solution.py:145
  (21 shorter events, 0.1 us)
Async XLA Ops:
  1.7 9.6 %collective-permute-start = (bf16[2,384,128]{2,1,0:T(8,128)(2,1)S(1)}, bf16[2,384,128]{2,1,0:T(8,128)(2,1)S(1)}, u32[]{:S(2)}, u32[]{:S(2)}) collective-permute-start(bf16[2,384,128]{2,1,0:T(8,128)(2,1)S(1)} %get-tuple-element.9), channel_id=1, source_target_pairs={{0,2},{2,4},{4,6},{6,8},{8,10},{10,12},{12,14},{14,16},{16,18},{18... | collective-permute-start | bytes 589832 | tf_op jit(solution)/shard_map/ppermute | solution.py:195
  6.1 7.7 %collective-permute-start.1 = (bf16[2,384,128]{2,1,0:T(8,128)(2,1)S(1)}, bf16[2,384,128]{2,1,0:T(8,128)(2,1)S(1)}, u32[]{:S(2)}, u32[]{:S(2)}) collective-permute-start(bf16[2,384,128]{2,1,0:T(8,128)(2,1)S(1)} %get-tuple-element.8), channel_id=1, source_target_pairs={{2,0},{4,2},{6,4},{8,6},{10,8},{12,10},{14,12},{16,14},{18,16},{20... | collective-permute-start | bytes 589832 | tf_op jit(solution)/shard_map/ppermute | solution.py:196
  11.2 3.8 copy-start.3
  13.8 1.2 copy-start.4
  302.8 111.9 %copy-start.2 = (s32[1,32,384]{2,1,0:T(8,128)S(1)}, s32[1,32,384]{2,1,0:T(8,128)}, u32[]{:S(2)}) copy-start(s32[1,32,384]{2,1,0:T(8,128)} %param.11) | copy-start | bytes 147460
  302.8 129.0 %copy-start.1 = (s32[1,64]{1,0:T(1,128)S(1)}, s32[1,64]{1,0:T(1,128)}, u32[]{:S(2)}) copy-start(s32[1,64]{1,0:T(1,128)} %param.18) | copy-start | bytes 772
  410.7 21.1 %collective-permute-start.3 = (bf16[64,2,128,256]{3,2,1,0:T(8,128)(2,1)}, bf16[64,2,128,256]{3,2,1,0:T(8,128)(2,1)}, u32[]{:S(2)}, u32[]{:S(2)}) collective-permute-start(bf16[64,2,128,256]{3,2,1,0:T(8,128)(2,1)} %all_to_all.10), channel_id=1, source_target_pairs={{0,1},{1,0},{2,3},{3,2},{4,5},{5,4},{6,7},{7,6},{8,9},{9,8},{10,11... | collective-permute-start | bytes 25165832 | tf_op jit(solution)/shard_map/ppermute | solution.py:230
  416.0 13.4 %all-to-all-start = ((bf16[64,2,128]{2,1,0:T(2,128)(2,1)}), bf16[64,2,128]{2,1,0:T(2,128)(2,1)S(1)}, u32[]{:S(2)}, u32[]{:S(2)}) async-start(bf16[64,2,128]{2,1,0:T(2,128)(2,1)} %bitcast.15), calls=%async_computation | async-start | bytes 65536 | tf_op jit(solution)/shard_map/all_to_all | solution.py:228
  429.5 2.3 collective-permute-start.2
  431.8 2.8 copy-start

commit v2 on v1

v2 whole, which is shorter than its diff:
```python
import functools

import jax
import jax.numpy as jnp
from jax import lax
from jax.experimental import pallas as pl
from jax.experimental.pallas import tpu as pltpu
from jax.sharding import PartitionSpec as P

BLOCK = 128
SCORE_SCALE = 10.0
FOLD_PENALTY = 200.0
ROWS_STEP = 4
PAIRS_STEP = 8


def side_copies(rows):
    cols = rows.shape[1]
    flat = rows.reshape(rows.shape[0] * cols, rows.shape[2])
    column = lax.broadcasted_iota(jnp.int32, rows.shape, 1).reshape(flat.shape)
    before = jnp.where(column == 0, 0.0, pltpu.roll(flat, 1, 0))
    after = jnp.where(column == cols - 1, 0.0, pltpu.roll(flat, flat.shape[0] - 1, 0))
    return [v.reshape(rows.shape).astype(jnp.bfloat16) for v in (before, flat, after)]


def describe_kernel(
    chosen_ref, source_ref, low_ref, own_ref, high_ref, enc_w_ref, enc_b_ref, head_w_ref,
    head_b_ref, final_w_ref, final_b_ref, out_ref, send_ref, anchor_ref, wide_ref, enc_ref,
    pair_w_ref, all_ref, out_sem, send_sem, anchor_sem,
):
    step = pl.program_id(0)
    last = pl.num_programs(0) - 1
    chan = own_ref.shape[2]
    tile_here = lax.axis_index("tile")
    top = jnp.where(tile_here == 0, 0, -1)
    bottom = jnp.where(tile_here == lax.axis_size("tile") - 1, enc_ref.shape[0] - 1, -1)
    enc_b = jnp.concatenate([enc_b_ref[...]] * 2, axis=-1)

    def put_features(first, rows):
        for b, copy in enumerate(side_copies(rows.astype(jnp.float32))):
            wide_ref[pl.ds(first, 2), :, b * chan : (b + 1) * chan] = copy

    def encode(first):
        window = jnp.concatenate([wide_ref[first + a] for a in range(4)], axis=-1)
        both = jnp.dot(window, pair_w_ref[...], preferred_element_type=jnp.float32)
        both = jnp.maximum(both + enc_b, 0.0)
        keep = [jnp.logical_not((first + d == top) | (first + d == bottom)) for d in range(2)]
        rows = jnp.stack(
            [jnp.where(keep[d], both[:, d * chan : (d + 1) * chan], 0.0) for d in range(2)]
        )
        for b, copy in enumerate(side_copies(rows)):
            enc_ref[pl.ds(first, 2), :, b * chan : (b + 1) * chan] = copy

    @pl.when(step == 0)
    def _():
        for p in range(4):
            for b in range(3):
                k = pl.ds((p * 3 + b) * chan, chan)
                zero = jnp.zeros((chan, chan), jnp.bfloat16)
                pair_w_ref[k, 0:chan] = enc_w_ref[p, b] if p < 3 else zero
                pair_w_ref[k, chan : 2 * chan] = enc_w_ref[p - 1, b] if p > 0 else zero
        put_features(0, low_ref[...])
        put_features(2, own_ref[pl.ds(0, 2)])
        encode(0)

    base = step * ROWS_STEP
    put_features(base + 4, own_ref[pl.ds(base + 2, 2)])

    @pl.when(step < last)
    def _():
        put_features(base + 6, own_ref[pl.ds(base + 4, 2)])

    @pl.when(step == last)
    def _():
        put_features(base + 6, high_ref[...])

    encode(base + 2)
    encode(base + 4)
    cols = own_ref.shape[1]
    row_blocks = cols // BLOCK
    for r in range(0, ROWS_STEP, 2):
        parts = [enc_ref[pl.ds(base + r + a, 2)] for a in range(3)]
        window = jnp.concatenate([v.reshape(2 * cols, 3 * chan) for v in parts], axis=-1)
        hidden = jnp.dot(window, head_w_ref[...], preferred_element_type=jnp.float32)
        hidden = jnp.maximum(hidden + head_b_ref[...], 0.0).astype(jnp.bfloat16)
        raw = jnp.dot(hidden, final_w_ref[...], preferred_element_type=jnp.float32)
        raw = raw + final_b_ref[...]
        norm = jnp.sum(raw * raw, axis=-1, keepdims=True)
        unit = (raw * lax.rsqrt(norm + 1e-06)).astype(jnp.bfloat16)
        all_ref[pl.ds((base + r) * row_blocks, 2 * row_blocks)] = unit.reshape(
            2 * row_blocks, BLOCK, unit.shape[1]
        )
    done = pl.ds(base * row_blocks, ROWS_STEP * row_blocks)
    pltpu.make_async_copy(all_ref.at[done], out_ref.at[done], out_sem).start()

    @pl.when(step == last)
    def _():
        def send(n):
            return pltpu.make_async_copy(all_ref.at[chosen_ref[n]], send_ref.at[n], send_sem)

        def anchor(n):
            return pltpu.make_async_copy(all_ref.at[source_ref[n]], anchor_ref.at[n], anchor_sem)

        @pl.loop(0, send_ref.shape[0])
        def _(n):
            pl.when(chosen_ref[n] >= 0)(lambda: send(n).start())

        pl.loop(0, anchor_ref.shape[0])(lambda n: anchor(n).start())

        @pl.loop(0, send_ref.shape[0])
        def _(n):
            pl.when(chosen_ref[n] >= 0)(lambda: send(n).wait())

        pltpu.make_async_copy(anchor_ref, anchor_ref, anchor_sem).wait()
        pltpu.make_async_copy(all_ref, out_ref, out_sem).wait()


def describe(
    chosen, source, low, own, high, enc_w, enc_b, head_w, head_b, final_w, final_b
):
    rows, cols, chan = own.shape
    desc = final_w.shape[1]
    count = rows * cols // BLOCK
    whole = pl.BlockSpec(memory_space=pltpu.VMEM)
    scalars = pl.BlockSpec(memory_space=pltpu.SMEM)
    macs = rows * cols * (12 * chan * chan + 9 * chan * desc + desc * desc)

    def blocks(n):
        return jax.ShapeDtypeStruct((n, BLOCK, desc), jnp.bfloat16)

    return pl.pallas_call(
        describe_kernel,
        grid=(rows // ROWS_STEP,),
        in_specs=[scalars] * 2 + [whole] * 9,
        out_specs=[pl.BlockSpec(memory_space=pl.ANY)] * 3,
        out_shape=[blocks(count), blocks(chosen.shape[0]), blocks(source.shape[0])],
        scratch_shapes=[
            pltpu.VMEM((rows + 4, cols, 3 * chan), jnp.bfloat16),
            pltpu.VMEM((rows + 2, cols, 3 * chan), jnp.bfloat16),
            pltpu.VMEM((12 * chan, 2 * chan), jnp.bfloat16),
            pltpu.VMEM((count, BLOCK, desc), jnp.bfloat16),
            pltpu.SemaphoreType.DMA,
            pltpu.SemaphoreType.DMA,
            pltpu.SemaphoreType.DMA,
        ],
        compiler_params=pltpu.CompilerParams(vmem_limit_bytes=56 * 2**20),
        cost_estimate=pl.CostEstimate(
            flops=2 * macs, bytes_accessed=rows * cols * (chan + desc) * 2, transcendentals=rows * cols
        ),
    )(
        chosen, source, low, own, high, enc_w, enc_b[None], head_w.reshape(-1, desc),
        head_b[None], final_w, final_b[None],
    )


def match_kernel(slot_ref, anchor_fold_ref, partner_fold_ref, anchor_ref, *refs):
    partners, out_ref = refs[:PAIRS_STEP], refs[-1]
    anchor_fold, partner_fold = anchor_fold_ref[...], partner_fold_ref[...]
    anchor_column, partner_column = jnp.transpose(anchor_fold), jnp.transpose(partner_fold)

    def scores(left, right, left_fold, right_fold):
        products = lax.dot_general(
            left, right, (((1,), (1,)), ((), ())), preferred_element_type=jnp.float32
        )
        return SCORE_SCALE * products - FOLD_PENALTY * (left_fold + right_fold)

    over_i = []
    for n in range(PAIRS_STEP):
        by_i = scores(
            anchor_ref[n], partners[n][0], anchor_column[:, n : n + 1], partner_fold[n : n + 1]
        )
        peak = jnp.max(by_i, axis=0, keepdims=True)
        over_i.append(peak + jnp.log(jnp.sum(jnp.exp(by_i - peak), axis=0, keepdims=True)))
    over_i = jnp.transpose(jnp.concatenate(over_i))
    for n in range(PAIRS_STEP):
        by_j = scores(
            partners[n][0], anchor_ref[n], partner_column[:, n : n + 1], anchor_fold[n : n + 1]
        )
        peak = jnp.max(by_j, axis=0, keepdims=True)
        total = jnp.sum(jnp.exp(by_j - peak), axis=0, keepdims=True)
        best = jnp.max(2.0 * by_j - over_i[:, n : n + 1], axis=0, keepdims=True)
        out_ref[n : n + 1, :] = jnp.exp(best - peak) / total


def match(slot, anchor_folds, partner_folds, anchors, arrived):
    pairs = slot.shape[0]
    shape = (1,) + arrived.shape[1:]
    folds = pl.BlockSpec((PAIRS_STEP, BLOCK), lambda i, s: (i, 0))

    def partner(n):
        return pl.BlockSpec(shape, lambda i, s: (s[i * PAIRS_STEP + n], 0, 0))

    return pl.pallas_call(
        match_kernel,
        grid_spec=pltpu.PrefetchScalarGridSpec(
            num_scalar_prefetch=1,
            grid=(pairs // PAIRS_STEP,),
            in_specs=[folds, folds]
            + [pl.BlockSpec((PAIRS_STEP,) + arrived.shape[1:], lambda i, s: (i, 0, 0))]
            + [partner(n) for n in range(PAIRS_STEP)],
            out_specs=folds,
        ),
        out_shape=jax.ShapeDtypeStruct((pairs, BLOCK), jnp.float32),
        compiler_params=pltpu.CompilerParams(vmem_limit_bytes=32 * 2**20),
    )(slot, anchor_folds, partner_folds, anchors, *([arrived] * PAIRS_STEP))


def local(
    features, fold_mask, encoder_weight, encoder_bias, head_weight, head_bias,
    final_weight, final_bias, pair_source, pair_target,
):
    own_band = features[0]
    band_rows, band_cols, _ = own_band.shape
    desc = final_weight.shape[1]
    tile_count = lax.axis_size("tile")
    tile_here = lax.axis_index("tile")
    section = lax.axis_index("sec")
    swap = [(0, 1), (1, 0)]
    down = [(i, i + 1) for i in range(tile_count - 1)]
    up = [(j, i) for i, j in down]
    low = lax.ppermute(own_band[-2:], "tile", down)
    high = lax.ppermute(own_band[:2], "tile", up)

    block_count = band_rows * band_cols // BLOCK
    pair_count = pair_source.shape[1]
    capacity = max(2, 2 * pair_count // tile_count)
    wanted = lax.dynamic_index_in_dim(pair_target, 1 - section, 0, keepdims=False).reshape(
        tile_count, pair_count
    )
    matched = (wanted // block_count == tile_here).astype(jnp.int32)
    order_rank = jnp.cumsum(matched, axis=1) - matched
    slot_hot = matched[:, :, None] * (
        order_rank[:, :, None] == jnp.arange(capacity)[None, None, :]
    ).astype(jnp.int32)
    chosen = jnp.sum(slot_hot * (wanted % block_count + 1)[:, :, None], axis=1) - 1
    targets = lax.dynamic_index_in_dim(wanted, tile_here, 0, keepdims=False)
    owners = targets // block_count
    earlier = jnp.arange(pair_count)[None, :] < jnp.arange(pair_count)[:, None]
    slot_rank = jnp.sum(((owners[None, :] == owners[:, None]) & earlier).astype(jnp.int32), axis=1)
    slot_index = owners * capacity + slot_rank

    own_folds = fold_mask[0].reshape(block_count, BLOCK).astype(jnp.bfloat16)
    all_folds = lax.all_gather(own_folds, "tile", tiled=True)
    anchor_folds = lax.ppermute(own_folds[pair_source[0]], "sec", swap)

    described, send_blocks, anchors = describe(
        chosen.reshape(-1), pair_source[0], low, own_band, high, encoder_weight, encoder_bias,
        head_weight, head_bias, final_weight, final_bias,
    )
    sibling_anchors = lax.ppermute(anchors, "sec", swap)
    arrived = lax.all_to_all(
        send_blocks.reshape(tile_count, capacity, BLOCK, desc),
        "tile", split_axis=0, concat_axis=0, tiled=True,
    ).reshape(tile_count * capacity, BLOCK, desc)
    confidence = match(
        slot_index,
        anchor_folds.astype(jnp.float32),
        all_folds[targets].astype(jnp.float32),
        sibling_anchors,
        arrived,
    )
    confidence = lax.ppermute(confidence, "sec", swap)
    return (described.reshape(1, band_rows, band_cols, desc), confidence[None])


def solution(mesh):
    return jax.shard_map(
        local,
        mesh=mesh,
        in_specs=(
            P("sec", "tile", None, None), P("sec", "tile", None), P(), P(), P(), P(), P(), P(),
            P("sec", "tile"), P(),
        ),
        out_specs=(P("sec", "tile", None, None), P("sec", "tile", None)),
        check_vma=False,
    )
```

time: 449 us -> 235 us (0.52)
  Pallas kernels: 301 us -> 44.8 us
  waiting for transfers between devices: 11.4 us -> 143 us
  blocking collectives: 108 us -> 0 us
  between operations: 0.79 us -> 14.2 us
  starting transfers between devices: 16 us -> 23.6 us
    pallas_call x2 -> x1, Pallas kernels: 288 us -> 34.5 us  [describe(): pl.pallas_call(describe_kernel, grid=(rows // ROWS_STEP,), in_specs=[scal...]
    all_gather x0 -> x1, waiting for transfers between devices: none -> 133 us  [local(): all_folds = lax.all_gather(own_folds, 'tile', tiled=True)]
    all_to_all x1 -> x0, blocking collectives: 108 us -> none  [local(): lax.all_to_all(send_blocks, 'tile', split_axis=0, concat_axis=0, tiled=True)]
    all_to_all x1, starting transfers between devices: 5.11 us -> 13.6 us  [local(): lax.all_to_all(send_blocks.reshape(tile_count, capacity, BLOCK, desc), 't...]
    all_to_all x1, waiting for transfers between devices: 8.05 us -> 0.01 us  [local(): lax.all_to_all(send_blocks.reshape(tile_count, capacity, BLOCK, desc), 't...]
  transfers between devices with their start and end apart: 5 -> 7, of which waited for: 3 -> 5; matrix products, arithmetic and copies ran while one was open for 1% -> 2% of each run, Pallas kernels for 0% -> 0%
where the time goes in v2:
time: 235 us; the launch traced here: 234 us
  waiting for transfers between devices  143 us (61%)
  Pallas kernels  44.8 us (19%)
  starting transfers between devices  23.6 us (10%)
  between operations  14.2 us (6%)
  local copies, waits for them, and re-layouts  7.43 us (3%)
    all_gather x1, waiting for transfers between devices, local(): all_folds = lax.all_gather(own_folds, 'tile', tiled=True)  133 us
    pallas_call x1, Pallas kernels, describe(): pl.pallas_call(describe_kernel, grid=(rows // ROWS_STEP,), in_specs=[scal...  34.5 us
    all_to_all x1, starting transfers between devices, local(): lax.all_to_all(send_blocks.reshape(tile_count, capacity, BLOCK, desc), 't...  13.6 us
    pallas_call x1, Pallas kernels, match(): pl.pallas_call(match_kernel, grid_spec=pltpu.PrefetchScalarGridSpec(num_s...  10.3 us
  transfers between devices with their start and end apart: 7, of which 5 were waited for; matrix products, arithmetic and copies ran while one was open for 2% of the time, Pallas kernels for 0%

profile of v2, /device:TPU:1, one launch (start us, length us, event | category | flops | bytes accessed | tf_op | source)
XLA Modules:
  0.0 233.9 jit_solution(13284398854093761836)
XLA Ops:
  7.2 0.0 copy-start
  7.2 1.1 slice_bitcast_fusion
  8.2 4.4 %collective-permute-start = (bf16[2,384,128]{2,1,0:T(8,128)(2,1)S(1)}, bf16[2,384,128]{2,1,0:T(8,128)(2,1)S(1)}, u32[]{:S(2)}, u32[]{:S(2)}) collective-permute-start(bf16[2,384,128]{2,1,0:T(8,128)(2,1)S(1)} %get-tuple-element.12), channel_id=1, source_target_pairs={{0,2},{2,4},{4,6},{6,8},{8,10},{10,12},{12,14},{14,16},{16,18},{18... | collective-permute-start | bytes 589832 | tf_op jit(solution)/shard_map/ppermute | solution.py:221
  12.6 1.3 collective-permute-start.1
  13.9 0.1 dynamic-slice_reduce_fusion
  14.0 0.1 reshape.172
  14.1 0.2 reduce_window_sum.11
  14.4 0.1 multiply_reduce_fusion
  14.5 0.1 copy.12
  14.6 0.7 sub.34.chosen_ref
  15.3 0.9 collective-permute-done.low_ref
  16.2 4.2 %collective-permute-done.1.high_ref = bf16[2,384,128]{2,1,0:T(8,128)(2,1)S(1)} collective-permute-done((bf16[2,384,128]{2,1,0:T(8,128)(2,1)S(1)}, bf16[2,384,128]{2,1,0:T(8,128)(2,1)S(1)}, u32[]{:S(2)}, u32[]{:S(2)}) %collective-permute-start.1) | collective-permute-done | bytes 196640 | tf_op jit(solution)/shard_map/ppermute | solution.py:222
  20.4 0.7 copy-done.3
  21.0 34.5 %shard_map.113 = (bf16[96,128,256]{2,1,0:T(8,128)(2,1)}, bf16[128,128,256]{2,1,0:T(8,128)(2,1)}, bf16[64,128,256]{2,1,0:T(8,128)(2,1)}) custom-call(s32[128]{0:T(128)} %sub.34.chosen_ref, s32[64]{0:T(128)} %bitcast.35, bf16[2,384,128]{2,1,0:T(8,128)(2,1)} %copy-done.2, bf16[32,384,128]{2,1,0:T(8,128)(2,1)} %bitcast.29, bf16[2,384,128]{2,1,0:T(8,128)(2,1)} %copy-done.3, ...), custom_call_target="tpu_custom_call" | custom-call | flops 13690208256 | bytes 9437184 | tf_op jit(solution)/shard_map/pallas_call | solution.py:131
  55.5 0.0 copy-start.1
  55.5 0.0 copy-start.4
  55.5 13.6 %all-to-all-start = ((bf16[64,2,128,256]{3,2,1,0:T(8,128)(2,1)}), bf16[64,2,128,256]{3,2,1,0:T(8,128)(2,1)}, u32[]{:S(2)}, u32[]{:S(2)}) async-start(bf16[64,2,128,256]{3,2,1,0:T(8,128)(2,1)} %bitcast.28), calls=%async_computation | async-start | bytes 16777216 | tf_op jit(solution)/shard_map/all_to_all | solution.py:251
  69.1 0.0 all-gather.2.cloned.1.call-start
  69.2 1.9 collective-permute-start.3
  71.1 0.6 convert_element_type.33
  71.7 0.0 all-gather.2.cloned.1.call-update
  71.8 1.3 gather_fusion
  73.1 0.1 collective-permute-start.2
  73.3 0.2 convert_reduce_fusion
  73.5 4.4 %collective-permute-done.2 = bf16[64,128]{1,0:T(8,128)(2,1)S(1)} collective-permute-done((bf16[64,128]{1,0:T(8,128)(2,1)S(1)}, bf16[64,128]{1,0:T(8,128)(2,1)S(1)}, u32[]{:S(2)}, u32[]{:S(2)}) %collective-permute-start.2) | collective-permute-done | bytes 16416 | tf_op jit(solution)/shard_map/ppermute | solution.py:244
  77.9 132.8 %all-gather.2.cloned.1.call-done = bf16[6144,128]{1,0:T(8,128)(2,1)} async-done(((bf16[96,128]{1,0:T(8,128)(2,1)}), bf16[6144,128]{1,0:T(8,128)(2,1)}) %all-gather.2.cloned.1.call-update) | async-done | bytes 1572880 | tf_op jit(solution)/shard_map/all_gather | solution.py:243
  210.7 2.2 gather_fusion.1
  212.9 0.0 all-to-all-done
  213.0 10.3 %shard_map.114 = f32[64,128]{1,0:T(8,128)S(1)} custom-call(s32[64]{0:T(128)S(1)} %multiply_add_fusion.slot_ref, f32[64,128]{1,0:T(8,128)S(1)} %convert_element_type.34.anchor_fold_ref, f32[64,128]{1,0:T(8,128)S(1)} %convert_element_type.35.partner_fold_ref, bf16[64,128,256]{2,1,0:T(8,128)(2,1)} %collective-permute-done.3.anchor_ref, ...), custom_call_target="tpu_custom_call" | custom-call | tf_op jit(solution)/shard_map/pallas_call | solution.py:193
  223.3 2.2 collective-permute-start.4
  225.5 0.9 collective-permute-done.4
  226.4 0.6 copy.14
  (21 shorter events, 0.2 us)
Async XLA Ops:
  7.2 6.8 %copy-start = (s32[2,4096]{1,0:T(2,128)S(1)}, s32[2,4096]{1,0:T(2,128)}, u32[]{:S(2)}) copy-start(s32[2,4096]{1,0:T(2,128)} %param.19) | copy-start | bytes 98308
  8.2 7.9 %collective-permute-start = (bf16[2,384,128]{2,1,0:T(8,128)(2,1)S(1)}, bf16[2,384,128]{2,1,0:T(8,128)(2,1)S(1)}, u32[]{:S(2)}, u32[]{:S(2)}) collective-permute-start(bf16[2,384,128]{2,1,0:T(8,128)(2,1)S(1)} %get-tuple-element.12), channel_id=1, source_target_pairs={{0,2},{2,4},{4,6},{6,8},{8,10},{10,12},{12,14},{14,16},{16,18},{18... | collective-permute-start | bytes 589832 | tf_op jit(solution)/shard_map/ppermute | solution.py:221
  12.6 7.7 %collective-permute-start.1 = (bf16[2,384,128]{2,1,0:T(8,128)(2,1)S(1)}, bf16[2,384,128]{2,1,0:T(8,128)(2,1)S(1)}, u32[]{:S(2)}, u32[]{:S(2)}) collective-permute-start(bf16[2,384,128]{2,1,0:T(8,128)(2,1)S(1)} %get-tuple-element.11), channel_id=1, source_target_pairs={{2,0},{4,2},{6,4},{8,6},{10,8},{12,10},{14,12},{16,14},{18,16},{20... | collective-permute-start | bytes 589832 | tf_op jit(solution)/shard_map/ppermute | solution.py:222
  16.2 4.2 %copy-start.2 = (bf16[2,384,128]{2,1,0:T(8,128)(2,1)}, bf16[2,384,128]{2,1,0:T(8,128)(2,1)S(1)}, u32[]{:S(2)}) copy-start(bf16[2,384,128]{2,1,0:T(8,128)(2,1)S(1)} %collective-permute-done.low_ref) | copy-start | bytes 589828
  20.3 0.7 copy-start.3
  55.5 15.6 %copy-start.1 = (s32[1,32,384]{2,1,0:T(8,128)S(1)}, s32[1,32,384]{2,1,0:T(8,128)}, u32[]{:S(2)}) copy-start(s32[1,32,384]{2,1,0:T(8,128)} %param.11) | copy-start | bytes 147460
  55.5 16.2 %copy-start.4 = (s32[1,64]{1,0:T(1,128)S(1)}, s32[1,64]{1,0:T(1,128)}, u32[]{:S(2)}) copy-start(s32[1,64]{1,0:T(1,128)} %param.18) | copy-start | bytes 772
  55.5 157.4 %all-to-all-start = ((bf16[64,2,128,256]{3,2,1,0:T(8,128)(2,1)}), bf16[64,2,128,256]{3,2,1,0:T(8,128)(2,1)}, u32[]{:S(2)}, u32[]{:S(2)}) async-start(bf16[64,2,128,256]{3,2,1,0:T(8,128)(2,1)} %bitcast.28), calls=%async_computation | async-start | bytes 16777216 | tf_op jit(solution)/shard_map/all_to_all | solution.py:251
  69.1 141.6 %all-gather.2.cloned.1.call-start = ((), (), s32[]{:S(2)}) async-start(), calls=%async_computation.1 | async-start | bytes 1597440 | tf_op jit(solution)/shard_map/all_gather | solution.py:243
  69.2 143.8 %collective-permute-start.3 = (bf16[64,128,256]{2,1,0:T(8,128)(2,1)}, bf16[64,128,256]{2,1,0:T(8,128)(2,1)}, u32[]{:S(2)}, u32[]{:S(2)}) collective-permute-start(bf16[64,128,256]{2,1,0:T(8,128)(2,1)} %get-tuple-element.6), channel_id=1, source_target_pairs={{0,1},{1,0},{2,3},{3,2},{4,5},{5,4},{6,7},{7,6},{8,9},{9,8},{10,11... | collective-permute-start | bytes 12582920 | tf_op jit(solution)/shard_map/ppermute | solution.py:250
  73.1 4.8 %collective-permute-start.2 = (bf16[64,128]{1,0:T(8,128)(2,1)S(1)}, bf16[64,128]{1,0:T(8,128)(2,1)S(1)}, u32[]{:S(2)}, u32[]{:S(2)}) collective-permute-start(bf16[64,128]{1,0:T(8,128)(2,1)S(1)} %gather_fusion), channel_id=1, source_target_pairs={{0,1},{1,0},{2,3},{3,2},{4,5},{5,4},{6,7},{7,6},{8,9},{9,8},{10,11... | collective-permute-start | bytes 49160 | tf_op jit(solution)/shard_map/ppermute | solution.py:244
  223.3 3.1 %collective-permute-start.4 = (f32[64,128]{1,0:T(8,128)S(1)}, f32[64,128]{1,0:T(8,128)S(1)}, u32[]{:S(2)}, u32[]{:S(2)}) collective-permute-start(f32[64,128]{1,0:T(8,128)S(1)} %shard_map.114), channel_id=1, source_target_pairs={{0,1},{1,0},{2,3},{3,2},{4,5},{5,4},{6,7},{7,6},{8,9},{9,8},{10,11... | collective-permute-start | bytes 98312 | tf_op jit(solution)/shard_map/ppermute | solution.py:262
Sparse Core Ops, SparseCore 0:
  73.4 137.3 all-gather.1

commit v3 on v2

--- a/solution.py
+++ b/solution.py
@@ -10,7 +10,9 @@
 BLOCK = 128
 SCORE_SCALE = 10.0
 FOLD_PENALTY = 200.0
-ROWS_STEP = 4
+ROWS_STEP = 8
+ENC_PAIRS = 1
+DOT_ROWS = 8
 PAIRS_STEP = 8
 
 
@@ -38,18 +40,25 @@
 
     def put_features(first, rows):
         for b, copy in enumerate(side_copies(rows.astype(jnp.float32))):
-            wide_ref[pl.ds(first, 2), :, b * chan : (b + 1) * chan] = copy
-
-    def encode(first):
-        window = jnp.concatenate([wide_ref[first + a] for a in range(4)], axis=-1)
+            wide_ref[pl.ds(first, rows.shape[0]), :, b * chan : (b + 1) * chan] = copy
+
+    def encode(first, pairs):
+        window = jnp.concatenate(
+            [
+                jnp.concatenate([wide_ref[first + 2 * k + a] for a in range(4)], axis=-1)
+                for k in range(pairs)
+            ]
+        )
         both = jnp.dot(window, pair_w_ref[...], preferred_element_type=jnp.float32)
         both = jnp.maximum(both + enc_b, 0.0)
-        keep = [jnp.logical_not((first + d == top) | (first + d == bottom)) for d in range(2)]
-        rows = jnp.stack(
-            [jnp.where(keep[d], both[:, d * chan : (d + 1) * chan], 0.0) for d in range(2)]
-        )
-        for b, copy in enumerate(side_copies(rows)):
-            enc_ref[pl.ds(first, 2), :, b * chan : (b + 1) * chan] = copy
+        cols = own_ref.shape[1]
+        rows = []
+        for d in range(2 * pairs):
+            row = both[d // 2 * cols : (d // 2 + 1) * cols, d % 2 * chan : (d % 2 + 1) * chan]
+            keep = jnp.logical_not((first + d == top) | (first + d == bottom))
+            rows.append(jnp.where(keep, row, 0.0))
+        for b, copy in enumerate(side_copies(jnp.stack(rows))):
+            enc_ref[pl.ds(first, 2 * pairs), :, b * chan : (b + 1) * chan] = copy
 
     @pl.when(step == 0)
     def _():
@@ -61,34 +70,34 @@
                 pair_w_ref[k, chan : 2 * chan] = enc_w_ref[p - 1, b] if p > 0 else zero
         put_features(0, low_ref[...])
         put_features(2, own_ref[pl.ds(0, 2)])
-        encode(0)
+        encode(0, 1)
 
     base = step * ROWS_STEP
-    put_features(base + 4, own_ref[pl.ds(base + 2, 2)])
+    put_features(base + 4, own_ref[pl.ds(base + 2, ROWS_STEP - 2)])
 
     @pl.when(step < last)
     def _():
-        put_features(base + 6, own_ref[pl.ds(base + 4, 2)])
+        put_features(base + ROWS_STEP + 2, own_ref[pl.ds(base + ROWS_STEP, 2)])
 
     @pl.when(step == last)
     def _():
-        put_features(base + 6, high_ref[...])
-
-    encode(base + 2)
-    encode(base + 4)
+        put_features(base + ROWS_STEP + 2, high_ref[...])
+
+    for d in range(0, ROWS_STEP, 2 * ENC_PAIRS):
+        encode(base + 2 + d, ENC_PAIRS)
     cols = own_ref.shape[1]
     row_blocks = cols // BLOCK
-    for r in range(0, ROWS_STEP, 2):
-        parts = [enc_ref[pl.ds(base + r + a, 2)] for a in range(3)]
-        window = jnp.concatenate([v.reshape(2 * cols, 3 * chan) for v in parts], axis=-1)
+    for r in range(0, ROWS_STEP, DOT_ROWS):
+        parts = [enc_ref[pl.ds(base + r + a, DOT_ROWS)] for a in range(3)]
+        window = jnp.concatenate([v.reshape(DOT_ROWS * cols, 3 * chan) for v in parts], axis=-1)
         hidden = jnp.dot(window, head_w_ref[...], preferred_element_type=jnp.float32)
         hidden = jnp.maximum(hidden + head_b_ref[...], 0.0).astype(jnp.bfloat16)
         raw = jnp.dot(hidden, final_w_ref[...], preferred_element_type=jnp.float32)
         raw = raw + final_b_ref[...]
         norm = jnp.sum(raw * raw, axis=-1, keepdims=True)
         unit = (raw * lax.rsqrt(norm + 1e-06)).astype(jnp.bfloat16)
-        all_ref[pl.ds((base + r) * row_blocks, 2 * row_blocks)] = unit.reshape(
-            2 * row_blocks, BLOCK, unit.shape[1]
+        all_ref[pl.ds((base + r) * row_blocks, DOT_ROWS * row_blocks)] = unit.reshape(
+            DOT_ROWS * row_blocks, BLOCK, unit.shape[1]
         )
     done = pl.ds(base * row_blocks, ROWS_STEP * row_blocks)
     pltpu.make_async_copy(all_ref.at[done], out_ref.at[done], out_sem).start()
@@ -247,6 +256,7 @@
         chosen.reshape(-1), pair_source[0], low, own_band, high, encoder_weight, encoder_bias,
         head_weight, head_bias, final_weight, final_bias,
     )
+    send_blocks, all_folds = lax.optimization_barrier((send_blocks, all_folds))
     sibling_anchors = lax.ppermute(anchors, "sec", swap)
     arrived = lax.all_to_all(
         send_blocks.reshape(tile_count, capacity, BLOCK, desc),

time: 235 us -> 225 us (0.957)
  Pallas kernels: 44.8 us -> 36.7 us
  starting transfers between devices: 23.6 us -> 18.3 us
  waiting for transfers between devices: 143 us -> 146 us
    all_to_all x1, waiting for transfers between devices: 0.01 us -> 106 us  [local(): lax.all_to_all(send_blocks.reshape(tile_count, capacity, BLOCK, desc), 't...]
    all_gather x1, waiting for transfers between devices: 133 us -> 31.3 us  [local(): all_folds = lax.all_gather(own_folds, 'tile', tiled=True)]
    pallas_call x1, Pallas kernels: 34.5 us -> 26.4 us  [describe(): pl.pallas_call(describe_kernel, grid=(rows // ROWS_STEP,), in_specs=[scal...]
    all_to_all x1, starting transfers between devices: 13.6 us -> 6.82 us  [local(): lax.all_to_all(send_blocks.reshape(tile_count, capacity, BLOCK, desc), 't...]
    ppermute x1, waiting for transfers between devices: 4.18 us -> 1.25 us  [local(): high = lax.ppermute(own_band[:2], 'tile', up)]
  transfers between devices with their start and end apart: 7 -> 7, of which waited for: 5 -> 6; matrix products, arithmetic and copies ran while one was open for 2% -> 2% of each run, Pallas kernels for 0% -> 12%
where the time goes in v3:
time: 225 us; the launch traced here: 224 us
  waiting for transfers between devices  146 us (65%)
  Pallas kernels  36.7 us (16%)
  starting transfers between devices  18.3 us (8%)
  between operations  14.2 us (6%)
  local copies, waits for them, and re-layouts  6.76 us (3%)
    all_to_all x1, waiting for transfers between devices, local(): lax.all_to_all(send_blocks.reshape(tile_count, capacity, BLOCK, desc), 't...  106 us
    all_gather x1, waiting for transfers between devices, local(): all_folds = lax.all_gather(own_folds, 'tile', tiled=True)  31.3 us
    pallas_call x1, Pallas kernels, describe(): pl.pallas_call(describe_kernel, grid=(rows // ROWS_STEP,), in_specs=[scal...  26.4 us
    pallas_call x1, Pallas kernels, match(): pl.pallas_call(match_kernel, grid_spec=pltpu.PrefetchScalarGridSpec(num_s...  10.3 us
    all_to_all x1, starting transfers between devices, local(): lax.all_to_all(send_blocks.reshape(tile_count, capacity, BLOCK, desc), 't...  6.82 us
    ppermute x1, waiting for transfers between devices, local(): anchor_folds = lax.ppermute(own_folds[pair_source[0]], 'sec', swap)  5.8 us
    ppermute x1, starting transfers between devices, local(): low = lax.ppermute(own_band[-2:], 'tile', down)  5.01 us
  transfers between devices with their start and end apart: 7, of which 6 were waited for; matrix products, arithmetic and copies ran while one was open for 2% of the time, Pallas kernels for 12%

profile of v3, /device:TPU:1, one launch (start us, length us, event | category | flops | bytes accessed | tf_op | source)
XLA Modules:
  0.0 223.7 jit_solution(9587717229408158142)
XLA Ops:
  7.2 0.0 copy-start
  7.2 0.0 all-gather.2.cloned.1.call-start
  7.2 0.8 convert_element_type.32
  8.0 0.6 convert_element_type.33
  8.7 0.0 all-gather.2.cloned.1.call-update
  8.7 1.1 slice_bitcast_fusion
  9.7 1.3 collective-permute-start.1
  11.0 5.0 %collective-permute-start = (bf16[2,384,128]{2,1,0:T(8,128)(2,1)S(1)}, bf16[2,384,128]{2,1,0:T(8,128)(2,1)S(1)}, u32[]{:S(2)}, u32[]{:S(2)}) collective-permute-start(bf16[2,384,128]{2,1,0:T(8,128)(2,1)S(1)} %get-tuple-element.16), channel_id=1, source_target_pairs={{0,2},{2,4},{4,6},{6,8},{8,10},{10,12},{12,14},{14,16},{16,18},{18... | collective-permute-start | bytes 589832 | tf_op jit(solution)/shard_map/ppermute | solution.py:230
  16.1 0.1 dynamic-slice_reduce_fusion
  16.1 0.1 reshape.172
  16.2 0.2 reduce_window_sum.11
  16.5 0.1 multiply_reduce_fusion
  16.7 0.1 copy.12
  16.8 0.7 sub.34.chosen_ref
  17.5 1.3 collective-permute-done.1.high_ref
  18.7 0.9 collective-permute-done.low_ref
  19.6 0.7 copy-done.3
  20.3 26.4 %shard_map.113 = (bf16[96,128,256]{2,1,0:T(8,128)(2,1)}, bf16[128,128,256]{2,1,0:T(8,128)(2,1)}, bf16[64,128,256]{2,1,0:T(8,128)(2,1)}) custom-call(s32[128]{0:T(128)} %sub.34.chosen_ref, s32[64]{0:T(128)} %bitcast.35, bf16[2,384,128]{2,1,0:T(8,128)(2,1)} %copy-done.3, bf16[32,384,128]{2,1,0:T(8,128)(2,1)} %bitcast.29, bf16[2,384,128]{2,1,0:T(8,128)(2,1)} %copy-done.2, ...), custom_call_target="tpu_custom_call" | custom-call | flops 13690208256 | bytes 9437184 | tf_op jit(solution)/shard_map/pallas_call | solution.py:140
  46.6 31.3 %all-gather.2.cloned.1.call-done = bf16[6144,128]{1,0:T(8,128)(2,1)} async-done(((bf16[96,128]{1,0:T(8,128)(2,1)}), bf16[6144,128]{1,0:T(8,128)(2,1)}) %all-gather.2.cloned.1.call-update) | async-done | bytes 1572880 | tf_op jit(solution)/shard_map/all_gather | solution.py:252
  77.9 6.8 %all-to-all-start = ((bf16[64,2,128,256]{3,2,1,0:T(8,128)(2,1)}), bf16[64,2,128,256]{3,2,1,0:T(8,128)(2,1)}, u32[]{:S(2)}, u32[]{:S(2)}) async-start(bf16[64,2,128,256]{3,2,1,0:T(8,128)(2,1)} %bitcast.28), calls=%async_computation | async-start | bytes 16777216 | tf_op jit(solution)/shard_map/all_to_all | solution.py:261
  84.7 2.2 collective-permute-start.3
  87.0 0.6 gather_fusion
  87.6 0.1 collective-permute-start.2
  87.7 0.2 convert_reduce_fusion
  87.9 5.8 %collective-permute-done.2 = bf16[64,128]{1,0:T(8,128)(2,1)S(1)} collective-permute-done((bf16[64,128]{1,0:T(8,128)(2,1)S(1)}, bf16[64,128]{1,0:T(8,128)(2,1)S(1)}, u32[]{:S(2)}, u32[]{:S(2)}) %collective-permute-start.2) | collective-permute-done | bytes 16416 | tf_op jit(solution)/shard_map/ppermute | solution.py:253
  93.7 2.2 gather_fusion.1
  96.0 0.0 collective-permute-done.3.anchor_ref
  96.0 106.2 %all-to-all-done = bf16[64,2,128,256]{3,2,1,0:T(8,128)(2,1)} async-done(((bf16[64,2,128,256]{3,2,1,0:T(8,128)(2,1)}), bf16[64,2,128,256]{3,2,1,0:T(8,128)(2,1)}, u32[]{:S(2)}, u32[]{:S(2)}) %all-to-all-start) | async-done | bytes 8388640 | tf_op jit(solution)/shard_map/all_to_all | solution.py:261
  202.2 10.3 %shard_map.114 = f32[64,128]{1,0:T(8,128)S(1)} custom-call(s32[64]{0:T(128)S(1)} %multiply_add_fusion.slot_ref, f32[64,128]{1,0:T(8,128)S(1)} %convert_element_type.34.anchor_fold_ref, f32[64,128]{1,0:T(8,128)S(1)} %convert_element_type.35.partner_fold_ref, bf16[64,128,256]{2,1,0:T(8,128)(2,1)} %collective-permute-done.3.anchor_ref, ...), custom_call_target="tpu_custom_call" | custom-call | tf_op jit(solution)/shard_map/pallas_call | solution.py:202
  212.5 2.8 %collective-permute-start.4 = (f32[64,128]{1,0:T(8,128)S(1)}, f32[64,128]{1,0:T(8,128)S(1)}, u32[]{:S(2)}, u32[]{:S(2)}) collective-permute-start(f32[64,128]{1,0:T(8,128)S(1)} %shard_map.114), channel_id=1, source_target_pairs={{0,1},{1,0},{2,3},{3,2},{4,5},{5,4},{6,7},{7,6},{8,9},{9,8},{10,11... | collective-permute-start | bytes 98312 | tf_op jit(solution)/shard_map/ppermute | solution.py:272
  215.4 0.9 collective-permute-done.4
  216.2 0.6 copy.14
  (21 shorter events, 0.2 us)
Async XLA Ops:
  7.2 8.9 %copy-start = (s32[2,4096]{1,0:T(2,128)S(1)}, s32[2,4096]{1,0:T(2,128)}, u32[]{:S(2)}) copy-start(s32[2,4096]{1,0:T(2,128)} %param.19) | copy-start | bytes 98308
  7.2 70.7 %all-gather.2.cloned.1.call-start = ((), (), s32[]{:S(2)}) async-start(), calls=%async_computation.1 | async-start | bytes 1597440 | tf_op jit(solution)/shard_map/all_gather | solution.py:252
  9.7 9.0 %collective-permute-start.1 = (bf16[2,384,128]{2,1,0:T(8,128)(2,1)S(1)}, bf16[2,384,128]{2,1,0:T(8,128)(2,1)S(1)}, u32[]{:S(2)}, u32[]{:S(2)}) collective-permute-start(bf16[2,384,128]{2,1,0:T(8,128)(2,1)S(1)} %get-tuple-element.15), channel_id=1, source_target_pairs={{2,0},{4,2},{6,4},{8,6},{10,8},{12,10},{14,12},{16,14},{18,16},{20... | collective-permute-start | bytes 589832 | tf_op jit(solution)/shard_map/ppermute | solution.py:231
  11.0 8.5 %collective-permute-start = (bf16[2,384,128]{2,1,0:T(8,128)(2,1)S(1)}, bf16[2,384,128]{2,1,0:T(8,128)(2,1)S(1)}, u32[]{:S(2)}, u32[]{:S(2)}) collective-permute-start(bf16[2,384,128]{2,1,0:T(8,128)(2,1)S(1)} %get-tuple-element.16), channel_id=1, source_target_pairs={{0,2},{2,4},{4,6},{6,8},{8,10},{10,12},{12,14},{14,16},{16,18},{18... | collective-permute-start | bytes 589832 | tf_op jit(solution)/shard_map/ppermute | solution.py:230
  18.7 0.9 copy-start.2
  19.6 0.7 copy-start.3
  77.9 9.0 %copy-start.4 = (s32[1,64]{1,0:T(1,128)S(1)}, s32[1,64]{1,0:T(1,128)}, u32[]{:S(2)}) copy-start(s32[1,64]{1,0:T(1,128)} %param.18) | copy-start | bytes 772
  77.9 9.0 %copy-start.1 = (bf16[96,128]{1,0:T(8,128)(2,1)S(1)}, bf16[96,128]{1,0:T(8,128)(2,1)}, u32[]{:S(2)}) copy-start(bf16[96,128]{1,0:T(8,128)(2,1)} %convert_element_type.33) | copy-start | bytes 73732
  77.9 124.3 %all-to-all-start = ((bf16[64,2,128,256]{3,2,1,0:T(8,128)(2,1)}), bf16[64,2,128,256]{3,2,1,0:T(8,128)(2,1)}, u32[]{:S(2)}, u32[]{:S(2)}) async-start(bf16[64,2,128,256]{3,2,1,0:T(8,128)(2,1)} %bitcast.28), calls=%async_computation | async-start | bytes 16777216 | tf_op jit(solution)/shard_map/all_to_all | solution.py:261
  84.7 11.2 %collective-permute-start.3 = (bf16[64,128,256]{2,1,0:T(8,128)(2,1)}, bf16[64,128,256]{2,1,0:T(8,128)(2,1)}, u32[]{:S(2)}, u32[]{:S(2)}) collective-permute-start(bf16[64,128,256]{2,1,0:T(8,128)(2,1)} %get-tuple-element.10), channel_id=1, source_target_pairs={{0,1},{1,0},{2,3},{3,2},{4,5},{5,4},{6,7},{7,6},{8,9},{9,8},{10,11... | collective-permute-start | bytes 12582920 | tf_op jit(solution)/shard_map/ppermute | solution.py:260
  87.6 6.1 %collective-permute-start.2 = (bf16[64,128]{1,0:T(8,128)(2,1)S(1)}, bf16[64,128]{1,0:T(8,128)(2,1)S(1)}, u32[]{:S(2)}, u32[]{:S(2)}) collective-permute-start(bf16[64,128]{1,0:T(8,128)(2,1)S(1)} %gather_fusion), channel_id=1, source_target_pairs={{0,1},{1,0},{2,3},{3,2},{4,5},{5,4},{6,7},{7,6},{8,9},{9,8},{10,11... | collective-permute-start | bytes 49160 | tf_op jit(solution)/shard_map/ppermute | solution.py:253
  212.5 3.7 %collective-permute-start.4 = (f32[64,128]{1,0:T(8,128)S(1)}, f32[64,128]{1,0:T(8,128)S(1)}, u32[]{:S(2)}, u32[]{:S(2)}) collective-permute-start(f32[64,128]{1,0:T(8,128)S(1)} %shard_map.114), channel_id=1, source_target_pairs={{0,1},{1,0},{2,3},{3,2},{4,5},{5,4},{6,7},{7,6},{8,9},{9,8},{10,11... | collective-permute-start | bytes 98312 | tf_op jit(solution)/shard_map/ppermute | solution.py:272
Sparse Core Ops, SparseCore 0:
  11.4 66.4 all-gather.1

commit v4 on v3

--- a/solution.py
+++ b/solution.py
@@ -13,7 +13,8 @@
 ROWS_STEP = 8
 ENC_PAIRS = 1
 DOT_ROWS = 8
-PAIRS_STEP = 8
+PAIRS_STEP = 16
+VMEM_MATCH = 56 * 2**20
 
 
 def side_copies(rows):
@@ -162,56 +163,75 @@
     )
 
 
-def match_kernel(slot_ref, anchor_fold_ref, partner_fold_ref, anchor_ref, *refs):
-    partners, out_ref = refs[:PAIRS_STEP], refs[-1]
-    anchor_fold, partner_fold = anchor_fold_ref[...], partner_fold_ref[...]
-    anchor_column, partner_column = jnp.transpose(anchor_fold), jnp.transpose(partner_fold)
-
-    def scores(left, right, left_fold, right_fold):
-        products = lax.dot_general(
+def match_kernel(
+    slot_ref, anchor_fold_ref, partner_fold_ref, anchors_ref, arrived_ref, out_ref, anchor_ref,
+    partner_ref, anchor_sem, partner_sem,
+):
+    groups = out_ref.shape[0] // PAIRS_STEP
+
+    def products(left, right):
+        return SCORE_SCALE * lax.dot_general(
             left, right, (((1,), (1,)), ((), ())), preferred_element_type=jnp.float32
         )
-        return SCORE_SCALE * products - FOLD_PENALTY * (left_fold + right_fold)
-
-    over_i = []
-    for n in range(PAIRS_STEP):
-        by_i = scores(
-            anchor_ref[n], partners[n][0], anchor_column[:, n : n + 1], partner_fold[n : n + 1]
+
+    def group(g):
+        return pl.ds(g * PAIRS_STEP, PAIRS_STEP)
+
+    def anchors(g):
+        return pltpu.make_async_copy(
+            anchors_ref.at[group(g)], anchor_ref.at[group(g)], anchor_sem.at[g]
         )
-        peak = jnp.max(by_i, axis=0, keepdims=True)
-        over_i.append(peak + jnp.log(jnp.sum(jnp.exp(by_i - peak), axis=0, keepdims=True)))
-    over_i = jnp.transpose(jnp.concatenate(over_i))
-    for n in range(PAIRS_STEP):
-        by_j = scores(
-            partners[n][0], anchor_ref[n], partner_column[:, n : n + 1], anchor_fold[n : n + 1]
-        )
-        peak = jnp.max(by_j, axis=0, keepdims=True)
-        total = jnp.sum(jnp.exp(by_j - peak), axis=0, keepdims=True)
-        best = jnp.max(2.0 * by_j - over_i[:, n : n + 1], axis=0, keepdims=True)
-        out_ref[n : n + 1, :] = jnp.exp(best - peak) / total
+
+    @pl.loop(0, groups)
+    def _(g):
+        anchors(g).start()
+        for n in range(PAIRS_STEP):
+            pair = g * PAIRS_STEP + n
+            pltpu.make_async_copy(
+                arrived_ref.at[slot_ref[pair]], partner_ref.at[pair], partner_sem.at[g]
+            ).start()
+
+    @pl.loop(0, groups)
+    def _(g):
+        anchor_cost = FOLD_PENALTY * anchor_fold_ref[group(g)]
+        anchor_column = jnp.transpose(anchor_cost)
+        partner_column = jnp.transpose(FOLD_PENALTY * partner_fold_ref[group(g)])
+        anchors(g).wait()
+        here = partner_ref.at[group(g)]
+        pltpu.make_async_copy(here, here, partner_sem.at[g]).wait()
+        left = [anchor_ref[g * PAIRS_STEP + n] for n in range(PAIRS_STEP)]
+        right = [partner_ref[g * PAIRS_STEP + n] for n in range(PAIRS_STEP)]
+
+        over_i = []
+        for n in range(PAIRS_STEP):
+            by_i = products(left[n], right[n]) - anchor_column[:, n : n + 1]
+            peak = jnp.max(by_i, axis=0, keepdims=True)
+            over_i.append(peak + jnp.log(jnp.sum(jnp.exp(by_i - peak), axis=0, keepdims=True)))
+        over_i = jnp.transpose(jnp.concatenate(over_i))
+        result = []
+        for n in range(PAIRS_STEP):
+            plain = products(right[n], left[n])
+            by_j = plain - partner_column[:, n : n + 1]
+            peak = jnp.max(by_j, axis=0, keepdims=True)
+            total = jnp.sum(jnp.exp(by_j - peak), axis=0, keepdims=True)
+            best = jnp.max(by_j + (plain - over_i[:, n : n + 1]), axis=0, keepdims=True)
+            result.append(jnp.exp(best - peak - anchor_cost[n : n + 1]) / total)
+        out_ref[group(g)] = jnp.concatenate(result)
 
 
 def match(slot, anchor_folds, partner_folds, anchors, arrived):
     pairs = slot.shape[0]
-    shape = (1,) + arrived.shape[1:]
-    folds = pl.BlockSpec((PAIRS_STEP, BLOCK), lambda i, s: (i, 0))
-
-    def partner(n):
-        return pl.BlockSpec(shape, lambda i, s: (s[i * PAIRS_STEP + n], 0, 0))
-
+    whole = pl.BlockSpec(memory_space=pltpu.VMEM)
     return pl.pallas_call(
         match_kernel,
-        grid_spec=pltpu.PrefetchScalarGridSpec(
-            num_scalar_prefetch=1,
-            grid=(pairs // PAIRS_STEP,),
-            in_specs=[folds, folds]
-            + [pl.BlockSpec((PAIRS_STEP,) + arrived.shape[1:], lambda i, s: (i, 0, 0))]
-            + [partner(n) for n in range(PAIRS_STEP)],
-            out_specs=folds,
-        ),
+        in_specs=[pl.BlockSpec(memory_space=pltpu.SMEM), whole, whole]
+        + [pl.BlockSpec(memory_space=pl.ANY)] * 2,
+        out_specs=whole,
         out_shape=jax.ShapeDtypeStruct((pairs, BLOCK), jnp.float32),
-        compiler_params=pltpu.CompilerParams(vmem_limit_bytes=32 * 2**20),
-    )(slot, anchor_folds, partner_folds, anchors, *([arrived] * PAIRS_STEP))
+        scratch_shapes=[pltpu.VMEM(anchors.shape, jnp.bfloat16)] * 2
+        + [pltpu.SemaphoreType.DMA((pairs // PAIRS_STEP,))] * 2,
+        compiler_params=pltpu.CompilerParams(vmem_limit_bytes=VMEM_MATCH),
+    )(slot, anchor_folds, partner_folds, anchors, arrived)
 
 
 def local(
@@ -249,23 +269,29 @@
     slot_index = owners * capacity + slot_rank
 
     own_folds = fold_mask[0].reshape(block_count, BLOCK).astype(jnp.bfloat16)
-    all_folds = lax.all_gather(own_folds, "tile", tiled=True)
-    anchor_folds = lax.ppermute(own_folds[pair_source[0]], "sec", swap)
+    send_folds = own_folds[jnp.maximum(chosen, 0)]
+    anchor_folds = own_folds[pair_source[0]]
 
     described, send_blocks, anchors = describe(
         chosen.reshape(-1), pair_source[0], low, own_band, high, encoder_weight, encoder_bias,
         head_weight, head_bias, final_weight, final_bias,
     )
-    send_blocks, all_folds = lax.optimization_barrier((send_blocks, all_folds))
-    sibling_anchors = lax.ppermute(anchors, "sec", swap)
     arrived = lax.all_to_all(
         send_blocks.reshape(tile_count, capacity, BLOCK, desc),
         "tile", split_axis=0, concat_axis=0, tiled=True,
     ).reshape(tile_count * capacity, BLOCK, desc)
+    sibling_anchors = lax.ppermute(anchors, "sec", swap)
+    send_folds, anchor_folds, sibling_anchors = lax.optimization_barrier(
+        (send_folds, anchor_folds, sibling_anchors)
+    )
+    anchor_folds = lax.ppermute(anchor_folds, "sec", swap)
+    partner_folds = lax.all_to_all(
+        send_folds, "tile", split_axis=0, concat_axis=0, tiled=True
+    ).reshape(tile_count * capacity, BLOCK)[slot_index]
     confidence = match(
         slot_index,
         anchor_folds.astype(jnp.float32),
-        all_folds[targets].astype(jnp.float32),
+        partner_folds.astype(jnp.float32),
         sibling_anchors,
         arrived,
     )

time: 225 us -> 205 us (0.911)
  waiting for transfers between devices: 146 us -> 119 us
  blocking collectives: 0 us -> 24 us
  between operations: 14.2 us -> 0.79 us
    all_gather x1 -> x0, waiting for transfers between devices: 31.3 us -> none  [local(): all_folds = lax.all_gather(own_folds, 'tile', tiled=True)]
    all_to_all x0 -> x1, blocking collectives: none -> 24 us  [local(): lax.all_to_all(send_folds, 'tile', split_axis=0, concat_axis=0, tiled=True)]
    ppermute x1, waiting for transfers between devices: 0.01 us -> 5.46 us  [local(): sibling_anchors = lax.ppermute(anchors, 'sec', swap)]
    ppermute x1, waiting for transfers between devices: 5.8 us -> 0.83 us  [local(): anchor_folds = lax.ppermute(anchor_folds, 'sec', swap)]
    all_to_all x1, waiting for transfers between devices: 106 us -> 109 us  [local(): lax.all_to_all(send_blocks.reshape(tile_count, capacity, BLOCK, desc), 't...]
  transfers between devices with their start and end apart: 7 -> 6, of which waited for: 6 -> 6; matrix products, arithmetic and copies ran while one was open for 2% -> 3% of each run, Pallas kernels for 12% -> 0%
where the time goes in v4:
time: 205 us
  waiting for transfers between devices  119 us (58%)
  Pallas kernels  34.9 us (17%)
  blocking collectives  24 us (12%)
  starting transfers between devices  18.3 us (9%)
  local copies, waits for them, and re-layouts  5.47 us (3%)
  other arithmetic  2.46 us (1%)
    all_to_all x1, waiting for transfers between devices, local(): lax.all_to_all(send_blocks.reshape(tile_count, capacity, BLOCK, desc), 't...  109 us
    pallas_call x1, Pallas kernels, describe(): pl.pallas_call(describe_kernel, grid=(rows // ROWS_STEP,), in_specs=[scal...  26.4 us
    all_to_all x1, blocking collectives, local(): lax.all_to_all(send_folds, 'tile', split_axis=0, concat_axis=0, tiled=True)  24 us
    pallas_call x1, Pallas kernels, match(): pl.pallas_call(match_kernel, in_specs=[pl.BlockSpec(memory_space=pltpu.SM...  8.54 us
    all_to_all x1, starting transfers between devices, local(): lax.all_to_all(send_blocks.reshape(tile_count, capacity, BLOCK, desc), 't...  5.76 us
    ppermute x1, waiting for transfers between devices, local(): sibling_anchors = lax.ppermute(anchors, 'sec', swap)  5.46 us
    ppermute x1, starting transfers between devices, local(): low = lax.ppermute(own_band[-2:], 'tile', down)  5.01 us
  transfers between devices with their start and end apart: 6, of which 6 were waited for; matrix products, arithmetic and copies ran while one was open for 3% of the time, Pallas kernels for 0%

profile of v4, /device:TPU:1, one launch (start us, length us, event | category | flops | bytes accessed | tf_op | source)
XLA Modules:
  0.0 204.6 jit_solution(13697055960340984476)
XLA Ops:
  0.6 1.1 slice_bitcast_fusion
  1.7 1.3 collective-permute-start.1
  3.0 5.0 %collective-permute-start = (bf16[2,384,128]{2,1,0:T(8,128)(2,1)S(1)}, bf16[2,384,128]{2,1,0:T(8,128)(2,1)S(1)}, u32[]{:S(2)}, u32[]{:S(2)}) collective-permute-start(bf16[2,384,128]{2,1,0:T(8,128)(2,1)S(1)} %get-tuple-element.18), channel_id=1, source_target_pairs={{0,2},{2,4},{4,6},{6,8},{8,10},{10,12},{12,14},{14,16},{16,18},{18... | collective-permute-start | bytes 589832 | tf_op jit(solution)/shard_map/ppermute | solution.py:250
  8.1 0.1 reshape.222
  8.2 0.2 reduce_window_sum.11
  8.5 0.1 multiply_reduce_fusion
  8.6 0.1 copy.12
  8.7 0.7 sub.36.chosen_ref
  9.4 1.3 collective-permute-done.1.high_ref
  10.7 0.9 collective-permute-done.low_ref
  11.6 0.7 copy-done.3
  12.2 26.4 %shard_map.113 = (bf16[96,128,256]{2,1,0:T(8,128)(2,1)}, bf16[128,128,256]{2,1,0:T(8,128)(2,1)}, bf16[64,128,256]{2,1,0:T(8,128)(2,1)}) custom-call(s32[128]{0:T(128)} %sub.36.chosen_ref, s32[64]{0:T(128)} %bitcast.53, bf16[2,384,128]{2,1,0:T(8,128)(2,1)} %copy-done.3, bf16[32,384,128]{2,1,0:T(8,128)(2,1)} %bitcast.47, bf16[2,384,128]{2,1,0:T(8,128)(2,1)} %copy-done.2, ...), custom_call_target="tpu_custom_call" | custom-call | flops 13690208256 | bytes 9437184 | tf_op jit(solution)/shard_map/pallas_call | solution.py:141
  38.6 1.9 collective-permute-start.2
  40.6 0.1 copy.13
  40.7 0.1 reshape.230
  40.8 0.6 gather_fusion.1
  41.5 0.7 gather_fusion
  42.2 5.5 %collective-permute-done.2.anchors_ref = bf16[64,128,256]{2,1,0:T(8,128)(2,1)} collective-permute-done((bf16[64,128,256]{2,1,0:T(8,128)(2,1)}, bf16[64,128,256]{2,1,0:T(8,128)(2,1)}, u32[]{:S(2)}, u32[]{:S(2)}) %collective-permute-start.2) | collective-permute-done | bytes 4194336 | tf_op jit(solution)/shard_map/ppermute | solution.py:283
  47.6 24.0 %all_to_all.10 = bf16[64,2,128]{2,1,0:T(2,128)(2,1)S(1)} all-to-all(bf16[64,2,128]{2,1,0:T(2,128)(2,1)S(1)} %bitcast.46), channel_id=1, replica_groups=mesh['tile'=64,'sec'=2] {'tile'}, dimensions={0} | all-to-all | bytes 65536 | tf_op jit(solution)/shard_map/all_to_all | solution.py:288
  71.6 5.8 %all-to-all-start.1 = ((bf16[64,2,128,256]{3,2,1,0:T(8,128)(2,1)}), bf16[64,2,128,256]{3,2,1,0:T(8,128)(2,1)}, u32[]{:S(2)}, u32[]{:S(2)}) async-start(bf16[64,2,128,256]{3,2,1,0:T(8,128)(2,1)} %bitcast.44), calls=%async_computation.1 | async-start | bytes 16777216 | tf_op jit(solution)/shard_map/all_to_all | solution.py:279
  77.4 0.2 convert_reduce_fusion
  77.6 0.6 multiply_add_fusion.slot_ref
  78.2 1.8 collective-permute-start.3
  80.0 0.8 collective-permute-done.3
  80.8 0.6 convert_element_type.34.anchor_fold_ref
  81.4 0.6 gather_fusion.2
  82.1 0.6 convert_element_type.35.partner_fold_ref
  82.7 109.1 %all-to-all-done.1 = bf16[64,2,128,256]{3,2,1,0:T(8,128)(2,1)} async-done(((bf16[64,2,128,256]{3,2,1,0:T(8,128)(2,1)}), bf16[64,2,128,256]{3,2,1,0:T(8,128)(2,1)}, u32[]{:S(2)}, u32[]{:S(2)}) %all-to-all-start.1) | async-done | bytes 8388640 | tf_op jit(solution)/shard_map/all_to_all | solution.py:279
  191.8 8.5 %shard_map.114 = f32[64,128]{1,0:T(8,128)} custom-call(s32[64]{0:T(128)} %multiply_add_fusion.slot_ref, f32[64,128]{1,0:T(8,128)} %convert_element_type.34.anchor_fold_ref, f32[64,128]{1,0:T(8,128)} %convert_element_type.35.partner_fold_ref, bf16[64,128,256]{2,1,0:T(8,128)(2,1)} %collective-permute-done.2.anchors_ref, bf16[128,128,256]{2,1,0:T(8,128)(2,1)} %bitcast.21.arrived_ref), custom_call_target="tpu_custom_call" | custom-call | tf_op jit(solution)/shard_map/pallas_call | solution.py:225
  200.4 2.5 %collective-permute-start.4 = (f32[64,128]{1,0:T(8,128)}, f32[64,128]{1,0:T(8,128)S(1)}, u32[]{:S(2)}, u32[]{:S(2)}) collective-permute-start(f32[64,128]{1,0:T(8,128)} %shard_map.114), channel_id=1, source_target_pairs={{0,1},{1,0},{2,3},{3,2},{4,5},{5,4},{6,7},{7,6},{8,9},{9,8},{10,11... | collective-permute-start | bytes 98312 | tf_op jit(solution)/shard_map/ppermute | solution.py:298
  202.9 1.1 collective-permute-done.4
  204.0 0.6 copy.15
  (23 shorter events, 0.3 us)
Async XLA Ops:
  0.6 7.4 %copy-start = (s32[2,4096]{1,0:T(2,128)S(1)}, s32[2,4096]{1,0:T(2,128)}, u32[]{:S(2)}) copy-start(s32[2,4096]{1,0:T(2,128)} %param.19) | copy-start | bytes 98308
  1.7 9.0 %collective-permute-start.1 = (bf16[2,384,128]{2,1,0:T(8,128)(2,1)S(1)}, bf16[2,384,128]{2,1,0:T(8,128)(2,1)S(1)}, u32[]{:S(2)}, u32[]{:S(2)}) collective-permute-start(bf16[2,384,128]{2,1,0:T(8,128)(2,1)S(1)} %get-tuple-element.17), channel_id=1, source_target_pairs={{2,0},{4,2},{6,4},{8,6},{10,8},{12,10},{14,12},{16,14},{18,16},{20... | collective-permute-start | bytes 589832 | tf_op jit(solution)/shard_map/ppermute | solution.py:251
  3.0 8.5 %collective-permute-start = (bf16[2,384,128]{2,1,0:T(8,128)(2,1)S(1)}, bf16[2,384,128]{2,1,0:T(8,128)(2,1)S(1)}, u32[]{:S(2)}, u32[]{:S(2)}) collective-permute-start(bf16[2,384,128]{2,1,0:T(8,128)(2,1)S(1)} %get-tuple-element.18), channel_id=1, source_target_pairs={{0,2},{2,4},{4,6},{6,8},{8,10},{10,12},{12,14},{14,16},{16,18},{18... | collective-permute-start | bytes 589832 | tf_op jit(solution)/shard_map/ppermute | solution.py:250
  10.7 0.9 copy-start.2
  11.5 0.7 copy-start.3
  12.2 28.3 %copy-start.1 = (s32[1,32,384]{2,1,0:T(8,128)S(1)}, s32[1,32,384]{2,1,0:T(8,128)}, u32[]{:S(2)}) copy-start(s32[1,32,384]{2,1,0:T(8,128)} %param.11) | copy-start | bytes 147460
  12.2 28.6 %copy-start.4 = (s32[1,64]{1,0:T(1,128)S(1)}, s32[1,64]{1,0:T(1,128)}, u32[]{:S(2)}) copy-start(s32[1,64]{1,0:T(1,128)} %param.18) | copy-start | bytes 772
  38.6 9.0 %collective-permute-start.2 = (bf16[64,128,256]{2,1,0:T(8,128)(2,1)}, bf16[64,128,256]{2,1,0:T(8,128)(2,1)}, u32[]{:S(2)}, u32[]{:S(2)}) collective-permute-start(bf16[64,128,256]{2,1,0:T(8,128)(2,1)} %get-tuple-element.9), channel_id=1, source_target_pairs={{0,1},{1,0},{2,3},{3,2},{4,5},{5,4},{6,7},{7,6},{8,9},{9,8},{10,11... | collective-permute-start | bytes 12582920 | tf_op jit(solution)/shard_map/ppermute | solution.py:283
  71.6 120.2 %all-to-all-start.1 = ((bf16[64,2,128,256]{3,2,1,0:T(8,128)(2,1)}), bf16[64,2,128,256]{3,2,1,0:T(8,128)(2,1)}, u32[]{:S(2)}, u32[]{:S(2)}) async-start(bf16[64,2,128,256]{3,2,1,0:T(8,128)(2,1)} %bitcast.44), calls=%async_computation.1 | async-start | bytes 16777216 | tf_op jit(solution)/shard_map/all_to_all | solution.py:279
  78.2 2.6 %collective-permute-start.3 = (bf16[64,128]{1,0:T(8,128)(2,1)S(1)}, bf16[64,128]{1,0:T(8,128)(2,1)S(1)}, u32[]{:S(2)}, u32[]{:S(2)}) collective-permute-start(bf16[64,128]{1,0:T(8,128)(2,1)S(1)} %gather_fusion.1), channel_id=1, source_target_pairs={{0,1},{1,0},{2,3},{3,2},{4,5},{5,4},{6,7},{7,6},{8,9},{9,8},{10,11... | collective-permute-start | bytes 49160 | tf_op jit(solution)/shard_map/ppermute | solution.py:287
  200.4 3.6 %collective-permute-start.4 = (f32[64,128]{1,0:T(8,128)}, f32[64,128]{1,0:T(8,128)S(1)}, u32[]{:S(2)}, u32[]{:S(2)}) collective-permute-start(f32[64,128]{1,0:T(8,128)} %shard_map.114), channel_id=1, source_target_pairs={{0,1},{1,0},{2,3},{3,2},{4,5},{5,4},{6,7},{7,6},{8,9},{9,8},{10,11... | collective-permute-start | bytes 98312 | tf_op jit(solution)/shard_map/ppermute | solution.py:298

commit v5 on v4

--- a/solution.py
+++ b/solution.py
@@ -269,32 +269,30 @@
     slot_index = owners * capacity + slot_rank
 
     own_folds = fold_mask[0].reshape(block_count, BLOCK).astype(jnp.bfloat16)
-    send_folds = own_folds[jnp.maximum(chosen, 0)]
-    anchor_folds = own_folds[pair_source[0]]
+    partner_folds = lax.all_to_all(
+        own_folds[jnp.maximum(chosen, 0)], "tile", split_axis=0, concat_axis=0, tiled=True
+    )
+    anchor_folds = lax.ppermute(own_folds[pair_source[0]], "sec", swap)
 
     described, send_blocks, anchors = describe(
         chosen.reshape(-1), pair_source[0], low, own_band, high, encoder_weight, encoder_bias,
         head_weight, head_bias, final_weight, final_bias,
+    )
+    anchors, partner_folds, anchor_folds = lax.optimization_barrier(
+        (anchors, partner_folds, anchor_folds)
+    )
+    sibling_anchors = lax.ppermute(anchors, "sec", swap)
+    partner_folds = partner_folds.reshape(tile_count * capacity, BLOCK)[slot_index]
+    partner_folds = partner_folds.astype(jnp.float32)
+    anchor_folds = anchor_folds.astype(jnp.float32)
+    send_blocks, sibling_anchors, slot_index, partner_folds, anchor_folds = lax.optimization_barrier(
+        (send_blocks, sibling_anchors, slot_index, partner_folds, anchor_folds)
     )
     arrived = lax.all_to_all(
         send_blocks.reshape(tile_count, capacity, BLOCK, desc),
         "tile", split_axis=0, concat_axis=0, tiled=True,
     ).reshape(tile_count * capacity, BLOCK, desc)
-    sibling_anchors = lax.ppermute(anchors, "sec", swap)
-    send_folds, anchor_folds, sibling_anchors = lax.optimization_barrier(
-        (send_folds, anchor_folds, sibling_anchors)
-    )
-    anchor_folds = lax.ppermute(anchor_folds, "sec", swap)
-    partner_folds = lax.all_to_all(
-        send_folds, "tile", split_axis=0, concat_axis=0, tiled=True
-    ).reshape(tile_count * capacity, BLOCK)[slot_index]
-    confidence = match(
-        slot_index,
-        anchor_folds.astype(jnp.float32),
-        partner_folds.astype(jnp.float32),
-        sibling_anchors,
-        arrived,
-    )
+    confidence = match(slot_index, anchor_folds, partner_folds, sibling_anchors, arrived)
     confidence = lax.ppermute(confidence, "sec", swap)
     return (described.reshape(1, band_rows, band_cols, desc), confidence[None])
 

time: 205 us -> 184 us (0.90)
  waiting for transfers between devices: 119 us -> 5.82 us
  blocking collectives: 24 us -> 106 us
  starting transfers between devices: 18.3 us -> 25.5 us
    all_to_all x1, waiting for transfers between devices: 109 us -> 0.01 us  [local(): lax.all_to_all(own_folds[jnp.maximum(chosen, 0)], 'tile', split_axis=0, c...]
    all_to_all x1, blocking collectives: 24 us -> 106 us  [local(): lax.all_to_all(send_blocks.reshape(tile_count, capacity, BLOCK, desc), 't...]
    all_to_all x1, starting transfers between devices: 5.76 us -> 14.9 us  [local(): lax.all_to_all(own_folds[jnp.maximum(chosen, 0)], 'tile', split_axis=0, c...]
  transfers between devices with their start and end apart: 6 -> 6, of which waited for: 6 -> 2; matrix products, arithmetic and copies ran while one was open for 3% -> 3% of each run, Pallas kernels for 0% -> 14%
where the time goes in v5:
time: 184 us
  blocking collectives  106 us (58%)
  Pallas kernels  35.3 us (19%)
  starting transfers between devices  25.5 us (14%)
  local copies, waits for them, and re-layouts  6.88 us (4%)
  waiting for transfers between devices  5.82 us (3%)
  other arithmetic  3.87 us (2%)
    all_to_all x1, blocking collectives, local(): lax.all_to_all(send_blocks.reshape(tile_count, capacity, BLOCK, desc), 't...  106 us
    pallas_call x1, Pallas kernels, describe(): pl.pallas_call(describe_kernel, grid=(rows // ROWS_STEP,), in_specs=[scal...  26.6 us
    all_to_all x1, starting transfers between devices, local(): lax.all_to_all(own_folds[jnp.maximum(chosen, 0)], 'tile', split_axis=0, c...  14.9 us
    pallas_call x1, Pallas kernels, match(): pl.pallas_call(match_kernel, in_specs=[pl.BlockSpec(memory_space=pltpu.SM...  8.77 us
    ppermute x1, waiting for transfers between devices, local(): sibling_anchors = lax.ppermute(anchors, 'sec', swap)  4.73 us
    ppermute x1, starting transfers between devices, local(): low = lax.ppermute(own_band[-2:], 'tile', down)  4.26 us
  transfers between devices with their start and end apart: 6, of which 2 were waited for; matrix products, arithmetic and copies ran while one was open for 3% of the time, Pallas kernels for 14%

profile of v5, /device:TPU:1, one launch (start us, length us, event | category | flops | bytes accessed | tf_op | source)
XLA Modules:
  0.0 184.0 jit_solution(5833015928463993386)
XLA Ops:
  0.7 0.7 copy-done
  1.4 0.1 reshape.222
  1.5 0.2 convert_reduce_fusion
  1.7 0.7 fusion.8
  2.4 0.8 convert_element_type.31
  3.2 0.6 gather_fusion.1
  3.9 1.5 collective-permute-start.2
  5.4 1.0 slice_bitcast_fusion
  6.4 1.3 collective-permute-start.1
  7.7 4.3 %collective-permute-start = (bf16[2,384,128]{2,1,0:T(8,128)(2,1)S(1)}, bf16[2,384,128]{2,1,0:T(8,128)(2,1)S(1)}, u32[]{:S(2)}, u32[]{:S(2)}) collective-permute-start(bf16[2,384,128]{2,1,0:T(8,128)(2,1)S(1)} %get-tuple-element.28), channel_id=1, source_target_pairs={{0,2},{2,4},{4,6},{6,8},{8,10},{10,12},{12,14},{14,16},{16,18},{18... | collective-permute-start | bytes 589832 | tf_op jit(solution)/shard_map/ppermute | solution.py:250
  12.1 0.2 reduce_window_sum.11
  12.3 0.1 multiply_reduce_fusion
  12.4 0.1 copy.13
  12.5 0.1 reshape.230
  12.7 1.3 gather_fusion
  14.0 14.9 %all-to-all-start = ((bf16[64,2,128]{2,1,0:T(2,128)(2,1)}), bf16[64,2,128]{2,1,0:T(2,128)(2,1)S(1)}, u32[]{:S(2)}, u32[]{:S(2)}) async-start(bf16[64,2,128]{2,1,0:T(2,128)(2,1)} %bitcast.9), calls=%async_computation | async-start | bytes 65536 | tf_op jit(solution)/shard_map/all_to_all | solution.py:272
  28.9 0.1 copy.12
  29.0 0.7 sub.36.chosen_ref
  29.7 0.7 copy-done.1
  30.4 0.1 copy-done.2
  30.4 26.6 %shard_map.113 = (bf16[96,128,256]{2,1,0:T(8,128)(2,1)}, bf16[128,128,256]{2,1,0:T(8,128)(2,1)}, bf16[64,128,256]{2,1,0:T(8,128)(2,1)}) custom-call(s32[128]{0:T(128)} %sub.36.chosen_ref, s32[64]{0:T(128)} %bitcast.49, bf16[2,384,128]{2,1,0:T(8,128)(2,1)} %copy-done.2, bf16[32,384,128]{2,1,0:T(8,128)(2,1)} %bitcast.47, bf16[2,384,128]{2,1,0:T(8,128)(2,1)} %copy-done.1, ...), custom_call_target="tpu_custom_call" | custom-call | flops 13690208256 | bytes 9437184 | tf_op jit(solution)/shard_map/pallas_call | solution.py:141
  57.0 1.1 collective-permute-start.3
  58.1 0.5 multiply_add_fusion.slot_ref
  58.7 0.6 gather_fusion.2
  59.3 0.6 convert_element_type.34.partner_fold_ref
  59.9 0.6 convert_element_type.35.anchor_fold_ref
  60.5 4.7 %collective-permute-done.3.anchors_ref = bf16[64,128,256]{2,1,0:T(8,128)(2,1)} collective-permute-done((bf16[64,128,256]{2,1,0:T(8,128)(2,1)}, bf16[64,128,256]{2,1,0:T(8,128)(2,1)}, u32[]{:S(2)}, u32[]{:S(2)}) %collective-permute-start.3) | collective-permute-done | bytes 4194336 | tf_op jit(solution)/shard_map/ppermute | solution.py:284
  65.3 105.9 %all_to_all.10 = bf16[64,2,128,256]{3,2,1,0:T(8,128)(2,1)} all-to-all(bf16[64,2,128,256]{3,2,1,0:T(8,128)(2,1)} %bitcast.45), channel_id=1, replica_groups=mesh['tile'=64,'sec'=2] {'tile'}, dimensions={0} | all-to-all | bytes 16777216 | tf_op jit(solution)/shard_map/all_to_all | solution.py:291
  171.1 8.8 %shard_map.114 = f32[64,128]{1,0:T(8,128)} custom-call(s32[64]{0:T(128)} %multiply_add_fusion.slot_ref, f32[64,128]{1,0:T(8,128)} %convert_element_type.35.anchor_fold_ref, f32[64,128]{1,0:T(8,128)} %convert_element_type.34.partner_fold_ref, bf16[64,128,256]{2,1,0:T(8,128)(2,1)} %collective-permute-done.3.anchors_ref, bf16[128,128,256]{2,1,0:T(8,128)(2,1)} %bitcast.44), custom_call_target="tpu_custom_call" | custom-call | tf_op jit(solution)/shard_map/pallas_call | solution.py:225
  179.9 2.4 %collective-permute-start.4 = (f32[64,128]{1,0:T(8,128)}, f32[64,128]{1,0:T(8,128)S(1)}, u32[]{:S(2)}, u32[]{:S(2)}) collective-permute-start(f32[64,128]{1,0:T(8,128)} %shard_map.114), channel_id=1, source_target_pairs={{0,1},{1,0},{2,3},{3,2},{4,5},{5,4},{6,7},{7,6},{8,9},{9,8},{10,11... | collective-permute-start | bytes 98312 | tf_op jit(solution)/shard_map/ppermute | solution.py:296
  182.3 1.1 collective-permute-done.4
  183.4 0.6 copy.15
  (18 shorter events, 0.2 us)
Async XLA Ops:
  0.6 0.8 copy-start
  3.9 53.2 %collective-permute-start.2 = (bf16[64,128]{1,0:T(8,128)(2,1)S(1)}, bf16[64,128]{1,0:T(8,128)(2,1)S(1)}, u32[]{:S(2)}, u32[]{:S(2)}) collective-permute-start(bf16[64,128]{1,0:T(8,128)(2,1)S(1)} %gather_fusion.1), channel_id=1, source_target_pairs={{0,1},{1,0},{2,3},{3,2},{4,5},{5,4},{6,7},{7,6},{8,9},{9,8},{10,11... | collective-permute-start | bytes 49160 | tf_op jit(solution)/shard_map/ppermute | solution.py:275
  6.4 23.3 %collective-permute-start.1 = (bf16[2,384,128]{2,1,0:T(8,128)(2,1)S(1)}, bf16[2,384,128]{2,1,0:T(8,128)(2,1)S(1)}, u32[]{:S(2)}, u32[]{:S(2)}) collective-permute-start(bf16[2,384,128]{2,1,0:T(8,128)(2,1)S(1)} %get-tuple-element.27), channel_id=1, source_target_pairs={{2,0},{4,2},{6,4},{8,6},{10,8},{12,10},{14,12},{16,14},{18,16},{20... | collective-permute-start | bytes 589832 | tf_op jit(solution)/shard_map/ppermute | solution.py:251
  7.7 22.0 %collective-permute-start = (bf16[2,384,128]{2,1,0:T(8,128)(2,1)S(1)}, bf16[2,384,128]{2,1,0:T(8,128)(2,1)S(1)}, u32[]{:S(2)}, u32[]{:S(2)}) collective-permute-start(bf16[2,384,128]{2,1,0:T(8,128)(2,1)S(1)} %get-tuple-element.28), channel_id=1, source_target_pairs={{0,2},{2,4},{4,6},{6,8},{8,10},{10,12},{12,14},{14,16},{16,18},{18... | collective-permute-start | bytes 589832 | tf_op jit(solution)/shard_map/ppermute | solution.py:250
  14.0 43.0 %all-to-all-start = ((bf16[64,2,128]{2,1,0:T(2,128)(2,1)}), bf16[64,2,128]{2,1,0:T(2,128)(2,1)S(1)}, u32[]{:S(2)}, u32[]{:S(2)}) async-start(bf16[64,2,128]{2,1,0:T(2,128)(2,1)} %bitcast.9), calls=%async_computation | async-start | bytes 65536 | tf_op jit(solution)/shard_map/all_to_all | solution.py:272
  29.7 0.7 copy-start.1
  29.7 0.8 copy-start.2
  57.0 8.2 %collective-permute-start.3 = (bf16[64,128,256]{2,1,0:T(8,128)(2,1)}, bf16[64,128,256]{2,1,0:T(8,128)(2,1)}, u32[]{:S(2)}, u32[]{:S(2)}) collective-permute-start(bf16[64,128,256]{2,1,0:T(8,128)(2,1)} %get-tuple-element.16), channel_id=1, source_target_pairs={{0,1},{1,0},{2,3},{3,2},{4,5},{5,4},{6,7},{7,6},{8,9},{9,8},{10,11... | collective-permute-start | bytes 12582920 | tf_op jit(solution)/shard_map/ppermute | solution.py:284
  179.9 3.5 %collective-permute-start.4 = (f32[64,128]{1,0:T(8,128)}, f32[64,128]{1,0:T(8,128)S(1)}, u32[]{:S(2)}, u32[]{:S(2)}) collective-permute-start(f32[64,128]{1,0:T(8,128)} %shard_map.114), channel_id=1, source_target_pairs={{0,1},{1,0},{2,3},{3,2},{4,5},{5,4},{6,7},{7,6},{8,9},{9,8},{10,11... | collective-permute-start | bytes 98312 | tf_op jit(solution)/shard_map/ppermute | solution.py:296

commit v6 on v5

--- a/solution.py
+++ b/solution.py
@@ -11,6 +11,7 @@
 SCORE_SCALE = 10.0
 FOLD_PENALTY = 200.0
 ROWS_STEP = 8
+FOLD_ROWS = 16
 ENC_PAIRS = 1
 DOT_ROWS = 8
 PAIRS_STEP = 16
@@ -27,9 +28,10 @@
 
 
 def describe_kernel(
-    chosen_ref, source_ref, low_ref, own_ref, high_ref, enc_w_ref, enc_b_ref, head_w_ref,
+    chosen_ref, source_ref, chosen_row_ref, source_row_ref, fold_ref, low_ref, own_ref, high_ref, enc_w_ref, enc_b_ref, head_w_ref,
     head_b_ref, final_w_ref, final_b_ref, out_ref, send_ref, anchor_ref, wide_ref, enc_ref,
-    pair_w_ref, all_ref, out_sem, send_sem, anchor_sem,
+    pair_w_ref, all_ref, send_fold_ref, anchor_fold_ref, out_sem, send_sem, anchor_sem,
+    fold_sem,
 ):
     step = pl.program_id(0)
     last = pl.num_programs(0) - 1
@@ -61,6 +63,58 @@
         for b, copy in enumerate(side_copies(jnp.stack(rows))):
             enc_ref[pl.ds(first, 2 * pairs), :, b * chan : (b + 1) * chan] = copy
 
+    cols = own_ref.shape[1]
+    row_blocks = cols // BLOCK
+    pairs = source_ref.shape[0]
+    peers = send_ref.shape[0]
+
+    def send(n):
+        place = send_ref.at[n % peers, pl.ds(pl.multiple_of(n // peers * BLOCK, BLOCK), BLOCK)]
+        return pltpu.make_async_copy(all_ref.at[chosen_ref[n]], place, send_sem)
+
+    def anchor(n):
+        return pltpu.make_async_copy(all_ref.at[source_ref[n]], anchor_ref.at[n], anchor_sem)
+
+    def ship(first, end):
+        @pl.loop(0, chosen_ref.shape[0], unroll=4)
+        def _(n):
+            pl.when((chosen_ref[n] >= first) & (chosen_ref[n] < end))(lambda: send(n).start())
+
+        @pl.loop(0, pairs, unroll=4)
+        def _(n):
+            pl.when((source_ref[n] >= first) & (source_ref[n] < end))(lambda: anchor(n).start())
+
+    def fold_copies():
+        return (
+            pltpu.make_async_copy(
+                send_fold_ref, send_ref.at[:, pl.ds(2 * BLOCK, FOLD_ROWS)], fold_sem.at[0]
+            ),
+            pltpu.make_async_copy(
+                anchor_fold_ref, anchor_ref.at[pairs, pl.ds(0, pairs), pl.ds(0, BLOCK)], fold_sem.at[1]
+            ),
+        )
+
+    @pl.when(step == 1)
+    def _():
+        stacked = jnp.concatenate(
+            [fold_ref[:, c * BLOCK : (c + 1) * BLOCK] for c in range(row_blocks)]
+        ).astype(jnp.float32)
+        order = lax.broadcasted_iota(jnp.int32, (stacked.shape[0], 1), 0)
+        block = lax.rem(order, fold_ref.shape[0]) * row_blocks + order // fold_ref.shape[0]
+
+        def picked(row):
+            return lax.dot_general(
+                (block == row).astype(jnp.float32), stacked, (((0,), (0,)), ((), ())),
+                preferred_element_type=jnp.float32,
+            )
+
+        rows = picked(chosen_row_ref[...])
+        both = jnp.concatenate([rows[:peers], rows[peers:]], axis=-1)
+        send_fold_ref[...] = jnp.broadcast_to(both[:, None], send_fold_ref.shape).astype(jnp.bfloat16)
+        anchor_fold_ref[...] = picked(source_row_ref[...]).astype(jnp.bfloat16)
+        for copy in fold_copies():
+            copy.start()
+
     @pl.when(step == 0)
     def _():
         for p in range(4):
@@ -86,8 +140,6 @@
 
     for d in range(0, ROWS_STEP, 2 * ENC_PAIRS):
         encode(base + 2 + d, ENC_PAIRS)
-    cols = own_ref.shape[1]
-    row_blocks = cols // BLOCK
     for r in range(0, ROWS_STEP, DOT_ROWS):
         parts = [enc_ref[pl.ds(base + r + a, DOT_ROWS)] for a in range(3)]
         window = jnp.concatenate([v.reshape(DOT_ROWS * cols, 3 * chan) for v in parts], axis=-1)
@@ -105,28 +157,21 @@
 
     @pl.when(step == last)
     def _():
-        def send(n):
-            return pltpu.make_async_copy(all_ref.at[chosen_ref[n]], send_ref.at[n], send_sem)
-
-        def anchor(n):
-            return pltpu.make_async_copy(all_ref.at[source_ref[n]], anchor_ref.at[n], anchor_sem)
-
-        @pl.loop(0, send_ref.shape[0])
-        def _(n):
-            pl.when(chosen_ref[n] >= 0)(lambda: send(n).start())
-
-        pl.loop(0, anchor_ref.shape[0])(lambda n: anchor(n).start())
-
-        @pl.loop(0, send_ref.shape[0])
+        ship(0, all_ref.shape[0])
+
+        @pl.loop(0, chosen_ref.shape[0], unroll=4)
         def _(n):
             pl.when(chosen_ref[n] >= 0)(lambda: send(n).wait())
 
-        pltpu.make_async_copy(anchor_ref, anchor_ref, anchor_sem).wait()
+        every = anchor_ref.at[pl.ds(0, source_ref.shape[0])]
+        pltpu.make_async_copy(every, every, anchor_sem).wait()
+        for copy in fold_copies():
+            copy.wait()
         pltpu.make_async_copy(all_ref, out_ref, out_sem).wait()
 
 
 def describe(
-    chosen, source, low, own, high, enc_w, enc_b, head_w, head_b, final_w, final_b
+    chosen, source, folds, low, own, high, enc_w, enc_b, head_w, head_b, final_w, final_b
 ):
     rows, cols, chan = own.shape
     desc = final_w.shape[1]
@@ -135,37 +180,44 @@
     scalars = pl.BlockSpec(memory_space=pltpu.SMEM)
     macs = rows * cols * (12 * chan * chan + 9 * chan * desc + desc * desc)
 
-    def blocks(n):
-        return jax.ShapeDtypeStruct((n, BLOCK, desc), jnp.bfloat16)
+    def blocks(n, height):
+        return jax.ShapeDtypeStruct((n, height, desc), jnp.bfloat16)
 
     return pl.pallas_call(
         describe_kernel,
         grid=(rows // ROWS_STEP,),
-        in_specs=[scalars] * 2 + [whole] * 9,
+        in_specs=[scalars] * 2 + [whole] * 12,
         out_specs=[pl.BlockSpec(memory_space=pl.ANY)] * 3,
-        out_shape=[blocks(count), blocks(chosen.shape[0]), blocks(source.shape[0])],
+        out_shape=[
+            blocks(count, BLOCK),
+            blocks(chosen.shape[0] // 2, 2 * BLOCK + FOLD_ROWS),
+            blocks(source.shape[0] + 1, BLOCK),
+        ],
         scratch_shapes=[
             pltpu.VMEM((rows + 4, cols, 3 * chan), jnp.bfloat16),
             pltpu.VMEM((rows + 2, cols, 3 * chan), jnp.bfloat16),
             pltpu.VMEM((12 * chan, 2 * chan), jnp.bfloat16),
             pltpu.VMEM((count, BLOCK, desc), jnp.bfloat16),
+            pltpu.VMEM((chosen.shape[0] // 2, FOLD_ROWS, desc), jnp.bfloat16),
+            pltpu.VMEM((source.shape[0], BLOCK), jnp.bfloat16),
             pltpu.SemaphoreType.DMA,
             pltpu.SemaphoreType.DMA,
             pltpu.SemaphoreType.DMA,
+            pltpu.SemaphoreType.DMA((2,)),
         ],
         compiler_params=pltpu.CompilerParams(vmem_limit_bytes=56 * 2**20),
         cost_estimate=pl.CostEstimate(
             flops=2 * macs, bytes_accessed=rows * cols * (chan + desc) * 2, transcendentals=rows * cols
         ),
     )(
-        chosen, source, low, own, high, enc_w, enc_b[None], head_w.reshape(-1, desc),
+        chosen, source, chosen[None], source[None], folds, low, own, high, enc_w, enc_b[None], head_w.reshape(-1, desc),
         head_b[None], final_w, final_b[None],
     )
 
 
 def match_kernel(
-    slot_ref, anchor_fold_ref, partner_fold_ref, anchors_ref, arrived_ref, out_ref, anchor_ref,
-    partner_ref, anchor_sem, partner_sem,
+    slot_ref, anchors_ref, arrived_ref, out_ref, anchor_ref, partner_ref, anchor_fold_ref,
+    partner_fold_ref, anchor_sem, partner_sem, fold_sem,
 ):
     groups = out_ref.shape[0] // PAIRS_STEP
 
@@ -181,21 +233,46 @@
         return pltpu.make_async_copy(
             anchors_ref.at[group(g)], anchor_ref.at[group(g)], anchor_sem.at[g]
         )
+
+    pairs = out_ref.shape[0]
+    fold_copies = (
+        pltpu.make_async_copy(
+            arrived_ref.at[:, pl.ds(2 * BLOCK, FOLD_ROWS)], partner_fold_ref, fold_sem.at[0]
+        ),
+        pltpu.make_async_copy(
+            anchors_ref.at[pairs, pl.ds(0, pairs), pl.ds(0, BLOCK)], anchor_fold_ref, fold_sem.at[1]
+        ),
+    )
+    for copy in fold_copies:
+        copy.start()
+
+    def place(pair):
+        return slot_ref[pair] // 2, pl.multiple_of(slot_ref[pair] % 2 * BLOCK, BLOCK)
 
     @pl.loop(0, groups)
     def _(g):
         anchors(g).start()
         for n in range(PAIRS_STEP):
             pair = g * PAIRS_STEP + n
+            owner, start = place(pair)
             pltpu.make_async_copy(
-                arrived_ref.at[slot_ref[pair]], partner_ref.at[pair], partner_sem.at[g]
+                arrived_ref.at[owner, pl.ds(start, BLOCK)], partner_ref.at[pair], partner_sem.at[g]
             ).start()
+
+    for copy in fold_copies:
+        copy.wait()
 
     @pl.loop(0, groups)
     def _(g):
-        anchor_cost = FOLD_PENALTY * anchor_fold_ref[group(g)]
+        anchor_cost = FOLD_PENALTY * anchor_fold_ref[group(g)].astype(jnp.float32)
         anchor_column = jnp.transpose(anchor_cost)
-        partner_column = jnp.transpose(FOLD_PENALTY * partner_fold_ref[group(g)])
+        partner_cost = []
+        for n in range(PAIRS_STEP):
+            owner, start = place(g * PAIRS_STEP + n)
+            both = partner_fold_ref[owner].astype(jnp.float32)
+            tile = jnp.where(start == 0, both[:, :BLOCK], both[:, BLOCK:])
+            partner_cost.append(tile[:1])
+        partner_column = jnp.transpose(FOLD_PENALTY * jnp.concatenate(partner_cost))
         anchors(g).wait()
         here = partner_ref.at[group(g)]
         pltpu.make_async_copy(here, here, partner_sem.at[g]).wait()
@@ -219,19 +296,23 @@
         out_ref[group(g)] = jnp.concatenate(result)
 
 
-def match(slot, anchor_folds, partner_folds, anchors, arrived):
+def match(slot, anchors, arrived):
     pairs = slot.shape[0]
-    whole = pl.BlockSpec(memory_space=pltpu.VMEM)
+    desc = arrived.shape[2]
     return pl.pallas_call(
         match_kernel,
-        in_specs=[pl.BlockSpec(memory_space=pltpu.SMEM), whole, whole]
-        + [pl.BlockSpec(memory_space=pl.ANY)] * 2,
-        out_specs=whole,
+        in_specs=[pl.BlockSpec(memory_space=pltpu.SMEM)] + [pl.BlockSpec(memory_space=pl.ANY)] * 2,
+        out_specs=pl.BlockSpec(memory_space=pltpu.VMEM),
         out_shape=jax.ShapeDtypeStruct((pairs, BLOCK), jnp.float32),
-        scratch_shapes=[pltpu.VMEM(anchors.shape, jnp.bfloat16)] * 2
-        + [pltpu.SemaphoreType.DMA((pairs // PAIRS_STEP,))] * 2,
+        scratch_shapes=[pltpu.VMEM((pairs, BLOCK, desc), jnp.bfloat16)] * 2
+        + [
+            pltpu.VMEM((pairs, BLOCK), jnp.bfloat16),
+            pltpu.VMEM((arrived.shape[0], FOLD_ROWS, desc), jnp.bfloat16),
+        ]
+        + [pltpu.SemaphoreType.DMA((pairs // PAIRS_STEP,))] * 2
+        + [pltpu.SemaphoreType.DMA((2,))],
         compiler_params=pltpu.CompilerParams(vmem_limit_bytes=VMEM_MATCH),
-    )(slot, anchor_folds, partner_folds, anchors, arrived)
+    )(slot, anchors, arrived)
 
 
 def local(
@@ -240,7 +321,6 @@
 ):
     own_band = features[0]
     band_rows, band_cols, _ = own_band.shape
-    desc = final_weight.shape[1]
     tile_count = lax.axis_size("tile")
     tile_here = lax.axis_index("tile")
     section = lax.axis_index("sec")
@@ -252,49 +332,34 @@
 
     block_count = band_rows * band_cols // BLOCK
     pair_count = pair_source.shape[1]
-    capacity = max(2, 2 * pair_count // tile_count)
+    capacity = 2
     wanted = lax.dynamic_index_in_dim(pair_target, 1 - section, 0, keepdims=False).reshape(
         tile_count, pair_count
     )
     matched = (wanted // block_count == tile_here).astype(jnp.int32)
     order_rank = jnp.cumsum(matched, axis=1) - matched
-    slot_hot = matched[:, :, None] * (
-        order_rank[:, :, None] == jnp.arange(capacity)[None, None, :]
+    slot_hot = matched[None] * (
+        order_rank[None] == jnp.arange(capacity)[:, None, None]
     ).astype(jnp.int32)
-    chosen = jnp.sum(slot_hot * (wanted % block_count + 1)[:, :, None], axis=1) - 1
+    chosen = jnp.sum(slot_hot * (wanted % block_count + 1)[None], axis=2) - 1
     targets = lax.dynamic_index_in_dim(wanted, tile_here, 0, keepdims=False)
     owners = targets // block_count
     earlier = jnp.arange(pair_count)[None, :] < jnp.arange(pair_count)[:, None]
     slot_rank = jnp.sum(((owners[None, :] == owners[:, None]) & earlier).astype(jnp.int32), axis=1)
     slot_index = owners * capacity + slot_rank
 
-    own_folds = fold_mask[0].reshape(block_count, BLOCK).astype(jnp.bfloat16)
-    partner_folds = lax.all_to_all(
-        own_folds[jnp.maximum(chosen, 0)], "tile", split_axis=0, concat_axis=0, tiled=True
-    )
-    anchor_folds = lax.ppermute(own_folds[pair_source[0]], "sec", swap)
-
     described, send_blocks, anchors = describe(
-        chosen.reshape(-1), pair_source[0], low, own_band, high, encoder_weight, encoder_bias,
-        head_weight, head_bias, final_weight, final_bias,
-    )
-    anchors, partner_folds, anchor_folds = lax.optimization_barrier(
-        (anchors, partner_folds, anchor_folds)
+        chosen.reshape(-1), pair_source[0], fold_mask[0], low, own_band, high, encoder_weight,
+        encoder_bias, head_weight, head_bias, final_weight, final_bias,
     )
     sibling_anchors = lax.ppermute(anchors, "sec", swap)
-    partner_folds = partner_folds.reshape(tile_count * capacity, BLOCK)[slot_index]
-    partner_folds = partner_folds.astype(jnp.float32)
-    anchor_folds = anchor_folds.astype(jnp.float32)
-    send_blocks, sibling_anchors, slot_index, partner_folds, anchor_folds = lax.optimization_barrier(
-        (send_blocks, sibling_anchors, slot_index, partner_folds, anchor_folds)
-    )
-    arrived = lax.all_to_all(
-        send_blocks.reshape(tile_count, capacity, BLOCK, desc),
-        "tile", split_axis=0, concat_axis=0, tiled=True,
-    ).reshape(tile_count * capacity, BLOCK, desc)
-    confidence = match(slot_index, anchor_folds, partner_folds, sibling_anchors, arrived)
+    send_blocks, sibling_anchors, slot_index = lax.optimization_barrier(
+        (send_blocks, sibling_anchors, slot_index)
+    )
+    arrived = lax.all_to_all(send_blocks, "tile", split_axis=0, concat_axis=0, tiled=True)
+    confidence = match(slot_index, sibling_anchors, arrived)
     confidence = lax.ppermute(confidence, "sec", swap)
-    return (described.reshape(1, band_rows, band_cols, desc), confidence[None])
+    return (described.reshape(1, band_rows, band_cols, -1), confidence[None])
 
 
 def solution(mesh):

time: 184 us -> 179 us (0.973)
  starting transfers between devices: 25.5 us -> 9.9 us
  blocking collectives: 106 us -> 118 us
  waiting for transfers between devices: 5.82 us -> 9.29 us
  local copies, waits for them, and re-layouts: 6.88 us -> 3.67 us
  other arithmetic: 3.87 us -> 1.16 us
    all_to_all x1 -> x0, starting transfers between devices: 14.9 us -> none  [local(): lax.all_to_all(own_folds[jnp.maximum(chosen, 0)], 'tile', split_axis=0, c...]
    all_to_all x1, blocking collectives: 106 us -> 118 us  [local(): lax.all_to_all(send_blocks, 'tile', split_axis=0, concat_axis=0, tiled=True)]
    gather x3 -> x0, local copies, waits for them, and re-layouts: 2.59 us -> none  [the longest x1 1.31 us: local(): own_folds[jnp.maximum(chosen, 0)]]
    convert_element_type x3 -> x0, other arithmetic: 2.03 us -> none  [the longest x1 0.81 us: local(): own_folds = fold_mask[0].reshape(block_count, BLOCK).astype(jnp.bfloat16)]
  transfers between devices with their start and end apart: 6 -> 4, of which waited for: 2 -> 4; matrix products, arithmetic and copies ran while one was open for 3% -> 1% of each run, Pallas kernels for 14% -> 0%
where the time goes in v6:
time: 179 us
  blocking collectives  118 us (66%)
  Pallas kernels  35.8 us (20%)
  starting transfers between devices  9.9 us (6%)
  waiting for transfers between devices  9.29 us (5%)
  local copies, waits for them, and re-layouts  3.67 us (2%)
    all_to_all x1, blocking collectives, local(): lax.all_to_all(send_blocks, 'tile', split_axis=0, concat_axis=0, tiled=True)  118 us
    pallas_call x1, Pallas kernels, describe(): pl.pallas_call(describe_kernel, grid=(rows // ROWS_STEP,), in_specs=[scal...  26.9 us
    pallas_call x1, Pallas kernels, match(): pl.pallas_call(match_kernel, in_specs=[pl.BlockSpec(memory_space=pltpu.SM...  8.87 us
    ppermute x1, waiting for transfers between devices, local(): sibling_anchors = lax.ppermute(anchors, 'sec', swap)  6.48 us
    ppermute x1, starting transfers between devices, local(): low = lax.ppermute(own_band[-2:], 'tile', down)  5.01 us
  transfers between devices with their start and end apart: 4, of which 4 were waited for; matrix products, arithmetic and copies ran while one was open for 1% of the time, Pallas kernels for 0%

profile of v6, /device:TPU:1, one launch (start us, length us, event | category | flops | bytes accessed | tf_op | source)
XLA Modules:
  0.0 178.7 jit_solution(12963497939284676533)
XLA Ops:
  0.6 0.0 copy-start
  0.6 1.1 slice_bitcast_fusion
  1.7 1.3 collective-permute-start.1
  3.0 5.0 %collective-permute-start = (bf16[2,384,128]{2,1,0:T(8,128)(2,1)S(1)}, bf16[2,384,128]{2,1,0:T(8,128)(2,1)S(1)}, u32[]{:S(2)}, u32[]{:S(2)}) collective-permute-start(bf16[2,384,128]{2,1,0:T(8,128)(2,1)S(1)} %get-tuple-element.18), channel_id=1, source_target_pairs={{0,2},{2,4},{4,6},{6,8},{8,10},{10,12},{12,14},{14,16},{16,18},{18... | collective-permute-start | bytes 589832 | tf_op jit(solution)/shard_map/ppermute | solution.py:330
  8.0 0.0 copy-done
  8.0 0.1 dynamic-slice_reduce_fusion
  8.1 0.1 reshape.121
  8.2 0.2 reduce_window_sum.11
  8.5 0.1 multiply_reduce_fusion
  8.6 0.6 sub.37.chosen_row_ref
  9.2 0.6 sub.36.chosen_ref
  9.8 0.9 collective-permute-done.1.high_ref
  10.7 0.0 copy-start.1
  10.7 0.9 collective-permute-done.low_ref
  11.5 0.0 copy-start.2
  11.5 0.0 copy-done.1
  11.6 0.7 copy-done.2
  12.2 26.9 %shard_map.113 = (bf16[96,128,256]{2,1,0:T(8,128)(2,1)}, bf16[64,272,256]{2,1,0:T(8,128)(2,1)}, bf16[65,128,256]{2,1,0:T(8,128)(2,1)}) custom-call(s32[128]{0:T(128)} %sub.36.chosen_ref, s32[64]{0:T(128)} %bitcast.25, s32[1,128]{1,0:T(1,128)} %sub.37.chosen_row_ref, s32[1,64]{1,0:T(1,128)} %source_row_ref.1, s32[32,384]{1,0:T(8,128)} %bitcast.22, ...), custom_call_target="tpu_custom_call" | custom-call | flops 13690208256 | bytes 9437184 | tf_op jit(solution)/shard_map/pallas_call | solution.py:186
  39.1 1.5 collective-permute-start.2
  40.7 0.2 convert_reduce_fusion
  40.9 0.5 multiply_add_fusion.slot_ref
  41.4 6.5 %collective-permute-done.2.anchors_ref = bf16[65,128,256]{2,1,0:T(8,128)(2,1)} collective-permute-done((bf16[65,128,256]{2,1,0:T(8,128)(2,1)}, bf16[65,128,256]{2,1,0:T(8,128)(2,1)}, u32[]{:S(2)}, u32[]{:S(2)}) %collective-permute-start.2) | collective-permute-done | bytes 4259872 | tf_op jit(solution)/shard_map/ppermute | solution.py:355
  47.9 118.1 %all_to_all.5.arrived_ref = bf16[64,272,256]{2,1,0:T(8,128)(2,1)} all-to-all(bf16[64,272,256]{2,1,0:T(8,128)(2,1)} %get-tuple-element.13), channel_id=1, replica_groups=mesh['tile'=64,'sec'=2] {'tile'}, dimensions={0} | all-to-all | bytes 17825792 | tf_op jit(solution)/shard_map/all_to_all | solution.py:359
  166.0 8.9 %shard_map.114 = f32[64,128]{1,0:T(8,128)} custom-call(s32[64]{0:T(128)} %multiply_add_fusion.slot_ref, bf16[65,128,256]{2,1,0:T(8,128)(2,1)} %collective-permute-done.2.anchors_ref, bf16[64,272,256]{2,1,0:T(8,128)(2,1)} %all_to_all.5.arrived_ref), custom_call_target="tpu_custom_call" | custom-call | tf_op jit(solution)/shard_map/pallas_call | solution.py:302
  174.9 2.1 %collective-permute-start.3 = (f32[64,128]{1,0:T(8,128)}, f32[64,128]{1,0:T(8,128)S(1)}, u32[]{:S(2)}, u32[]{:S(2)}) collective-permute-start(f32[64,128]{1,0:T(8,128)} %shard_map.114), channel_id=1, source_target_pairs={{0,1},{1,0},{2,3},{3,2},{4,5},{5,4},{6,7},{7,6},{8,9},{9,8},{10,11... | collective-permute-start | bytes 98312 | tf_op jit(solution)/shard_map/ppermute | solution.py:361
  177.0 1.1 collective-permute-done.3
  178.1 0.6 copy.13
  (6 shorter events, 0.1 us)
Async XLA Ops:
  0.6 7.4 %copy-start = (s32[2,4096]{1,0:T(2,128)S(1)}, s32[2,4096]{1,0:T(2,128)}, u32[]{:S(2)}) copy-start(s32[2,4096]{1,0:T(2,128)} %param.19) | copy-start | bytes 98308
  1.7 9.0 %collective-permute-start.1 = (bf16[2,384,128]{2,1,0:T(8,128)(2,1)S(1)}, bf16[2,384,128]{2,1,0:T(8,128)(2,1)S(1)}, u32[]{:S(2)}, u32[]{:S(2)}) collective-permute-start(bf16[2,384,128]{2,1,0:T(8,128)(2,1)S(1)} %get-tuple-element.17), channel_id=1, source_target_pairs={{2,0},{4,2},{6,4},{8,6},{10,8},{12,10},{14,12},{16,14},{18,16},{20... | collective-permute-start | bytes 589832 | tf_op jit(solution)/shard_map/ppermute | solution.py:331
  3.0 8.5 %collective-permute-start = (bf16[2,384,128]{2,1,0:T(8,128)(2,1)S(1)}, bf16[2,384,128]{2,1,0:T(8,128)(2,1)S(1)}, u32[]{:S(2)}, u32[]{:S(2)}) collective-permute-start(bf16[2,384,128]{2,1,0:T(8,128)(2,1)S(1)} %get-tuple-element.18), channel_id=1, source_target_pairs={{0,2},{2,4},{4,6},{6,8},{8,10},{10,12},{12,14},{14,16},{16,18},{18... | collective-permute-start | bytes 589832 | tf_op jit(solution)/shard_map/ppermute | solution.py:330
  10.7 0.9 copy-start.1
  11.5 0.7 copy-start.2
  39.1 8.8 %collective-permute-start.2 = (bf16[65,128,256]{2,1,0:T(8,128)(2,1)}, bf16[65,128,256]{2,1,0:T(8,128)(2,1)}, u32[]{:S(2)}, u32[]{:S(2)}) collective-permute-start(bf16[65,128,256]{2,1,0:T(8,128)(2,1)} %get-tuple-element.10), channel_id=1, source_target_pairs={{0,1},{1,0},{2,3},{3,2},{4,5},{5,4},{6,7},{7,6},{8,9},{9,8},{10,11... | collective-permute-start | bytes 12779528 | tf_op jit(solution)/shard_map/ppermute | solution.py:355
  174.9 3.1 %collective-permute-start.3 = (f32[64,128]{1,0:T(8,128)}, f32[64,128]{1,0:T(8,128)S(1)}, u32[]{:S(2)}, u32[]{:S(2)}) collective-permute-start(f32[64,128]{1,0:T(8,128)} %shard_map.114), channel_id=1, source_target_pairs={{0,1},{1,0},{2,3},{3,2},{4,5},{5,4},{6,7},{7,6},{8,9},{9,8},{10,11... | collective-permute-start | bytes 98312 | tf_op jit(solution)/shard_map/ppermute | solution.py:361

commit v7 on v6

--- a/solution.py
+++ b/solution.py
@@ -12,6 +12,7 @@
 FOLD_PENALTY = 200.0
 ROWS_STEP = 8
 FOLD_ROWS = 16
+LANES = 128
 ENC_PAIRS = 1
 DOT_ROWS = 8
 PAIRS_STEP = 16
@@ -69,7 +70,8 @@
     peers = send_ref.shape[0]
 
     def send(n):
-        place = send_ref.at[n % peers, pl.ds(pl.multiple_of(n // peers * BLOCK, BLOCK), BLOCK)]
+        start = pl.multiple_of(n // peers * 2 * BLOCK, 2 * BLOCK)
+        place = send_ref.at[n % peers, pl.ds(start, 2 * BLOCK)]
         return pltpu.make_async_copy(all_ref.at[chosen_ref[n]], place, send_sem)
 
     def anchor(n):
@@ -87,10 +89,10 @@
     def fold_copies():
         return (
             pltpu.make_async_copy(
-                send_fold_ref, send_ref.at[:, pl.ds(2 * BLOCK, FOLD_ROWS)], fold_sem.at[0]
+                send_fold_ref, send_ref.at[:, pl.ds(4 * BLOCK, FOLD_ROWS)], fold_sem.at[0]
             ),
             pltpu.make_async_copy(
-                anchor_fold_ref, anchor_ref.at[pairs, pl.ds(0, pairs), pl.ds(0, BLOCK)], fold_sem.at[1]
+                anchor_fold_ref, anchor_ref.at[pairs, pl.ds(0, pairs)], fold_sem.at[1]
             ),
         )
 
@@ -109,8 +111,9 @@
             )
 
         rows = picked(chosen_row_ref[...])
-        both = jnp.concatenate([rows[:peers], rows[peers:]], axis=-1)
-        send_fold_ref[...] = jnp.broadcast_to(both[:, None], send_fold_ref.shape).astype(jnp.bfloat16)
+        place = lax.broadcasted_iota(jnp.int32, send_fold_ref.shape, 1)
+        both = jnp.where(place == 0, rows[:peers][:, None], rows[peers:][:, None])
+        send_fold_ref[...] = both.astype(jnp.bfloat16)
         anchor_fold_ref[...] = picked(source_row_ref[...]).astype(jnp.bfloat16)
         for copy in fold_copies():
             copy.start()
@@ -149,11 +152,18 @@
         raw = raw + final_b_ref[...]
         norm = jnp.sum(raw * raw, axis=-1, keepdims=True)
         unit = (raw * lax.rsqrt(norm + 1e-06)).astype(jnp.bfloat16)
-        all_ref[pl.ds((base + r) * row_blocks, DOT_ROWS * row_blocks)] = unit.reshape(
-            DOT_ROWS * row_blocks, BLOCK, unit.shape[1]
-        )
+        place = pl.ds((base + r) * row_blocks, DOT_ROWS * row_blocks)
+        for h in range(2):
+            all_ref[place, h * BLOCK : (h + 1) * BLOCK] = unit[:, h * LANES : (h + 1) * LANES].reshape(
+                DOT_ROWS * row_blocks, BLOCK, LANES
+            )
     done = pl.ds(base * row_blocks, ROWS_STEP * row_blocks)
-    pltpu.make_async_copy(all_ref.at[done], out_ref.at[done], out_sem).start()
+    for h in range(2):
+        pltpu.make_async_copy(
+            all_ref.at[done, pl.ds(h * BLOCK, BLOCK)],
+            out_ref.at[done, :, pl.ds(h * LANES, LANES)],
+            out_sem,
+        ).start()
 
     @pl.when(step == last)
     def _():
@@ -167,7 +177,7 @@
         pltpu.make_async_copy(every, every, anchor_sem).wait()
         for copy in fold_copies():
             copy.wait()
-        pltpu.make_async_copy(all_ref, out_ref, out_sem).wait()
+        pltpu.make_async_copy(all_ref, all_ref, out_sem).wait()
 
 
 def describe(
@@ -180,8 +190,8 @@
     scalars = pl.BlockSpec(memory_space=pltpu.SMEM)
     macs = rows * cols * (12 * chan * chan + 9 * chan * desc + desc * desc)
 
-    def blocks(n, height):
-        return jax.ShapeDtypeStruct((n, height, desc), jnp.bfloat16)
+    def half_lanes(n, height):
+        return jax.ShapeDtypeStruct((n, height, LANES), jnp.bfloat16)
 
     return pl.pallas_call(
         describe_kernel,
@@ -189,16 +199,16 @@
         in_specs=[scalars] * 2 + [whole] * 12,
         out_specs=[pl.BlockSpec(memory_space=pl.ANY)] * 3,
         out_shape=[
-            blocks(count, BLOCK),
-            blocks(chosen.shape[0] // 2, 2 * BLOCK + FOLD_ROWS),
-            blocks(source.shape[0] + 1, BLOCK),
+            jax.ShapeDtypeStruct((count, BLOCK, desc), jnp.bfloat16),
+            half_lanes(chosen.shape[0] // 2, 4 * BLOCK + FOLD_ROWS),
+            half_lanes(source.shape[0] + 1, 2 * BLOCK),
         ],
         scratch_shapes=[
             pltpu.VMEM((rows + 4, cols, 3 * chan), jnp.bfloat16),
             pltpu.VMEM((rows + 2, cols, 3 * chan), jnp.bfloat16),
             pltpu.VMEM((12 * chan, 2 * chan), jnp.bfloat16),
-            pltpu.VMEM((count, BLOCK, desc), jnp.bfloat16),
-            pltpu.VMEM((chosen.shape[0] // 2, FOLD_ROWS, desc), jnp.bfloat16),
+            pltpu.VMEM((count, 2 * BLOCK, LANES), jnp.bfloat16),
+            pltpu.VMEM((chosen.shape[0] // 2, FOLD_ROWS, LANES), jnp.bfloat16),
             pltpu.VMEM((source.shape[0], BLOCK), jnp.bfloat16),
             pltpu.SemaphoreType.DMA,
             pltpu.SemaphoreType.DMA,
@@ -237,17 +247,17 @@
     pairs = out_ref.shape[0]
     fold_copies = (
         pltpu.make_async_copy(
-            arrived_ref.at[:, pl.ds(2 * BLOCK, FOLD_ROWS)], partner_fold_ref, fold_sem.at[0]
+            arrived_ref.at[:, pl.ds(4 * BLOCK, FOLD_ROWS)], partner_fold_ref, fold_sem.at[0]
         ),
         pltpu.make_async_copy(
-            anchors_ref.at[pairs, pl.ds(0, pairs), pl.ds(0, BLOCK)], anchor_fold_ref, fold_sem.at[1]
+            anchors_ref.at[pairs, pl.ds(0, pairs)], anchor_fold_ref, fold_sem.at[1]
         ),
     )
     for copy in fold_copies:
         copy.start()
 
     def place(pair):
-        return slot_ref[pair] // 2, pl.multiple_of(slot_ref[pair] % 2 * BLOCK, BLOCK)
+        return slot_ref[pair] // 2, pl.multiple_of(slot_ref[pair] % 2 * 2 * BLOCK, 2 * BLOCK)
 
     @pl.loop(0, groups)
     def _(g):
@@ -256,7 +266,7 @@
             pair = g * PAIRS_STEP + n
             owner, start = place(pair)
             pltpu.make_async_copy(
-                arrived_ref.at[owner, pl.ds(start, BLOCK)], partner_ref.at[pair], partner_sem.at[g]
+                arrived_ref.at[owner, pl.ds(start, 2 * BLOCK)], partner_ref.at[pair], partner_sem.at[g]
             ).start()
 
     for copy in fold_copies:
@@ -270,14 +280,18 @@
         for n in range(PAIRS_STEP):
             owner, start = place(g * PAIRS_STEP + n)
             both = partner_fold_ref[owner].astype(jnp.float32)
-            tile = jnp.where(start == 0, both[:, :BLOCK], both[:, BLOCK:])
-            partner_cost.append(tile[:1])
+            partner_cost.append(jnp.where(start == 0, both[0:1], both[1:2]))
         partner_column = jnp.transpose(FOLD_PENALTY * jnp.concatenate(partner_cost))
         anchors(g).wait()
         here = partner_ref.at[group(g)]
         pltpu.make_async_copy(here, here, partner_sem.at[g]).wait()
-        left = [anchor_ref[g * PAIRS_STEP + n] for n in range(PAIRS_STEP)]
-        right = [partner_ref[g * PAIRS_STEP + n] for n in range(PAIRS_STEP)]
+        left, right = [
+            [
+                jnp.concatenate([ref[g * PAIRS_STEP + n, h * BLOCK : (h + 1) * BLOCK] for h in range(2)], axis=1)
+                for n in range(PAIRS_STEP)
+            ]
+            for ref in (anchor_ref, partner_ref)
+        ]
 
         over_i = []
         for n in range(PAIRS_STEP):
@@ -298,16 +312,15 @@
 
 def match(slot, anchors, arrived):
     pairs = slot.shape[0]
-    desc = arrived.shape[2]
     return pl.pallas_call(
         match_kernel,
         in_specs=[pl.BlockSpec(memory_space=pltpu.SMEM)] + [pl.BlockSpec(memory_space=pl.ANY)] * 2,
         out_specs=pl.BlockSpec(memory_space=pltpu.VMEM),
         out_shape=jax.ShapeDtypeStruct((pairs, BLOCK), jnp.float32),
-        scratch_shapes=[pltpu.VMEM((pairs, BLOCK, desc), jnp.bfloat16)] * 2
+        scratch_shapes=[pltpu.VMEM((pairs, 2 * BLOCK, LANES), jnp.bfloat16)] * 2
         + [
             pltpu.VMEM((pairs, BLOCK), jnp.bfloat16),
-            pltpu.VMEM((arrived.shape[0], FOLD_ROWS, desc), jnp.bfloat16),
+            pltpu.VMEM((arrived.shape[0], FOLD_ROWS, LANES), jnp.bfloat16),
         ]
         + [pltpu.SemaphoreType.DMA((pairs // PAIRS_STEP,))] * 2
         + [pltpu.SemaphoreType.DMA((2,))],

time: 179 us -> 176 us (0.983)
  blocking collectives: 118 us -> 115 us
    all_to_all x1, blocking collectives: 118 us -> 115 us  [local(): lax.all_to_all(send_blocks, 'tile', split_axis=0, concat_axis=0, tiled=True)]
where the time goes in v7:
time: 176 us
  blocking collectives  115 us (65%)
  Pallas kernels  35.6 us (20%)
  starting transfers between devices  9.91 us (6%)
  waiting for transfers between devices  9.26 us (5%)
  local copies, waits for them, and re-layouts  3.7 us (2%)
    all_to_all x1, blocking collectives, local(): lax.all_to_all(send_blocks, 'tile', split_axis=0, concat_axis=0, tiled=True)  115 us
    pallas_call x1, Pallas kernels, describe(): pl.pallas_call(describe_kernel, grid=(rows // ROWS_STEP,), in_specs=[scal...  26.9 us
    pallas_call x1, Pallas kernels, match(): pl.pallas_call(match_kernel, in_specs=[pl.BlockSpec(memory_space=pltpu.SM...  8.78 us
    ppermute x1, waiting for transfers between devices, local(): sibling_anchors = lax.ppermute(anchors, 'sec', swap)  6.48 us
    ppermute x1, starting transfers between devices, local(): low = lax.ppermute(own_band[-2:], 'tile', down)  5.01 us
  transfers between devices with their start and end apart: 4, of which 4 were waited for; matrix products, arithmetic and copies ran while one was open for 1% of the time, Pallas kernels for 0%

profile of v7, /device:TPU:1, one launch (start us, length us, event | category | flops | bytes accessed | tf_op | source)
XLA Modules:
  0.0 175.9 jit_solution(17979297143253200707)
XLA Ops:
  0.6 0.0 copy-start
  0.6 1.1 slice_bitcast_fusion
  1.7 1.3 collective-permute-start.1
  3.0 5.0 %collective-permute-start = (bf16[2,384,128]{2,1,0:T(8,128)(2,1)S(1)}, bf16[2,384,128]{2,1,0:T(8,128)(2,1)S(1)}, u32[]{:S(2)}, u32[]{:S(2)}) collective-permute-start(bf16[2,384,128]{2,1,0:T(8,128)(2,1)S(1)} %get-tuple-element.18), channel_id=1, source_target_pairs={{0,2},{2,4},{4,6},{6,8},{8,10},{10,12},{12,14},{14,16},{16,18},{18... | collective-permute-start | bytes 589832 | tf_op jit(solution)/shard_map/ppermute | solution.py:343
  8.0 0.0 copy-done
  8.0 0.1 dynamic-slice_reduce_fusion
  8.1 0.1 reshape.121
  8.2 0.2 reduce_window_sum.11
  8.5 0.1 multiply_reduce_fusion
  8.6 0.6 sub.37.chosen_row_ref
  9.2 0.6 sub.36.chosen_ref
  9.8 0.8 collective-permute-done.1.high_ref
  10.7 0.0 copy-start.1
  10.7 0.9 collective-permute-done.low_ref
  11.5 0.0 copy-start.2
  11.5 0.0 copy-done.1
  11.6 0.7 copy-done.2
  12.2 26.9 %shard_map.113 = (bf16[96,128,256]{2,1,0:T(8,128)(2,1)}, bf16[64,528,128]{2,1,0:T(8,128)(2,1)}, bf16[65,256,128]{2,1,0:T(8,128)(2,1)}) custom-call(s32[128]{0:T(128)} %sub.36.chosen_ref, s32[64]{0:T(128)} %bitcast.25, s32[1,128]{1,0:T(1,128)} %sub.37.chosen_row_ref, s32[1,64]{1,0:T(1,128)} %source_row_ref.1, s32[32,384]{1,0:T(8,128)} %bitcast.22, ...), custom_call_target="tpu_custom_call" | custom-call | flops 13690208256 | bytes 9437184 | tf_op jit(solution)/shard_map/pallas_call | solution.py:196
  39.1 1.9 %collective-permute-start.2 = (bf16[65,256,128]{2,1,0:T(8,128)(2,1)}, bf16[65,256,128]{2,1,0:T(8,128)(2,1)}, u32[]{:S(2)}, u32[]{:S(2)}) collective-permute-start(bf16[65,256,128]{2,1,0:T(8,128)(2,1)} %get-tuple-element.10), channel_id=1, source_target_pairs={{0,1},{1,0},{2,3},{3,2},{4,5},{5,4},{6,7},{7,6},{8,9},{9,8},{10,11... | collective-permute-start | bytes 12779528 | tf_op jit(solution)/shard_map/ppermute | solution.py:368
  41.1 0.2 convert_reduce_fusion
  41.2 0.5 multiply_add_fusion.slot_ref
  41.8 6.5 %collective-permute-done.2.anchors_ref = bf16[65,256,128]{2,1,0:T(8,128)(2,1)} collective-permute-done((bf16[65,256,128]{2,1,0:T(8,128)(2,1)}, bf16[65,256,128]{2,1,0:T(8,128)(2,1)}, u32[]{:S(2)}, u32[]{:S(2)}) %collective-permute-start.2) | collective-permute-done | bytes 4259872 | tf_op jit(solution)/shard_map/ppermute | solution.py:368
  48.2 115.5 %all_to_all.5.arrived_ref = bf16[64,528,128]{2,1,0:T(8,128)(2,1)} all-to-all(bf16[64,528,128]{2,1,0:T(8,128)(2,1)} %get-tuple-element.13), channel_id=1, replica_groups=mesh['tile'=64,'sec'=2] {'tile'}, dimensions={0} | all-to-all | bytes 17301504 | tf_op jit(solution)/shard_map/all_to_all | solution.py:372
  163.7 8.8 %shard_map.114 = f32[64,128]{1,0:T(8,128)} custom-call(s32[64]{0:T(128)} %multiply_add_fusion.slot_ref, bf16[65,256,128]{2,1,0:T(8,128)(2,1)} %collective-permute-done.2.anchors_ref, bf16[64,528,128]{2,1,0:T(8,128)(2,1)} %all_to_all.5.arrived_ref), custom_call_target="tpu_custom_call" | custom-call | tf_op jit(solution)/shard_map/pallas_call | solution.py:315
  172.5 1.7 collective-permute-start.3
  174.2 1.1 collective-permute-done.3
  175.3 0.6 copy.13
  (6 shorter events, 0.1 us)
Async XLA Ops:
  0.6 7.4 %copy-start = (s32[2,4096]{1,0:T(2,128)S(1)}, s32[2,4096]{1,0:T(2,128)}, u32[]{:S(2)}) copy-start(s32[2,4096]{1,0:T(2,128)} %param.19) | copy-start | bytes 98308
  1.7 9.0 %collective-permute-start.1 = (bf16[2,384,128]{2,1,0:T(8,128)(2,1)S(1)}, bf16[2,384,128]{2,1,0:T(8,128)(2,1)S(1)}, u32[]{:S(2)}, u32[]{:S(2)}) collective-permute-start(bf16[2,384,128]{2,1,0:T(8,128)(2,1)S(1)} %get-tuple-element.17), channel_id=1, source_target_pairs={{2,0},{4,2},{6,4},{8,6},{10,8},{12,10},{14,12},{16,14},{18,16},{20... | collective-permute-start | bytes 589832 | tf_op jit(solution)/shard_map/ppermute | solution.py:344
  3.0 8.5 %collective-permute-start = (bf16[2,384,128]{2,1,0:T(8,128)(2,1)S(1)}, bf16[2,384,128]{2,1,0:T(8,128)(2,1)S(1)}, u32[]{:S(2)}, u32[]{:S(2)}) collective-permute-start(bf16[2,384,128]{2,1,0:T(8,128)(2,1)S(1)} %get-tuple-element.18), channel_id=1, source_target_pairs={{0,2},{2,4},{4,6},{6,8},{8,10},{10,12},{12,14},{14,16},{16,18},{18... | collective-permute-start | bytes 589832 | tf_op jit(solution)/shard_map/ppermute | solution.py:343
  10.7 0.9 copy-start.1
  11.5 0.7 copy-start.2
  39.1 9.1 %collective-permute-start.2 = (bf16[65,256,128]{2,1,0:T(8,128)(2,1)}, bf16[65,256,128]{2,1,0:T(8,128)(2,1)}, u32[]{:S(2)}, u32[]{:S(2)}) collective-permute-start(bf16[65,256,128]{2,1,0:T(8,128)(2,1)} %get-tuple-element.10), channel_id=1, source_target_pairs={{0,1},{1,0},{2,3},{3,2},{4,5},{5,4},{6,7},{7,6},{8,9},{9,8},{10,11... | collective-permute-start | bytes 12779528 | tf_op jit(solution)/shard_map/ppermute | solution.py:368
  172.5 2.8 %collective-permute-start.3 = (f32[64,128]{1,0:T(8,128)}, f32[64,128]{1,0:T(8,128)S(1)}, u32[]{:S(2)}, u32[]{:S(2)}) collective-permute-start(f32[64,128]{1,0:T(8,128)} %shard_map.114), channel_id=1, source_target_pairs={{0,1},{1,0},{2,3},{3,2},{4,5},{5,4},{6,7},{7,6},{8,9},{9,8},{10,11... | collective-permute-start | bytes 98312 | tf_op jit(solution)/shard_map/ppermute | solution.py:374

commit v8 on v7

--- a/solution.py
+++ b/solution.py
@@ -10,12 +10,13 @@
 BLOCK = 128
 SCORE_SCALE = 10.0
 FOLD_PENALTY = 200.0
+LOG2_E = 1.4426950408889634
 ROWS_STEP = 8
 FOLD_ROWS = 16
 LANES = 128
 ENC_PAIRS = 1
 DOT_ROWS = 8
-PAIRS_STEP = 16
+PAIRS_STEP = 32
 VMEM_MATCH = 56 * 2**20
 
 
@@ -29,22 +30,68 @@
 
 
 def describe_kernel(
-    chosen_ref, source_ref, chosen_row_ref, source_row_ref, fold_ref, low_ref, own_ref, high_ref, enc_w_ref, enc_b_ref, head_w_ref,
-    head_b_ref, final_w_ref, final_b_ref, out_ref, send_ref, anchor_ref, wide_ref, enc_ref,
-    pair_w_ref, all_ref, send_fold_ref, anchor_fold_ref, out_sem, send_sem, anchor_sem,
+    chosen_ref, source_ref, chosen_row_ref, source_row_ref, fold_ref, low_ref, own_ref, high_ref,
+    enc_w_hbm, enc_b_ref, head_w_hbm, head_b_ref, final_w_hbm, final_b_ref, out_ref, send_ref,
+    anchor_ref, feature_ref, enc_w_ref, head_w_ref, final_w_ref, in_sem, weight_sem, wide_ref,
+    enc_ref, pair_w_ref, all_ref, send_fold_ref, anchor_fold_ref, out_sem, send_sem, anchor_sem,
     fold_sem,
 ):
     step = pl.program_id(0)
     last = pl.num_programs(0) - 1
     chan = own_ref.shape[2]
+    height = own_ref.shape[0]
+    steps = height // ROWS_STEP
     tile_here = lax.axis_index("tile")
     top = jnp.where(tile_here == 0, 0, -1)
     bottom = jnp.where(tile_here == lax.axis_size("tile") - 1, enc_ref.shape[0] - 1, -1)
     enc_b = jnp.concatenate([enc_b_ref[...]] * 2, axis=-1)
 
-    def put_features(first, rows):
+    def feature_copies(i):
+        first = 0 if i == 0 else i * ROWS_STEP + 2
+        end = min((i + 1) * ROWS_STEP + 2, height)
+        parts = [(own_ref.at[pl.ds(first, end - first)], first + 2)]
+        if i == 0:
+            parts.append((low_ref, 0))
+        if i == steps - 1:
+            parts.append((high_ref, height + 2))
+        return [
+            pltpu.make_async_copy(
+                part, feature_ref.at[pl.ds(place, part.shape[0])], in_sem.at[2 * i + n]
+            )
+            for n, (part, place) in enumerate(parts)
+        ]
+
+    weight_copies = [
+        pltpu.make_async_copy(source, place, weight_sem.at[n])
+        for n, (source, place) in enumerate(
+            ((enc_w_hbm, enc_w_ref), (head_w_hbm, head_w_ref), (final_w_hbm, final_w_ref))
+        )
+    ]
+
+    @pl.when(step == 0)
+    def _():
+        weight_copies[0].start()
+        for copy in feature_copies(0):
+            copy.start()
+        for copy in weight_copies[1:]:
+            copy.start()
+        for i in range(1, steps):
+            for copy in feature_copies(i):
+                copy.start()
+
+    for i in range(steps):
+
+        @pl.when(step == i)
+        def _(i=i):
+            if i == 0:
+                weight_copies[0].wait()
+            for copy in feature_copies(i):
+                copy.wait()
+
+    def put_features(first, count):
+        rows = feature_ref[pl.ds(first, count)]
         for b, copy in enumerate(side_copies(rows.astype(jnp.float32))):
-            wide_ref[pl.ds(first, rows.shape[0]), :, b * chan : (b + 1) * chan] = copy
+            wide_ref[pl.ds(first, count), :, b * chan : (b + 1) * chan] = copy
 
     def encode(first, pairs):
         window = jnp.concatenate(
@@ -126,23 +173,20 @@
                 zero = jnp.zeros((chan, chan), jnp.bfloat16)
                 pair_w_ref[k, 0:chan] = enc_w_ref[p, b] if p < 3 else zero
                 pair_w_ref[k, chan : 2 * chan] = enc_w_ref[p - 1, b] if p > 0 else zero
-        put_features(0, low_ref[...])
-        put_features(2, own_ref[pl.ds(0, 2)])
+        put_features(0, 4)
         encode(0, 1)
 
     base = step * ROWS_STEP
-    put_features(base + 4, own_ref[pl.ds(base + 2, ROWS_STEP - 2)])
-
-    @pl.when(step < last)
-    def _():
-        put_features(base + ROWS_STEP + 2, own_ref[pl.ds(base + ROWS_STEP, 2)])
-
-    @pl.when(step == last)
-    def _():
-        put_features(base + ROWS_STEP + 2, high_ref[...])
+    put_features(base + 4, ROWS_STEP)
 
     for d in range(0, ROWS_STEP, 2 * ENC_PAIRS):
         encode(base + 2 + d, ENC_PAIRS)
+
+    @pl.when(step == 0)
+    def _():
+        for copy in weight_copies[1:]:
+            copy.wait()
+
     for r in range(0, ROWS_STEP, DOT_ROWS):
         parts = [enc_ref[pl.ds(base + r + a, DOT_ROWS)] for a in range(3)]
         window = jnp.concatenate([v.reshape(DOT_ROWS * cols, 3 * chan) for v in parts], axis=-1)
@@ -188,6 +232,7 @@
     count = rows * cols // BLOCK
     whole = pl.BlockSpec(memory_space=pltpu.VMEM)
     scalars = pl.BlockSpec(memory_space=pltpu.SMEM)
+    anywhere = pl.BlockSpec(memory_space=pl.ANY)
     macs = rows * cols * (12 * chan * chan + 9 * chan * desc + desc * desc)
 
     def half_lanes(n, height):
@@ -196,7 +241,10 @@
     return pl.pallas_call(
         describe_kernel,
         grid=(rows // ROWS_STEP,),
-        in_specs=[scalars] * 2 + [whole] * 12,
+        in_specs=[scalars] * 2
+        + [whole] * 3
+        + [anywhere] * 4
+        + [whole, anywhere, whole, anywhere, whole],
         out_specs=[pl.BlockSpec(memory_space=pl.ANY)] * 3,
         out_shape=[
             jax.ShapeDtypeStruct((count, BLOCK, desc), jnp.bfloat16),
@@ -204,6 +252,12 @@
             half_lanes(source.shape[0] + 1, 2 * BLOCK),
         ],
         scratch_shapes=[
+            pltpu.VMEM((rows + 4, cols, chan), jnp.bfloat16),
+            pltpu.VMEM(enc_w.shape, jnp.bfloat16),
+            pltpu.VMEM((9 * chan, desc), jnp.bfloat16),
+            pltpu.VMEM(final_w.shape, jnp.bfloat16),
+            pltpu.SemaphoreType.DMA((2 * (rows // ROWS_STEP),)),
+            pltpu.SemaphoreType.DMA((3,)),
             pltpu.VMEM((rows + 4, cols, 3 * chan), jnp.bfloat16),
             pltpu.VMEM((rows + 2, cols, 3 * chan), jnp.bfloat16),
             pltpu.VMEM((12 * chan, 2 * chan), jnp.bfloat16),
@@ -232,9 +286,13 @@
     groups = out_ref.shape[0] // PAIRS_STEP
 
     def products(left, right):
-        return SCORE_SCALE * lax.dot_general(
+        return SCORE_SCALE * LOG2_E * lax.dot_general(
             left, right, (((1,), (1,)), ((), ())), preferred_element_type=jnp.float32
         )
+
+    def relative_cost(folds):
+        least = jnp.min(folds, axis=1, keepdims=True)
+        return FOLD_PENALTY * LOG2_E * (folds - least)
 
     def group(g):
         return pl.ds(g * PAIRS_STEP, PAIRS_STEP)
@@ -274,14 +332,14 @@
 
     @pl.loop(0, groups)
     def _(g):
-        anchor_cost = FOLD_PENALTY * anchor_fold_ref[group(g)].astype(jnp.float32)
+        anchor_cost = relative_cost(anchor_fold_ref[group(g)].astype(jnp.float32))
         anchor_column = jnp.transpose(anchor_cost)
-        partner_cost = []
+        partner_fold = []
         for n in range(PAIRS_STEP):
             owner, start = place(g * PAIRS_STEP + n)
             both = partner_fold_ref[owner].astype(jnp.float32)
-            partner_cost.append(jnp.where(start == 0, both[0:1], both[1:2]))
-        partner_column = jnp.transpose(FOLD_PENALTY * jnp.concatenate(partner_cost))
+            partner_fold.append(jnp.where(start == 0, both[0:1], both[1:2]))
+        partner_column = jnp.transpose(relative_cost(jnp.concatenate(partner_fold)))
         anchors(g).wait()
         here = partner_ref.at[group(g)]
         pltpu.make_async_copy(here, here, partner_sem.at[g]).wait()
@@ -296,17 +354,15 @@
         over_i = []
         for n in range(PAIRS_STEP):
             by_i = products(left[n], right[n]) - anchor_column[:, n : n + 1]
-            peak = jnp.max(by_i, axis=0, keepdims=True)
-            over_i.append(peak + jnp.log(jnp.sum(jnp.exp(by_i - peak), axis=0, keepdims=True)))
+            over_i.append(jnp.log2(jnp.sum(jnp.exp2(by_i), axis=0, keepdims=True)))
         over_i = jnp.transpose(jnp.concatenate(over_i))
         result = []
         for n in range(PAIRS_STEP):
             plain = products(right[n], left[n])
             by_j = plain - partner_column[:, n : n + 1]
-            peak = jnp.max(by_j, axis=0, keepdims=True)
-            total = jnp.sum(jnp.exp(by_j - peak), axis=0, keepdims=True)
+            total = jnp.sum(jnp.exp2(by_j), axis=0, keepdims=True)
             best = jnp.max(by_j + (plain - over_i[:, n : n + 1]), axis=0, keepdims=True)
-            result.append(jnp.exp(best - peak - anchor_cost[n : n + 1]) / total)
+            result.append(jnp.exp2(best - anchor_cost[n : n + 1]) / total)
         out_ref[group(g)] = jnp.concatenate(result)
 
 

time: 176 us -> 174 us (0.989)
  Pallas kernels: 35.6 us -> 33.5 us
where the time goes in v8:
time: 174 us
  blocking collectives  116 us (67%)
  Pallas kernels  33.5 us (19%)
  starting transfers between devices  9.79 us (6%)
  waiting for transfers between devices  9.26 us (5%)
  local copies, waits for them, and re-layouts  3.7 us (2%)
    all_to_all x1, blocking collectives, local(): lax.all_to_all(send_blocks, 'tile', split_axis=0, concat_axis=0, tiled=True)  116 us
    pallas_call x1, Pallas kernels, describe(): pl.pallas_call(describe_kernel, grid=(rows // ROWS_STEP,), in_specs=[scal...  25.4 us
    pallas_call x1, Pallas kernels, match(): pl.pallas_call(match_kernel, in_specs=[pl.BlockSpec(memory_space=pltpu.SM...  8.11 us
    ppermute x1, waiting for transfers between devices, local(): sibling_anchors = lax.ppermute(anchors, 'sec', swap)  6.48 us
    ppermute x1, starting transfers between devices, local(): low = lax.ppermute(own_band[-2:], 'tile', down)  5.01 us
  transfers between devices with their start and end apart: 4, of which 4 were waited for; matrix products, arithmetic and copies ran while one was open for 1% of the time, Pallas kernels for 0%

profile of v8, /device:TPU:1, one launch (start us, length us, event | category | flops | bytes accessed | tf_op | source)
XLA Modules:
  0.0 174.0 jit_solution(8048811048943822402)
XLA Ops:
  0.6 0.0 copy-start
  0.6 1.1 slice_bitcast_fusion
  1.7 1.3 collective-permute-start.1
  3.0 5.0 %collective-permute-start = (bf16[2,384,128]{2,1,0:T(8,128)(2,1)S(1)}, bf16[2,384,128]{2,1,0:T(8,128)(2,1)S(1)}, u32[]{:S(2)}, u32[]{:S(2)}) collective-permute-start(bf16[2,384,128]{2,1,0:T(8,128)(2,1)S(1)} %get-tuple-element.18), channel_id=1, source_target_pairs={{0,2},{2,4},{4,6},{6,8},{8,10},{10,12},{12,14},{14,16},{16,18},{18... | collective-permute-start | bytes 589832 | tf_op jit(solution)/shard_map/ppermute | solution.py:399
  8.0 0.0 copy-done
  8.0 0.1 dynamic-slice_reduce_fusion
  8.1 0.1 reshape.121
  8.2 0.2 reduce_window_sum.11
  8.5 0.1 multiply_reduce_fusion
  8.6 0.6 sub.37.chosen_row_ref
  9.2 0.6 sub.36.chosen_ref
  9.8 0.8 collective-permute-done.1.high_ref
  10.7 0.0 copy-start.1
  10.7 0.9 collective-permute-done.low_ref
  11.5 0.0 copy-start.2
  11.5 0.0 copy-done.1
  11.6 0.7 copy-done.2
  12.2 25.4 %shard_map.113 = (bf16[96,128,256]{2,1,0:T(8,128)(2,1)}, bf16[64,528,128]{2,1,0:T(8,128)(2,1)}, bf16[65,256,128]{2,1,0:T(8,128)(2,1)}) custom-call(s32[128]{0:T(128)} %sub.36.chosen_ref, s32[64]{0:T(128)} %bitcast.25, s32[1,128]{1,0:T(1,128)} %sub.37.chosen_row_ref, s32[1,64]{1,0:T(1,128)} %source_row_ref.1, s32[32,384]{1,0:T(8,128)} %bitcast.22, ...), custom_call_target="tpu_custom_call" | custom-call | flops 13690208256 | bytes 9437184 | tf_op jit(solution)/shard_map/pallas_call | solution.py:241
  37.7 1.8 %collective-permute-start.2 = (bf16[65,256,128]{2,1,0:T(8,128)(2,1)}, bf16[65,256,128]{2,1,0:T(8,128)(2,1)}, u32[]{:S(2)}, u32[]{:S(2)}) collective-permute-start(bf16[65,256,128]{2,1,0:T(8,128)(2,1)} %get-tuple-element.10), channel_id=1, source_target_pairs={{0,1},{1,0},{2,3},{3,2},{4,5},{5,4},{6,7},{7,6},{8,9},{9,8},{10,11... | collective-permute-start | bytes 12779528 | tf_op jit(solution)/shard_map/ppermute | solution.py:424
  39.5 0.2 convert_reduce_fusion
  39.7 0.5 multiply_add_fusion.slot_ref
  40.2 6.5 %collective-permute-done.2.anchors_ref = bf16[65,256,128]{2,1,0:T(8,128)(2,1)} collective-permute-done((bf16[65,256,128]{2,1,0:T(8,128)(2,1)}, bf16[65,256,128]{2,1,0:T(8,128)(2,1)}, u32[]{:S(2)}, u32[]{:S(2)}) %collective-permute-start.2) | collective-permute-done | bytes 4259872 | tf_op jit(solution)/shard_map/ppermute | solution.py:424
  46.7 115.8 %all_to_all.5.arrived_ref = bf16[64,528,128]{2,1,0:T(8,128)(2,1)} all-to-all(bf16[64,528,128]{2,1,0:T(8,128)(2,1)} %get-tuple-element.13), channel_id=1, replica_groups=mesh['tile'=64,'sec'=2] {'tile'}, dimensions={0} | all-to-all | bytes 17301504 | tf_op jit(solution)/shard_map/all_to_all | solution.py:428
  162.5 8.1 %shard_map.114 = f32[64,128]{1,0:T(8,128)} custom-call(s32[64]{0:T(128)} %multiply_add_fusion.slot_ref, bf16[65,256,128]{2,1,0:T(8,128)(2,1)} %collective-permute-done.2.anchors_ref, bf16[64,528,128]{2,1,0:T(8,128)(2,1)} %all_to_all.5.arrived_ref), custom_call_target="tpu_custom_call" | custom-call | tf_op jit(solution)/shard_map/pallas_call | solution.py:371
  170.6 1.7 collective-permute-start.3
  172.3 1.1 collective-permute-done.3
  173.4 0.6 copy.13
  (6 shorter events, 0.1 us)
Async XLA Ops:
  0.6 7.4 %copy-start = (s32[2,4096]{1,0:T(2,128)S(1)}, s32[2,4096]{1,0:T(2,128)}, u32[]{:S(2)}) copy-start(s32[2,4096]{1,0:T(2,128)} %param.19) | copy-start | bytes 98308
  1.7 9.0 %collective-permute-start.1 = (bf16[2,384,128]{2,1,0:T(8,128)(2,1)S(1)}, bf16[2,384,128]{2,1,0:T(8,128)(2,1)S(1)}, u32[]{:S(2)}, u32[]{:S(2)}) collective-permute-start(bf16[2,384,128]{2,1,0:T(8,128)(2,1)S(1)} %get-tuple-element.17), channel_id=1, source_target_pairs={{2,0},{4,2},{6,4},{8,6},{10,8},{12,10},{14,12},{16,14},{18,16},{20... | collective-permute-start | bytes 589832 | tf_op jit(solution)/shard_map/ppermute | solution.py:400
  3.0 8.5 %collective-permute-start = (bf16[2,384,128]{2,1,0:T(8,128)(2,1)S(1)}, bf16[2,384,128]{2,1,0:T(8,128)(2,1)S(1)}, u32[]{:S(2)}, u32[]{:S(2)}) collective-permute-start(bf16[2,384,128]{2,1,0:T(8,128)(2,1)S(1)} %get-tuple-element.18), channel_id=1, source_target_pairs={{0,2},{2,4},{4,6},{6,8},{8,10},{10,12},{12,14},{14,16},{16,18},{18... | collective-permute-start | bytes 589832 | tf_op jit(solution)/shard_map/ppermute | solution.py:399
  10.7 0.9 copy-start.1
  11.5 0.7 copy-start.2
  37.7 9.0 %collective-permute-start.2 = (bf16[65,256,128]{2,1,0:T(8,128)(2,1)}, bf16[65,256,128]{2,1,0:T(8,128)(2,1)}, u32[]{:S(2)}, u32[]{:S(2)}) collective-permute-start(bf16[65,256,128]{2,1,0:T(8,128)(2,1)} %get-tuple-element.10), channel_id=1, source_target_pairs={{0,1},{1,0},{2,3},{3,2},{4,5},{5,4},{6,7},{7,6},{8,9},{9,8},{10,11... | collective-permute-start | bytes 12779528 | tf_op jit(solution)/shard_map/ppermute | solution.py:424
  170.6 2.8 %collective-permute-start.3 = (f32[64,128]{1,0:T(8,128)}, f32[64,128]{1,0:T(8,128)S(1)}, u32[]{:S(2)}, u32[]{:S(2)}) collective-permute-start(f32[64,128]{1,0:T(8,128)} %shard_map.114), channel_id=1, source_target_pairs={{0,1},{1,0},{2,3},{3,2},{4,5},{5,4},{6,7},{7,6},{8,9},{9,8},{10,11... | collective-permute-start | bytes 98312 | tf_op jit(solution)/shard_map/ppermute | solution.py:430

commit v9 on v8

--- a/solution.py
+++ b/solution.py
@@ -405,16 +405,15 @@
     wanted = lax.dynamic_index_in_dim(pair_target, 1 - section, 0, keepdims=False).reshape(
         tile_count, pair_count
     )
-    matched = (wanted // block_count == tile_here).astype(jnp.int32)
-    order_rank = jnp.cumsum(matched, axis=1) - matched
-    slot_hot = matched[None] * (
-        order_rank[None] == jnp.arange(capacity)[:, None, None]
-    ).astype(jnp.int32)
-    chosen = jnp.sum(slot_hot * (wanted % block_count + 1)[None], axis=2) - 1
+    matched = wanted // block_count == tile_here
+    within = wanted % block_count
+    lower = jnp.min(jnp.where(matched, within, block_count), axis=1)
+    upper = jnp.max(jnp.where(matched, within, -1), axis=1)
+    chosen = jnp.stack([jnp.where(upper >= 0, lower, -1), jnp.where(upper > lower, upper, -1)])
     targets = lax.dynamic_index_in_dim(wanted, tile_here, 0, keepdims=False)
     owners = targets // block_count
-    earlier = jnp.arange(pair_count)[None, :] < jnp.arange(pair_count)[:, None]
-    slot_rank = jnp.sum(((owners[None, :] == owners[:, None]) & earlier).astype(jnp.int32), axis=1)
+    lower_named = (owners[None, :] == owners[:, None]) & (targets[None, :] < targets[:, None])
+    slot_rank = jnp.any(lower_named, axis=1).astype(jnp.int32)
     slot_index = owners * capacity + slot_rank
 
     described, send_blocks, anchors = describe(

time: 174 us -> 174 us (level)
  no operation moved by 1% of the time
where the time goes in v9:
time: 174 us
  blocking collectives  116 us (67%)
  Pallas kernels  33.9 us (19%)
  waiting for transfers between devices  9.51 us (5%)
  starting transfers between devices  9.28 us (5%)
  local copies, waits for them, and re-layouts  3.69 us (2%)
    all_to_all x1, blocking collectives, local(): lax.all_to_all(send_blocks, 'tile', split_axis=0, concat_axis=0, tiled=True)  116 us
    pallas_call x1, Pallas kernels, describe(): pl.pallas_call(describe_kernel, grid=(rows // ROWS_STEP,), in_specs=[scal...  25.8 us
    pallas_call x1, Pallas kernels, match(): pl.pallas_call(match_kernel, in_specs=[pl.BlockSpec(memory_space=pltpu.SM...  8.12 us
    ppermute x1, waiting for transfers between devices, local(): sibling_anchors = lax.ppermute(anchors, 'sec', swap)  6.42 us
    ppermute x1, starting transfers between devices, local(): low = lax.ppermute(own_band[-2:], 'tile', down)  5.01 us
  transfers between devices with their start and end apart: 4, of which 4 were waited for; matrix products, arithmetic and copies ran while one was open for 1% of the time, Pallas kernels for 0%

profile of v9, /device:TPU:1, one launch (start us, length us, event | category | flops | bytes accessed | tf_op | source)
XLA Modules:
  0.0 174.1 jit_solution(5181754447428470506)
XLA Ops:
  0.6 0.0 copy-start
  0.6 1.1 slice_bitcast_fusion
  1.7 1.3 collective-permute-start.1
  3.0 5.0 %collective-permute-start = (bf16[2,384,128]{2,1,0:T(8,128)(2,1)S(1)}, bf16[2,384,128]{2,1,0:T(8,128)(2,1)S(1)}, u32[]{:S(2)}, u32[]{:S(2)}) collective-permute-start(bf16[2,384,128]{2,1,0:T(8,128)(2,1)S(1)} %get-tuple-element.19), channel_id=1, source_target_pairs={{0,2},{2,4},{4,6},{6,8},{8,10},{10,12},{12,14},{14,16},{16,18},{18... | collective-permute-start | bytes 589832 | tf_op jit(solution)/shard_map/ppermute | solution.py:399
  8.0 0.0 copy-done
  8.0 0.1 dynamic-slice_reduce_fusion
  8.1 0.1 reshape.67
  8.2 0.1 select_reduce_fusion.1
  8.3 0.6 broadcast_in_dim_reshape.3.chosen_row_ref
  8.9 0.6 reshape.68.chosen_ref
  9.5 1.2 collective-permute-done.1.high_ref
  10.7 0.0 copy-start.1
  10.7 0.9 collective-permute-done.low_ref
  11.5 0.0 copy-start.2
  11.5 0.0 copy-done.1
  11.6 0.7 copy-done.2
  12.3 25.8 %shard_map.113 = (bf16[96,128,256]{2,1,0:T(8,128)(2,1)}, bf16[64,528,128]{2,1,0:T(8,128)(2,1)}, bf16[65,256,128]{2,1,0:T(8,128)(2,1)}) custom-call(s32[128]{0:T(128)} %reshape.68.chosen_ref, s32[64]{0:T(128)} %bitcast.30, s32[1,128]{1,0:T(1,128)} %broadcast_in_dim_reshape.3.chosen_row_ref, s32[1,64]{1,0:T(1,128)} %source_row_ref.1, s32[32,384]{1,0:T(8,128)} %bitcast.27, ...), custom_call_target="tpu_custom_call" | custom-call | flops 13690208256 | bytes 9437184 | tf_op jit(solution)/shard_map/pallas_call | solution.py:241
  38.1 1.3 collective-permute-start.2
  39.4 0.2 and_reduce_fusion
  39.6 0.6 convert_add_fusion.slot_ref
  40.1 6.4 %collective-permute-done.2.anchors_ref = bf16[65,256,128]{2,1,0:T(8,128)(2,1)} collective-permute-done((bf16[65,256,128]{2,1,0:T(8,128)(2,1)}, bf16[65,256,128]{2,1,0:T(8,128)(2,1)}, u32[]{:S(2)}, u32[]{:S(2)}) %collective-permute-start.2) | collective-permute-done | bytes 4259872 | tf_op jit(solution)/shard_map/ppermute | solution.py:423
  46.6 116.1 %all_to_all.5.arrived_ref = bf16[64,528,128]{2,1,0:T(8,128)(2,1)} all-to-all(bf16[64,528,128]{2,1,0:T(8,128)(2,1)} %get-tuple-element.13), channel_id=1, replica_groups=mesh['tile'=64,'sec'=2] {'tile'}, dimensions={0} | all-to-all | bytes 17301504 | tf_op jit(solution)/shard_map/all_to_all | solution.py:427
  162.6 8.1 %shard_map.114 = f32[64,128]{1,0:T(8,128)} custom-call(s32[64]{0:T(128)} %convert_add_fusion.slot_ref, bf16[65,256,128]{2,1,0:T(8,128)(2,1)} %collective-permute-done.2.anchors_ref, bf16[64,528,128]{2,1,0:T(8,128)(2,1)} %all_to_all.5.arrived_ref), custom_call_target="tpu_custom_call" | custom-call | tf_op jit(solution)/shard_map/pallas_call | solution.py:371
  170.8 1.7 collective-permute-start.3
  172.4 1.1 collective-permute-done.3
  173.5 0.6 copy.13
  (4 shorter events, 0.1 us)
Async XLA Ops:
  0.6 7.4 %copy-start = (s32[2,4096]{1,0:T(2,128)S(1)}, s32[2,4096]{1,0:T(2,128)}, u32[]{:S(2)}) copy-start(s32[2,4096]{1,0:T(2,128)} %param.19) | copy-start | bytes 98308
  1.7 9.0 %collective-permute-start.1 = (bf16[2,384,128]{2,1,0:T(8,128)(2,1)S(1)}, bf16[2,384,128]{2,1,0:T(8,128)(2,1)S(1)}, u32[]{:S(2)}, u32[]{:S(2)}) collective-permute-start(bf16[2,384,128]{2,1,0:T(8,128)(2,1)S(1)} %get-tuple-element.18), channel_id=1, source_target_pairs={{2,0},{4,2},{6,4},{8,6},{10,8},{12,10},{14,12},{16,14},{18,16},{20... | collective-permute-start | bytes 589832 | tf_op jit(solution)/shard_map/ppermute | solution.py:400
  3.0 8.5 %collective-permute-start = (bf16[2,384,128]{2,1,0:T(8,128)(2,1)S(1)}, bf16[2,384,128]{2,1,0:T(8,128)(2,1)S(1)}, u32[]{:S(2)}, u32[]{:S(2)}) collective-permute-start(bf16[2,384,128]{2,1,0:T(8,128)(2,1)S(1)} %get-tuple-element.19), channel_id=1, source_target_pairs={{0,2},{2,4},{4,6},{6,8},{8,10},{10,12},{12,14},{14,16},{16,18},{18... | collective-permute-start | bytes 589832 | tf_op jit(solution)/shard_map/ppermute | solution.py:399
  10.7 0.9 copy-start.1
  11.5 0.7 copy-start.2
  38.1 8.5 %collective-permute-start.2 = (bf16[65,256,128]{2,1,0:T(8,128)(2,1)}, bf16[65,256,128]{2,1,0:T(8,128)(2,1)}, u32[]{:S(2)}, u32[]{:S(2)}) collective-permute-start(bf16[65,256,128]{2,1,0:T(8,128)(2,1)} %get-tuple-element.10), channel_id=1, source_target_pairs={{0,1},{1,0},{2,3},{3,2},{4,5},{5,4},{6,7},{7,6},{8,9},{9,8},{10,11... | collective-permute-start | bytes 12779528 | tf_op jit(solution)/shard_map/ppermute | solution.py:423
  170.8 2.8 %collective-permute-start.3 = (f32[64,128]{1,0:T(8,128)}, f32[64,128]{1,0:T(8,128)S(1)}, u32[]{:S(2)}, u32[]{:S(2)}) collective-permute-start(f32[64,128]{1,0:T(8,128)} %shard_map.114), channel_id=1, source_target_pairs={{0,1},{1,0},{2,3},{3,2},{4,5},{5,4},{6,7},{7,6},{8,9},{9,8},{10,11... | collective-permute-start | bytes 98312 | tf_op jit(solution)/shard_map/ppermute | solution.py:429

commit v10 on v9

--- a/solution.py
+++ b/solution.py
@@ -124,14 +124,14 @@
     def anchor(n):
         return pltpu.make_async_copy(all_ref.at[source_ref[n]], anchor_ref.at[n], anchor_sem)
 
-    def ship(first, end):
-        @pl.loop(0, chosen_ref.shape[0], unroll=4)
-        def _(n):
-            pl.when((chosen_ref[n] >= first) & (chosen_ref[n] < end))(lambda: send(n).start())
-
+    def ship_anchors(first, end):
         @pl.loop(0, pairs, unroll=4)
         def _(n):
             pl.when((source_ref[n] >= first) & (source_ref[n] < end))(lambda: anchor(n).start())
+
+    @pl.when(step == last)
+    def _():
+        ship_anchors(0, step * ROWS_STEP * row_blocks)
 
     def fold_copies():
         return (
@@ -211,7 +211,11 @@
 
     @pl.when(step == last)
     def _():
-        ship(0, all_ref.shape[0])
+        @pl.loop(0, chosen_ref.shape[0], unroll=4)
+        def _(n):
+            pl.when(chosen_ref[n] >= 0)(lambda: send(n).start())
+
+        ship_anchors(base * row_blocks, all_ref.shape[0])
 
         @pl.loop(0, chosen_ref.shape[0], unroll=4)
         def _(n):

time: 174 us -> 174 us (level)
  no operation moved by 1% of the time
where the time goes in v10:
time: 174 us
  blocking collectives  116 us (67%)
  Pallas kernels  33.5 us (19%)
  starting transfers between devices  9.7 us (6%)
  waiting for transfers between devices  9.51 us (5%)
  local copies, waits for them, and re-layouts  3.69 us (2%)
    all_to_all x1, blocking collectives, local(): lax.all_to_all(send_blocks, 'tile', split_axis=0, concat_axis=0, tiled=True)  116 us
    pallas_call x1, Pallas kernels, describe(): pl.pallas_call(describe_kernel, grid=(rows // ROWS_STEP,), in_specs=[scal...  25.4 us
    pallas_call x1, Pallas kernels, match(): pl.pallas_call(match_kernel, in_specs=[pl.BlockSpec(memory_space=pltpu.SM...  8.11 us
    ppermute x1, waiting for transfers between devices, local(): sibling_anchors = lax.ppermute(anchors, 'sec', swap)  6.42 us
    ppermute x1, starting transfers between devices, local(): low = lax.ppermute(own_band[-2:], 'tile', down)  5.01 us
  transfers between devices with their start and end apart: 4, of which 4 were waited for; matrix products, arithmetic and copies ran while one was open for 1% of the time, Pallas kernels for 0%

profile of v10, /device:TPU:1, one launch (start us, length us, event | category | flops | bytes accessed | tf_op | source)
XLA Modules:
  0.0 173.8 jit_solution(978748435042113413)
XLA Ops:
  0.6 0.0 copy-start
  0.6 1.1 slice_bitcast_fusion
  1.7 1.3 collective-permute-start.1
  3.0 5.0 %collective-permute-start = (bf16[2,384,128]{2,1,0:T(8,128)(2,1)S(1)}, bf16[2,384,128]{2,1,0:T(8,128)(2,1)S(1)}, u32[]{:S(2)}, u32[]{:S(2)}) collective-permute-start(bf16[2,384,128]{2,1,0:T(8,128)(2,1)S(1)} %get-tuple-element.19), channel_id=1, source_target_pairs={{0,2},{2,4},{4,6},{6,8},{8,10},{10,12},{12,14},{14,16},{16,18},{18... | collective-permute-start | bytes 589832 | tf_op jit(solution)/shard_map/ppermute | solution.py:403
  8.0 0.0 copy-done
  8.0 0.1 dynamic-slice_reduce_fusion
  8.1 0.1 reshape.67
  8.2 0.1 select_reduce_fusion.1
  8.3 0.6 broadcast_in_dim_reshape.3.chosen_row_ref
  8.9 0.6 reshape.68.chosen_ref
  9.5 1.2 collective-permute-done.1.high_ref
  10.7 0.0 copy-start.1
  10.7 0.9 collective-permute-done.low_ref
  11.5 0.0 copy-start.2
  11.5 0.0 copy-done.1
  11.6 0.7 copy-done.2
  12.3 25.4 %shard_map.113 = (bf16[96,128,256]{2,1,0:T(8,128)(2,1)}, bf16[64,528,128]{2,1,0:T(8,128)(2,1)}, bf16[65,256,128]{2,1,0:T(8,128)(2,1)}) custom-call(s32[128]{0:T(128)} %reshape.68.chosen_ref, s32[64]{0:T(128)} %bitcast.30, s32[1,128]{1,0:T(1,128)} %broadcast_in_dim_reshape.3.chosen_row_ref, s32[1,64]{1,0:T(1,128)} %source_row_ref.1, s32[32,384]{1,0:T(8,128)} %bitcast.27, ...), custom_call_target="tpu_custom_call" | custom-call | flops 13690208256 | bytes 9437184 | tf_op jit(solution)/shard_map/pallas_call | solution.py:245
  37.6 1.7 collective-permute-start.2
  39.4 0.2 and_reduce_fusion
  39.5 0.6 convert_add_fusion.slot_ref
  40.1 6.4 %collective-permute-done.2.anchors_ref = bf16[65,256,128]{2,1,0:T(8,128)(2,1)} collective-permute-done((bf16[65,256,128]{2,1,0:T(8,128)(2,1)}, bf16[65,256,128]{2,1,0:T(8,128)(2,1)}, u32[]{:S(2)}, u32[]{:S(2)}) %collective-permute-start.2) | collective-permute-done | bytes 4259872 | tf_op jit(solution)/shard_map/ppermute | solution.py:427
  46.5 115.7 %all_to_all.5.arrived_ref = bf16[64,528,128]{2,1,0:T(8,128)(2,1)} all-to-all(bf16[64,528,128]{2,1,0:T(8,128)(2,1)} %get-tuple-element.13), channel_id=1, replica_groups=mesh['tile'=64,'sec'=2] {'tile'}, dimensions={0} | all-to-all | bytes 17301504 | tf_op jit(solution)/shard_map/all_to_all | solution.py:431
  162.3 8.1 %shard_map.114 = f32[64,128]{1,0:T(8,128)} custom-call(s32[64]{0:T(128)} %convert_add_fusion.slot_ref, bf16[65,256,128]{2,1,0:T(8,128)(2,1)} %collective-permute-done.2.anchors_ref, bf16[64,528,128]{2,1,0:T(8,128)(2,1)} %all_to_all.5.arrived_ref), custom_call_target="tpu_custom_call" | custom-call | tf_op jit(solution)/shard_map/pallas_call | solution.py:375
  170.4 1.7 collective-permute-start.3
  172.1 1.1 collective-permute-done.3
  173.1 0.6 copy.13
  (4 shorter events, 0.1 us)
Async XLA Ops:
  0.6 7.4 %copy-start = (s32[2,4096]{1,0:T(2,128)S(1)}, s32[2,4096]{1,0:T(2,128)}, u32[]{:S(2)}) copy-start(s32[2,4096]{1,0:T(2,128)} %param.19) | copy-start | bytes 98308
  1.7 9.0 %collective-permute-start.1 = (bf16[2,384,128]{2,1,0:T(8,128)(2,1)S(1)}, bf16[2,384,128]{2,1,0:T(8,128)(2,1)S(1)}, u32[]{:S(2)}, u32[]{:S(2)}) collective-permute-start(bf16[2,384,128]{2,1,0:T(8,128)(2,1)S(1)} %get-tuple-element.18), channel_id=1, source_target_pairs={{2,0},{4,2},{6,4},{8,6},{10,8},{12,10},{14,12},{16,14},{18,16},{20... | collective-permute-start | bytes 589832 | tf_op jit(solution)/shard_map/ppermute | solution.py:404
  3.0 8.5 %collective-permute-start = (bf16[2,384,128]{2,1,0:T(8,128)(2,1)S(1)}, bf16[2,384,128]{2,1,0:T(8,128)(2,1)S(1)}, u32[]{:S(2)}, u32[]{:S(2)}) collective-permute-start(bf16[2,384,128]{2,1,0:T(8,128)(2,1)S(1)} %get-tuple-element.19), channel_id=1, source_target_pairs={{0,2},{2,4},{4,6},{6,8},{8,10},{10,12},{12,14},{14,16},{16,18},{18... | collective-permute-start | bytes 589832 | tf_op jit(solution)/shard_map/ppermute | solution.py:403
  10.7 0.9 copy-start.1
  11.5 0.7 copy-start.2
  37.6 8.9 %collective-permute-start.2 = (bf16[65,256,128]{2,1,0:T(8,128)(2,1)}, bf16[65,256,128]{2,1,0:T(8,128)(2,1)}, u32[]{:S(2)}, u32[]{:S(2)}) collective-permute-start(bf16[65,256,128]{2,1,0:T(8,128)(2,1)} %get-tuple-element.10), channel_id=1, source_target_pairs={{0,1},{1,0},{2,3},{3,2},{4,5},{5,4},{6,7},{7,6},{8,9},{9,8},{10,11... | collective-permute-start | bytes 12779528 | tf_op jit(solution)/shard_map/ppermute | solution.py:427
  170.4 2.8 %collective-permute-start.3 = (f32[64,128]{1,0:T(8,128)}, f32[64,128]{1,0:T(8,128)S(1)}, u32[]{:S(2)}, u32[]{:S(2)}) collective-permute-start(f32[64,128]{1,0:T(8,128)} %shard_map.114), channel_id=1, source_target_pairs={{0,1},{1,0},{2,3},{3,2},{4,5},{5,4},{6,7},{7,6},{8,9},{9,8},{10,11... | collective-permute-start | bytes 98312 | tf_op jit(solution)/shard_map/ppermute | solution.py:433
